TPU v7x, 32 devices: a whole 2x2x4 slice. The times are simulated.
32 devices in a mesh: ctx: 8 (over y, x, core), fsdp: 4 (over z).
Axes of the slice: x: 2, y: 2, z: 4, core: 2. Of those that a mesh axis runs over, the one named last changes fastest.
Arguments:
- tokens: bfloat16 [2, 8, 1024, 1536], P(None, 'fsdp', 'ctx'), may hold values from -6 to 6
- lengths: int32 [2, 8], P(None, 'fsdp'), may hold values from 256 to 1024, as said below
- expert_picks: int32 [2, 8, 1024, 4], P(None, 'fsdp', 'ctx'), may hold values from 0 to 31, all different within a row; in each aligned block of 128 rows (0 to 127, 128 to 255, ..., all dimensions but the last counted through in order) at most 20 rows name the same one
- router_weights: float32 [2, 8, 1024, 4], P(None, 'fsdp', 'ctx'), may hold values from 0.12 to 0.36
- first_gain: bfloat16 [1536], P('fsdp'), may hold values from 0.5 to 1.5
- second_gain: bfloat16 [1536], P('fsdp'), may hold values from 0.5 to 1.5
- query_weight: bfloat16 [1536, 1536], P('fsdp'), may hold values from -0.15625 to 0.15625
- key_weight: bfloat16 [1536, 256], P('fsdp'), may hold values from -0.15625 to 0.15625
- value_weight: bfloat16 [1536, 256], P('fsdp'), may hold values from -0.15625 to 0.15625
- output_weight: bfloat16 [1536, 1536], P('fsdp'), may hold values from -2 to 2
- up_weight: bfloat16 [32, 1536, 1536], P('ctx', 'fsdp'), may hold values from -0.15625 to 0.15625
- down_weight: bfloat16 [32, 768, 1536], P('ctx', 'fsdp'), may hold values from -0.3125 to 0.3125
- cotangent: bfloat16 [2, 8, 1024, 1536], P(None, 'fsdp', 'ctx'), may hold values from -6 to 6
Outputs:
- block_output: bfloat16 [2, 8, 1024, 1536], P(None, 'fsdp', 'ctx')
- grad_tokens: float32 [2, 8, 1024, 1536], P(None, 'fsdp', 'ctx')
- grad_router: float32 [2, 8, 1024, 4], P(None, 'fsdp', 'ctx')
- grad_first: float32 [1536], P('fsdp')
- grad_second: float32 [1536], P('fsdp')
- grad_query: float32 [1536, 1536], P('fsdp')
- grad_key: float32 [1536, 256], P('fsdp')
- grad_value: float32 [1536, 256], P('fsdp')
- grad_projection: float32 [1536, 1536], P('fsdp')
- grad_up: float32 [32, 1536, 1536], P('ctx', 'fsdp')
- grad_down: float32 [32, 768, 1536], P('ctx', 'fsdp')
Inputs may be any that keep to these rules, and one draw needn't show every extreme that they name: `lengths`: in each micro-batch, one of the 2 sequences of each index of fsdp has the full length 1024. `expert_picks`: A row names 4 different experts. Among the 128 rows of one sequence that lie on one device, no expert is named by more than 20 rows, a bound that some block reaches.
All inputs are finite; a program needn't handle non-finite values.
Results may differ from a plain program's by a relative error of at most 0.02.
Values may be sent and summed in bfloat16 or wider, within the bound.
No kernel may reach another device: no remote copies, remote signals or barrier semaphores. Data moves between devices by JAX's collectives and lax.ppermute only.
A program may use at most 200 MiB of HBM per device.

v0:
```python
import jax
import jax.numpy as jnp
from jax import lax
from jax.sharding import PartitionSpec as P

H = 12
KV = 2
HD = 128
TOP = 4
EXPERTS = 32


EPSILON = 1e-06
ROPE_BASE = 10000.0
NEGATIVE = -1e30
HIGHEST = lax.Precision.HIGHEST


def rotate(vectors, positions, direction):
    half_dim = HD // 2
    frequency = ROPE_BASE ** (-(jnp.arange(half_dim, dtype=jnp.float32) * 2.0 / HD))
    angles = positions.astype(jnp.float32)[:, None] * frequency[None, :]
    cosine_part = jnp.cos(angles)[:, None, :]
    sine_part = direction * jnp.sin(angles)[:, None, :]
    leading = vectors[..., :half_dim]
    trailing = vectors[..., half_dim:]
    return jnp.concatenate(
        [
            leading * cosine_part - trailing * sine_part,
            trailing * cosine_part + leading * sine_part,
        ],
        axis=-1,
    )


def norm_forward(values, gain_row):
    inverse = lax.rsqrt(jnp.mean(values * values, axis=-1, keepdims=True) + EPSILON)
    return (values * inverse * gain_row, inverse)


def norm_backward(values, inverse, gain_row, upstream):
    gain_grad = jnp.sum(upstream * values * inverse, axis=(0, 1))
    scaled = upstream * gain_row
    projected = jnp.mean(scaled * values, axis=-1, keepdims=True)
    return (inverse * scaled - values * inverse**3 * projected, gain_grad)


def local(
    tokens,
    lengths,
    expert_picks,
    router_weights,
    first_gain,
    second_gain,
    query_weight,
    key_weight,
    value_weight,
    output_weight,
    up_weight,
    down_weight,
    cotangent,
):
    batches, seqs_here, local_len, model_width = tokens.shape
    ctx_count = lax.axis_size("ctx")
    split = max(1, ctx_count // EXPERTS)
    pieces = up_weight.shape[0]
    capacity = max(2, (5 * local_len * TOP + 4 * EXPERTS - 1) // (4 * EXPERTS))
    full_len = local_len * ctx_count
    groups = H // KV
    group_rows = groups * local_len
    pair_width = KV * HD
    slot_count = EXPERTS * capacity
    factor = HD ** (-0.5)
    positions = lax.axis_index("ctx") * local_len + jnp.arange(local_len, dtype=jnp.int32)
    query_positions = jnp.tile(positions, groups)
    key_positions_all = jnp.arange(full_len, dtype=jnp.int32)

    def to_pieces(slots):
        widened = jnp.repeat(
            slots.reshape(seqs_here, EXPERTS, capacity, model_width), split, axis=1
        )
        return widened.reshape(seqs_here, ctx_count, pieces, capacity, model_width)

    def from_pieces(parts):
        summed = jnp.sum(parts.reshape(seqs_here, EXPERTS, split, capacity, model_width), axis=2)
        return summed.astype(jnp.bfloat16).reshape(seqs_here, slot_count, model_width)

    totals = None
    outputs_list = []
    entry_list = []
    router_list = []
    for batch_index in range(batches):
        weights = (
            lax.all_gather(first_gain, "fsdp", axis=0, tiled=True),
            lax.all_gather(second_gain, "fsdp", axis=0, tiled=True),
            lax.all_gather(query_weight, "fsdp", axis=0, tiled=True),
            lax.all_gather(key_weight, "fsdp", axis=0, tiled=True),
            lax.all_gather(value_weight, "fsdp", axis=0, tiled=True),
            lax.all_gather(output_weight, "fsdp", axis=0, tiled=True),
            lax.all_gather(up_weight, "fsdp", axis=1, tiled=True),
            lax.all_gather(down_weight, "fsdp", axis=1, tiled=True),
        )
        (
            first_scale,
            second_scale,
            query_full,
            key_full,
            value_full,
            output_full,
            up_full,
            down_full,
        ) = weights
        first_scale = first_scale.astype(jnp.float32)
        second_scale = second_scale.astype(jnp.float32)
        block_width = down_full.shape[1]
        inputs = tokens[batch_index].astype(jnp.float32)
        seq_lengths = lengths[batch_index]
        live_mask = positions[None, :] < seq_lengths[:, None]
        live_rows = live_mask.astype(jnp.float32)[..., None]
        normed, inverse_one = norm_forward(inputs, first_scale)
        normed_low = normed.astype(jnp.bfloat16).reshape(-1, model_width)
        query_pre = jnp.dot(normed_low, query_full, preferred_element_type=jnp.float32).reshape(
            seqs_here, local_len, H, HD
        )
        key_pre = jnp.dot(normed_low, key_full, preferred_element_type=jnp.float32).reshape(
            seqs_here, local_len, KV, HD
        )
        value_pre = jnp.dot(normed_low, value_full, preferred_element_type=jnp.float32)
        turned_query = rotate(query_pre, positions, 1.0).astype(jnp.bfloat16)
        turned_key = (
            rotate(key_pre, positions, 1.0)
            .astype(jnp.bfloat16)
            .reshape(seqs_here, local_len, pair_width)
        )
        value_low = value_pre.astype(jnp.bfloat16).reshape(seqs_here, local_len, pair_width)
        query_groups = (
            turned_query.reshape(seqs_here, local_len, KV, groups, HD)
            .transpose(0, 2, 3, 1, 4)
            .reshape(seqs_here, KV, group_rows, HD)
        )
        top_score = jnp.full((seqs_here, KV, group_rows), NEGATIVE, jnp.float32)
        key_part = lax.all_gather(turned_key, "ctx", axis=1, tiled=True).reshape(
            seqs_here, -1, KV, HD
        )
        value_part = lax.all_gather(value_low, "ctx", axis=1, tiled=True).reshape(
            seqs_here, -1, KV, HD
        )
        attend_scores = (
            jnp.einsum(
                "skqd,snkd->skqn", query_groups, key_part, preferred_element_type=jnp.float32
            )
            * factor
        )
        key_positions = jnp.arange(key_part.shape[1], dtype=jnp.int32)
        attend_allowed = (
            key_positions[None, None, None, :] <= query_positions[None, None, :, None]
        ) & (key_positions[None, None, None, :] < seq_lengths[:, None, None, None])
        new_top = jnp.maximum(
            top_score, jnp.max(jnp.where(attend_allowed, attend_scores, NEGATIVE), axis=-1)
        )
        shares = jnp.where(attend_allowed, jnp.exp(attend_scores - new_top[..., None]), 0.0)
        denominator = jnp.sum(shares, axis=-1)
        weighted_sum = jnp.einsum(
            "skqn,snkd->skqd",
            shares.astype(jnp.bfloat16),
            value_part,
            preferred_element_type=jnp.float32,
        )
        top_score, denominator, weighted_sum = (new_top, denominator, weighted_sum)
        log_total = top_score + jnp.log(denominator)
        attended = weighted_sum / denominator[..., None]
        attended_rows = (
            attended.reshape(seqs_here, KV, groups, local_len, HD)
            .transpose(0, 3, 1, 2, 4)
            .reshape(-1, H * HD)
        )
        attended_low = attended_rows.astype(jnp.bfloat16)
        branch = jnp.dot(attended_low, output_full, preferred_element_type=jnp.float32).reshape(
            seqs_here, local_len, model_width
        )
        hidden = inputs + live_rows * branch
        second, inverse_two = norm_forward(hidden, second_scale)
        second_low = second.astype(jnp.bfloat16)
        chosen = expert_picks[batch_index]
        matches = (
            (
                (chosen[..., None] == jnp.arange(EXPERTS, dtype=jnp.int32))
                & live_mask[..., None, None]
            )
            .astype(jnp.int32)
            .reshape(seqs_here, local_len * TOP, EXPERTS)
        )
        earlier = jnp.cumsum(matches, axis=1) - matches
        ranking = jnp.sum(earlier * matches, axis=-1).reshape(seqs_here, local_len, TOP)
        slot_index = chosen * capacity + ranking
        selected = (
            (slot_index[..., None] == jnp.arange(slot_count, dtype=jnp.int32))
            & live_mask[..., None, None]
        ).astype(jnp.bfloat16)
        routing = jnp.sum(selected, axis=2)
        outgoing = to_pieces(
            jnp.einsum(
                "stc,std->scd", routing, second_low, preferred_element_type=jnp.float32
            ).astype(jnp.bfloat16)
        )
        arrived = lax.all_to_all(outgoing, "ctx", split_axis=1, concat_axis=1, tiled=True)
        gate_up = jnp.einsum(
            "snpcd,pdf->snpcf", arrived, up_full, preferred_element_type=jnp.float32
        )
        active = (jax.nn.silu(gate_up[..., :block_width]) * gate_up[..., block_width:]).astype(
            jnp.bfloat16
        )
        produced = jnp.einsum(
            "snpcf,pfd->snpcd", active, down_full, preferred_element_type=jnp.float32
        )
        sent_back = lax.all_to_all(
            produced.astype(jnp.bfloat16), "ctx", split_axis=1, concat_axis=1, tiled=True
        ).astype(produced.dtype)
        returned, arrived, gate_up, active = (sent_back, arrived, gate_up, active)
        back_slots = from_pieces(returned)
        picked = jnp.einsum(
            "stkc,scd->stkd", selected, back_slots, preferred_element_type=jnp.float32
        )
        gate_values = router_weights[batch_index]
        block_rows = hidden + jnp.sum(gate_values[..., None] * picked, axis=2)
        outputs_list.append(block_rows.astype(jnp.bfloat16))
        upstream = cotangent[batch_index].astype(jnp.float32)
        router_list.append(jnp.sum(upstream[:, :, None, :] * picked, axis=-1))
        weighted = jnp.sum(selected.astype(jnp.float32) * gate_values[..., None], axis=2)
        slot_grads = to_pieces(
            jnp.einsum("stc,std->scd", weighted, upstream, precision=HIGHEST).astype(jnp.bfloat16)
        )
        arrived_grads = lax.all_to_all(slot_grads, "ctx", split_axis=1, concat_axis=1, tiled=True)
        gate_part = gate_up[..., :block_width]
        up_part = gate_up[..., block_width:]
        logistic = jax.nn.sigmoid(gate_part)
        silu_gate = jax.nn.silu(gate_part)
        down_grad = jnp.einsum(
            "snpcf,snpcd->pfd", active, arrived_grads, preferred_element_type=jnp.float32
        )
        active_grad = jnp.einsum(
            "snpcd,pfd->snpcf", arrived_grads, down_full, preferred_element_type=jnp.float32
        )
        derivative = logistic * (1.0 + gate_part * (1.0 - logistic))
        up_grads = jnp.concatenate(
            [active_grad * up_part * derivative, active_grad * silu_gate], axis=-1
        ).astype(jnp.bfloat16)
        upper_grad = jnp.einsum(
            "snpcd,snpcf->pdf", arrived, up_grads, preferred_element_type=jnp.float32
        )
        input_grads = jnp.einsum(
            "snpcf,pdf->snpcd", up_grads, up_full, preferred_element_type=jnp.float32
        )
        returned_grads = lax.all_to_all(
            input_grads.astype(jnp.bfloat16), "ctx", split_axis=1, concat_axis=1, tiled=True
        ).astype(input_grads.dtype)
        back_grads = from_pieces(returned_grads)
        dispatch_grad = jnp.einsum(
            "stc,scd->std", routing, back_grads, preferred_element_type=jnp.float32
        )
        norm_grad, second_grads = norm_backward(hidden, inverse_two, second_scale, dispatch_grad)
        hidden_grad = upstream + norm_grad
        branch_grad = (live_rows * hidden_grad).astype(jnp.bfloat16).reshape(-1, model_width)
        output_grad = jnp.dot(attended_low.T, branch_grad, preferred_element_type=jnp.float32)
        attended_grad = jnp.dot(
            branch_grad, output_full.T, preferred_element_type=jnp.float32
        ).astype(jnp.bfloat16)
        grad_groups = (
            attended_grad.reshape(seqs_here, local_len, KV, groups, HD)
            .transpose(0, 2, 3, 1, 4)
            .reshape(seqs_here, KV, group_rows, HD)
        )
        deltas = jnp.sum(grad_groups.astype(jnp.float32) * attended, axis=-1)
        every_key, every_value = (
            lax.all_gather(turned_key, "ctx", axis=1, tiled=True),
            lax.all_gather(value_low, "ctx", axis=1, tiled=True),
        )
        query_parts = []
        key_terms = []
        for seq_index in range(seqs_here):
            key_heads = every_key[seq_index].reshape(full_len, KV, HD)
            value_heads = every_value[seq_index].reshape(full_len, KV, HD)
            scores = (
                jnp.einsum(
                    "kqd,nkd->kqn",
                    query_groups[seq_index],
                    key_heads,
                    preferred_element_type=jnp.float32,
                )
                * factor
            )
            allowed = (key_positions_all[None, None, :] <= query_positions[None, :, None]) & (
                key_positions_all[None, None, :] < seq_lengths[seq_index]
            )
            probability = jnp.where(allowed, jnp.exp(scores - log_total[seq_index][..., None]), 0.0)
            share_grads = jnp.einsum(
                "kqd,nkd->kqn",
                grad_groups[seq_index],
                value_heads,
                preferred_element_type=jnp.float32,
            )
            score_grads = (probability * (share_grads - deltas[seq_index][..., None])).astype(
                jnp.bfloat16
            )
            query_parts.append(
                jnp.einsum(
                    "kqn,nkd->kqd", score_grads, key_heads, preferred_element_type=jnp.float32
                )
                * factor
            )
            key_grad = (
                jnp.einsum(
                    "kqn,kqd->nkd",
                    score_grads,
                    query_groups[seq_index],
                    preferred_element_type=jnp.float32,
                )
                * factor
            )
            value_grad = jnp.einsum(
                "kqn,kqd->nkd",
                probability.astype(jnp.bfloat16),
                grad_groups[seq_index],
                preferred_element_type=jnp.float32,
            )
            key_terms.append(
                jnp.concatenate(
                    [
                        key_grad.reshape(full_len, pair_width),
                        value_grad.reshape(full_len, pair_width),
                    ],
                    axis=-1,
                )
            )
        partial_terms = jnp.stack(key_terms, axis=1)
        own_terms = lax.psum_scatter(
            partial_terms, "ctx", scatter_dimension=0, tiled=True
        ).transpose(1, 0, 2)
        key_back = (
            rotate(
                own_terms[..., :pair_width].reshape(seqs_here, local_len, KV, HD), positions, -1.0
            )
            .astype(jnp.bfloat16)
            .reshape(-1, pair_width)
        )
        value_back = own_terms[..., pair_width:].astype(jnp.bfloat16).reshape(-1, pair_width)
        query_grad = (
            jnp.stack(query_parts)
            .reshape(seqs_here, KV, groups, local_len, HD)
            .transpose(0, 3, 1, 2, 4)
            .reshape(seqs_here, local_len, H, HD)
        )
        query_back = rotate(query_grad, positions, -1.0).astype(jnp.bfloat16).reshape(-1, H * HD)
        query_grads = jnp.dot(normed_low.T, query_back, preferred_element_type=jnp.float32)
        key_grads = jnp.dot(normed_low.T, key_back, preferred_element_type=jnp.float32)
        value_grads = jnp.dot(normed_low.T, value_back, preferred_element_type=jnp.float32)
        normed_grad = jnp.dot(query_back, query_full.T, preferred_element_type=jnp.float32)
        normed_grad = normed_grad + jnp.dot(
            key_back, key_full.T, preferred_element_type=jnp.float32
        )
        normed_grad = normed_grad + jnp.dot(
            value_back, value_full.T, preferred_element_type=jnp.float32
        )
        entry_grad, first_grads = norm_backward(
            inputs, inverse_one, first_scale, normed_grad.reshape(seqs_here, local_len, model_width)
        )
        entry_list.append(hidden_grad + entry_grad)
        grads = (
            first_grads,
            second_grads,
            query_grads,
            key_grads,
            value_grads,
            output_grad,
            upper_grad,
            down_grad,
        )
        shard_sums = (
            lax.psum_scatter(
                grads[0].astype(jnp.bfloat16), "fsdp", scatter_dimension=0, tiled=True
            ).astype(jnp.float32),
            lax.psum_scatter(
                grads[1].astype(jnp.bfloat16), "fsdp", scatter_dimension=0, tiled=True
            ).astype(jnp.float32),
            lax.psum_scatter(
                grads[2].astype(jnp.bfloat16), "fsdp", scatter_dimension=0, tiled=True
            ).astype(jnp.float32),
            lax.psum_scatter(
                grads[3].astype(jnp.bfloat16), "fsdp", scatter_dimension=0, tiled=True
            ).astype(jnp.float32),
            lax.psum_scatter(
                grads[4].astype(jnp.bfloat16), "fsdp", scatter_dimension=0, tiled=True
            ).astype(jnp.float32),
            lax.psum_scatter(
                grads[5].astype(jnp.bfloat16), "fsdp", scatter_dimension=0, tiled=True
            ).astype(jnp.float32),
            lax.psum_scatter(
                grads[6].astype(jnp.bfloat16), "fsdp", scatter_dimension=1, tiled=True
            ).astype(jnp.float32),
            lax.psum_scatter(
                grads[7].astype(jnp.bfloat16), "fsdp", scatter_dimension=1, tiled=True
            ).astype(jnp.float32),
        )
        totals = shard_sums if totals is None else jax.tree.map(jnp.add, totals, shard_sums)
    context_sums = lax.psum(
        (totals[0], totals[1], totals[2], totals[3], totals[4], totals[5]), "ctx"
    )
    return (
        jnp.stack(outputs_list),
        jnp.stack(entry_list),
        jnp.stack(router_list),
        context_sums[0],
        context_sums[1],
        context_sums[2],
        context_sums[3],
        context_sums[4],
        context_sums[5],
        totals[6],
        totals[7],
    )


def solution(mesh):
    placed = (
        P(None, "fsdp", "ctx", None),
        P(None, "fsdp"),
        P(None, "fsdp", "ctx", None),
        P(None, "fsdp", "ctx", None),
        P("fsdp"),
        P("fsdp"),
        P("fsdp", None),
        P("fsdp", None),
        P("fsdp", None),
        P("fsdp", None),
        P("ctx", "fsdp", None),
        P("ctx", "fsdp", None),
        P(None, "fsdp", "ctx", None),
    )
    return jax.shard_map(
        local,
        mesh=mesh,
        in_specs=placed,
        out_specs=(
            P(None, "fsdp", "ctx", None),
            P(None, "fsdp", "ctx", None),
            P(None, "fsdp", "ctx", None),
            P("fsdp"),
            P("fsdp"),
            P("fsdp", None),
            P("fsdp", None),
            P("fsdp", None),
            P("fsdp", None),
            P("ctx", "fsdp", None),
            P("ctx", "fsdp", None),
        ),
        check_vma=False,
    )
```

profile of v0, /device:TPU:0, one launch (start us, length us, event | category | flops | bytes accessed | tf_op | source)
XLA Modules:
  0.0 2745.9 jit_solution(244310323111109166)
XLA Ops:
  8.7 13.5 all-gather
  22.2 29.1 %all_gather.50 = bf16[1536,256]{1,0:T(8,128)(2,1)S(1)} all-gather(bf16[384,256]{1,0:T(8,128)(2,1)} %param.20), channel_id=1, replica_groups=mesh['ctx'=8,'fsdp'=4] {'fsdp'}, dimensions={0}, use_global_device_ids=true | all-gather | bytes 983040 | tf_op jit(solution)/shard_map/all_gather | solution.py:97
  57.6 30.7 %all_gather.52 = bf16[1536,256]{1,0:T(8,128)(2,1)S(1)} all-gather(bf16[384,256]{1,0:T(8,128)(2,1)} %param.21), channel_id=1, replica_groups=mesh['ctx'=8,'fsdp'=4] {'fsdp'}, dimensions={0}, use_global_device_ids=true | all-gather | bytes 983040 | tf_op jit(solution)/shard_map/all_gather | solution.py:98
  134.2 12.1 all-gather.1
  187.3 7.0 copy.284
  211.9 7.8 fusion.248
  220.2 62.5 %all-gather.17.cloned.1.call-done = bf16[1536,1536]{1,0:T(8,128)(2,1)} async-done(((bf16[384,1536]{1,0:T(8,128)(2,1)}), bf16[1536,1536]{1,0:T(8,128)(2,1)}) %all-gather.17.cloned.1.call-update) | async-done | bytes 4718608 | tf_op jit(solution)/shard_map/all_gather | solution.py:99
  307.0 8.7 select_reduce_fusion.1
  320.6 7.1 fusion.8
  327.6 8.2 all-gather.15.cloned.1.call-done
  335.9 7.4 fusion.247
  359.6 10.1 all-to-all-done.2
  374.6 290.8 %all-gather.19.cloned.1.call-done = bf16[4,1536,1536]{2,1,0:T(8,128)(2,1)} async-done(((bf16[4,384,1536]{2,1,0:T(8,128)(2,1)}), bf16[4,1536,1536]{2,1,0:T(8,128)(2,1)}) %all-gather.19.cloned.1.call-update) | async-done | bytes 18874384 | tf_op jit(solution)/shard_map/all_gather | solution.py:100
  665.4 16.9 fusion.29
  682.3 150.0 %all-gather.21.cloned.1.call-done = bf16[4,768,1536]{2,1,0:T(8,128)(2,1)} async-done(((bf16[4,192,1536]{2,1,0:T(8,128)(2,1)}), bf16[4,768,1536]{2,1,0:T(8,128)(2,1)}) %all-gather.21.cloned.1.call-update) | async-done | bytes 9437200 | tf_op jit(solution)/shard_map/all_gather | solution.py:101
  832.2 15.3 fusion.37
  852.3 13.6 convert_bitcast_fusion
  865.9 7.2 copy.352
  873.1 16.9 fusion.26
  890.1 8.6 all-to-all-done.4
  903.6 15.6 fusion.40
  919.2 13.6 convert_bitcast_fusion.1
  932.7 7.3 copy.322
  940.0 9.9 all-to-all-done.7
  958.5 7.8 convert_bitcast_fusion.2
  971.2 29.6 %all-to-all-done.5 = bf16[2,8,4,20,1536]{4,2,3,0,1:T(4,128)(2,1)} async-done(((bf16[2,8,4,20,1536]{4,2,3,0,1:T(4,128)(2,1)}), bf16[2,8,4,20,1536]{4,2,3,0,1:T(4,128)(2,1)}, u32[]{:S(2)}, u32[]{:S(2)}) %all-to-all-start.5) | async-done | bytes 3932192 | tf_op jit(solution)/shard_map/all_to_all | solution.py:254
  1021.6 8.1 copy.353
  1043.5 8.2 all-to-all-done.3
  1051.7 8.1 copy.316
  1059.9 6.6 multiply_reduce_fusion
  1166.2 48.3 %reduce-scatter.17.cloned.1.call-done = f32[128,2,512]{2,0,1:T(8,128)} async-done(((f32[1024,2,512]{2,0,1:T(8,128)}), f32[128,2,512]{2,0,1:T(8,128)}) %reduce-scatter.17.cloned.1.call-update) | async-done | bytes 524304 | tf_op jit(solution)/shard_map/reduce_scatter | solution.py:336
  1274.6 10.2 bitcast_convert_fusion.2
  1286.5 10.2 bitcast_convert_fusion.3
  1298.3 16.9 bitcast_convert_fusion
  1316.9 16.8 bitcast_convert_fusion.1
  1335.4 7.7 convert_bitcast_fusion.3
  1354.6 44.6 %all-to-all-done.1 = bf16[2,8,4,20,1536]{4,2,3,0,1:T(4,128)(2,1)} async-done(((bf16[2,8,4,20,1536]{4,2,3,0,1:T(4,128)(2,1)}), bf16[2,8,4,20,1536]{4,2,3,0,1:T(4,128)(2,1)}, u32[]{:S(2)}, u32[]{:S(2)}) %all-to-all-start.1) | async-done | bytes 3932192 | tf_op jit(solution)/shard_map/all_to_all | solution.py:216
  1420.0 19.2 all-reduce.6
  1439.4 13.3 all-reduce.4
  1462.4 29.1 %reduce-scatter.19.cloned.1.call-done = bf16[384,1536]{1,0:T(8,128)(2,1)} async-done(((bf16[1536,1536]{1,0:T(8,128)(2,1)}), bf16[384,1536]{1,0:T(8,128)(2,1)}) %reduce-scatter.19.cloned.1.call-update) | async-done | bytes 1179664 | tf_op jit(solution)/shard_map/reduce_scatter | solution.py:385
  1494.9 84.5 %reduce-scatter.33.cloned.1.call-done = bf16[384,1536]{1,0:T(8,128)(2,1)} async-done(((bf16[1536,1536]{1,0:T(8,128)(2,1)}), bf16[384,1536]{1,0:T(8,128)(2,1)}) %reduce-scatter.33.cloned.1.call-update) | async-done | bytes 1179664 | tf_op jit(solution)/shard_map/reduce_scatter | solution.py:394
  1579.4 88.0 %reduce-scatter.31.cloned.1.call-done = bf16[384,1536]{1,0:T(8,128)(2,1)} async-done(((bf16[1536,1536]{1,0:T(8,128)(2,1)}), bf16[384,1536]{1,0:T(8,128)(2,1)}) %reduce-scatter.31.cloned.1.call-update) | async-done | bytes 1179664 | tf_op jit(solution)/shard_map/reduce_scatter | solution.py:394
  1677.2 155.0 %reduce-scatter.41.cloned.1.call-done = bf16[4,192,1536]{2,1,0:T(8,128)(2,1)} async-done(((bf16[4,768,1536]{2,1,0:T(8,128)(2,1)}), bf16[4,192,1536]{2,1,0:T(8,128)(2,1)}) %reduce-scatter.41.cloned.1.call-update) | async-done | bytes 2359312 | tf_op jit(solution)/shard_map/reduce_scatter | solution.py:400
  1832.1 164.4 %reduce-scatter.39.cloned.1.call-done = bf16[4,192,1536]{2,1,0:T(8,128)(2,1)} async-done(((bf16[4,768,1536]{2,1,0:T(8,128)(2,1)}), bf16[4,192,1536]{2,1,0:T(8,128)(2,1)}) %reduce-scatter.39.cloned.1.call-update) | async-done | bytes 2359312 | tf_op jit(solution)/shard_map/reduce_scatter | solution.py:400
  2001.8 311.7 %reduce-scatter.37.cloned.1.call-done = bf16[4,384,1536]{2,1,0:T(8,128)(2,1)} async-done(((bf16[4,1536,1536]{2,1,0:T(8,128)(2,1)}), bf16[4,384,1536]{2,1,0:T(8,128)(2,1)}) %reduce-scatter.37.cloned.1.call-update) | async-done | bytes 4718608 | tf_op jit(solution)/shard_map/reduce_scatter | solution.py:397
  2313.5 317.4 %reduce-scatter.35.cloned.1.call-done = bf16[4,384,1536]{2,1,0:T(8,128)(2,1)} async-done(((bf16[4,1536,1536]{2,1,0:T(8,128)(2,1)}), bf16[4,384,1536]{2,1,0:T(8,128)(2,1)}) %reduce-scatter.35.cloned.1.call-update) | async-done | bytes 4718608 | tf_op jit(solution)/shard_map/reduce_scatter | solution.py:397
  2630.9 9.0 convert_add_fusion
  2639.9 93.0 %all-reduce.9.cloned.1.call-done = (f32[384,1536]{1,0:T(8,128)}, f32[384,256]{1,0:T(8,128)}, f32[384,256]{1,0:T(8,128)}, f32[384,1536]{1,0:T(8,128)}) async-done(((f32[384,1536]{1,0:T(8,128)}, f32[384,256]{1,0:T(8,128)}, f32[384,256]{1,0:T(8,128)}, f32[384,1536]{1,0:T(8,128)}), (f32[384,1536]{1,0:T(8,128)}, f32[384,256]{1,0:T(8,128)}, f32[384,256]{1,0:T(8,128)}, ...) | async-done | bytes 5505040 | tf_op jit(solution)/shard_map/psum | solution.py:405
  (635 shorter events, 451.2 us)
Async XLA Ops:
  7.2 180.1 %all-gather.11.cloned.1.call-start = ((), (), s32[]{:S(2)}) async-start(), calls=%async_computation.22 | async-start | bytes 5898240 | tf_op jit(solution)/shard_map/all_gather | solution.py:96
  7.9 193.6 %all-gather.23.cloned.1.call-start = ((), (), s32[]{:S(2)}) async-start(), calls=%async_computation.28 | async-start | bytes 1179648 | tf_op jit(solution)/shard_map/all_gather | solution.py:142
  22.2 66.0 %copy-start.91 = (f32[1536]{0:T(1024)}, f32[1536]{0:T(1024)S(1)}, u32[]{:S(2)}) copy-start(f32[1536]{0:T(1024)S(1)} %reshape.1103) | copy-start | bytes 18436
  54.5 145.3 %copy-start.76 = (f32[128,64]{0,1:T(8,128)}, f32[128,64]{0,1:T(8,128)S(1)}, u32[]{:S(2)}) copy-start(f32[128,64]{0,1:T(8,128)S(1)} %get-tuple-element.133) | copy-start | bytes 98308
  57.5 154.4 %all-gather.25.cloned.1.call-start = ((), (), s32[]{:S(2)}) async-start(), calls=%async_computation.29 | async-start | bytes 1179648 | tf_op jit(solution)/shard_map/all_gather | solution.py:145
  89.8 192.8 %all-gather.17.cloned.1.call-start = ((), (), s32[]{:S(2)}) async-start(), calls=%async_computation.25 | async-start | bytes 5898240 | tf_op jit(solution)/shard_map/all_gather | solution.py:99
  90.4 216.6 %all-gather.13.cloned.1.call-start = ((), (), s32[]{:S(2)}) async-start(), calls=%async_computation.23 | async-start | bytes 1179648 | tf_op jit(solution)/shard_map/all_gather | solution.py:142
  91.2 244.7 %all-gather.15.cloned.1.call-start = ((), (), s32[]{:S(2)}) async-start(), calls=%async_computation.24 | async-start | bytes 1179648 | tf_op jit(solution)/shard_map/all_gather | solution.py:145
  92.4 572.9 %all-gather.19.cloned.1.call-start = ((), (), s32[]{:S(2)}) async-start(), calls=%async_computation.26 | async-start | bytes 23592960 | tf_op jit(solution)/shard_map/all_gather | solution.py:100
  118.7 197.1 %all-to-all-start.6 = ((bf16[2,8,4,20,1536]{4,2,3,0,1:T(4,128)(2,1)}), bf16[2,8,4,20,1536]{4,2,3,0,1:T(4,128)(2,1)}, u32[]{:S(2)}, u32[]{:S(2)}) async-start(bf16[2,8,4,20,1536]{4,2,3,0,1:T(4,128)(2,1)} %copy.350), calls=%async_computation.7 | async-start | bytes 7864320 | tf_op jit(solution)/shard_map/all_to_all | solution.py:233
  123.2 709.0 %all-gather.21.cloned.1.call-start = ((), (), s32[]{:S(2)}) async-start(), calls=%async_computation.27 | async-start | bytes 11796480 | tf_op jit(solution)/shard_map/all_gather | solution.py:101
  125.8 161.4 %copy-start.63 = (bf16[2,128,640]{2,1,0:T(8,128)(2,1)}, bf16[2,128,640]{2,1,0:T(8,128)(2,1)S(1)}, u32[]{:S(2)}) copy-start(bf16[2,128,640]{2,1,0:T(8,128)(2,1)S(1)} %fusion.112) | copy-start | bytes 983044
  146.4 920.2 %copy-start.82 = (f32[1536]{0:T(1024)}, f32[1536]{0:T(1024)S(1)}, u32[]{:S(2)}) copy-start(f32[1536]{0:T(1024)S(1)} %reshape.1104) | copy-start | bytes 18436
  211.9 70.8 %copy-start.128 = (f32[2,128]{1,0:T(2,128)S(1)}, f32[2,128]{1,0:T(2,128)}, u32[]{:S(2)}) copy-start(f32[2,128]{1,0:T(2,128)} %get-tuple-element.138) | copy-start | bytes 3076
  219.8 66.8 %copy-start.58 = (bf16[2,2,768,128]{3,2,1,0:T(8,128)(2,1)}, bf16[2,2,768,128]{3,2,1,0:T(8,128)(2,1)S(1)}, u32[]{:S(2)}) copy-start(bf16[2,2,768,128]{3,2,1,0:T(8,128)(2,1)S(1)} %get-tuple-element.148) | copy-start | bytes 2359300
  315.8 53.9 %all-to-all-start.2 = ((bf16[2,8,4,20,1536]{4,2,3,0,1:T(4,128)(2,1)}), bf16[2,8,4,20,1536]{4,2,3,0,1:T(4,128)(2,1)}, u32[]{:S(2)}, u32[]{:S(2)}) async-start(bf16[2,8,4,20,1536]{4,2,3,0,1:T(4,128)(2,1)} %copy.313), calls=%async_computation.2 | async-start | bytes 7864320 | tf_op jit(solution)/shard_map/all_to_all | solution.py:206
  349.7 716.9 %copy-start.3 = (f32[2,128,1536]{2,1,0:T(8,128)}, f32[2,128,1536]{2,1,0:T(8,128)S(1)}, u32[]{:S(2)}) copy-start(f32[2,128,1536]{2,1,0:T(8,128)S(1)} %get-tuple-element.145) | copy-start | bytes 4718596
  350.3 688.7 %copy-start.109 = (f32[2,128]{1,0:T(2,128)}, f32[2,128]{1,0:T(2,128)S(1)}, u32[]{:S(2)}) copy-start(f32[2,128]{1,0:T(2,128)S(1)} %get-tuple-element.130) | copy-start | bytes 3076
  369.7 477.9 %all-to-all-start = ((bf16[2,8,4,20,1536]{4,2,3,0,1:T(4,128)(2,1)}), bf16[2,8,4,20,1536]{4,2,3,0,1:T(4,128)(2,1)}, u32[]{:S(2)}, u32[]{:S(2)}) async-start(bf16[2,8,4,20,1536]{4,2,3,0,1:T(4,128)(2,1)} %copy.297), calls=%async_computation | async-start | bytes 7864320 | tf_op jit(solution)/shard_map/all_to_all | solution.py:206
  847.6 51.1 %all-to-all-start.4 = ((bf16[2,8,4,20,1536]{4,2,3,0,1:T(4,128)(2,1)}), bf16[2,8,4,20,1536]{4,2,3,0,1:T(4,128)(2,1)}, u32[]{:S(2)}, u32[]{:S(2)}) async-start(bf16[2,8,4,20,1536]{4,2,3,0,1:T(4,128)(2,1)} %copy.320), calls=%async_computation.4 | async-start | bytes 7864320 | tf_op jit(solution)/shard_map/all_to_all | solution.py:233
  898.7 51.3 %all-to-all-start.7 = ((bf16[2,8,4,20,1536]{4,2,3,0,1:T(4,128)(2,1)}), bf16[2,8,4,20,1536]{4,2,3,0,1:T(4,128)(2,1)}, u32[]{:S(2)}, u32[]{:S(2)}) async-start(bf16[2,8,4,20,1536]{4,2,3,0,1:T(4,128)(2,1)} %copy.352), calls=%async_computation.8 | async-start | bytes 7864320 | tf_op jit(solution)/shard_map/all_to_all | solution.py:254
  949.9 50.9 %all-to-all-start.5 = ((bf16[2,8,4,20,1536]{4,2,3,0,1:T(4,128)(2,1)}), bf16[2,8,4,20,1536]{4,2,3,0,1:T(4,128)(2,1)}, u32[]{:S(2)}, u32[]{:S(2)}) async-start(bf16[2,8,4,20,1536]{4,2,3,0,1:T(4,128)(2,1)} %copy.322), calls=%async_computation.5 | async-start | bytes 7864320 | tf_op jit(solution)/shard_map/all_to_all | solution.py:254
  957.5 60.6 %copy-start.38 = (bf16[1,1024,256]{1,2,0:T(8,128)(2,1)}, bf16[1,1024,256]{1,2,0:T(8,128)(2,1)S(1)}, u32[]{:S(2)}) copy-start(bf16[1,1024,256]{1,2,0:T(8,128)(2,1)S(1)} %get-tuple-element.68) | copy-start | bytes 1572868
  1000.8 50.9 %all-to-all-start.3 = ((bf16[2,8,4,20,1536]{4,2,3,0,1:T(4,128)(2,1)}), bf16[2,8,4,20,1536]{4,2,3,0,1:T(4,128)(2,1)}, u32[]{:S(2)}, u32[]{:S(2)}) async-start(bf16[2,8,4,20,1536]{4,2,3,0,1:T(4,128)(2,1)} %copy.315), calls=%async_computation.3 | async-start | bytes 7864320 | tf_op jit(solution)/shard_map/all_to_all | solution.py:216
  1005.4 159.6 %reduce-scatter.15.cloned.1.call-start = ((), (), s32[]{:S(2)}) async-start(), calls=%async_computation.30 | async-start | bytes 4718592 | tf_op jit(solution)/shard_map/reduce_scatter | solution.py:336
  1111.1 103.4 %reduce-scatter.17.cloned.1.call-start = ((), (), s32[]{:S(2)}) async-start(), calls=%async_computation.31 | async-start | bytes 4718592 | tf_op jit(solution)/shard_map/reduce_scatter | solution.py:336
  1164.9 50.7 %copy-start.77 = (f32[128,64]{0,1:T(8,128)S(1)}, f32[128,64]{0,1:T(8,128)}, u32[]{:S(2)}) copy-start(f32[128,64]{0,1:T(8,128)} %copy-done.76) | copy-start | bytes 98308
  1164.9 50.7 %copy-start.89 = (f32[128,64]{0,1:T(8,128)S(1)}, f32[128,64]{0,1:T(8,128)}, u32[]{:S(2)}) copy-start(f32[128,64]{0,1:T(8,128)} %get-tuple-element.131) | copy-start | bytes 98308
  1164.9 51.6 %copy-start.18 = (bf16[1,2,128,1536]{3,2,1,0:T(8,128)(2,1)S(1)}, bf16[1,2,128,1536]{3,2,1,0:T(8,128)(2,1)}, u32[]{:S(2)}) copy-start(bf16[1,2,128,1536]{3,2,1,0:T(8,128)(2,1)} %copy-done.16) | copy-start | bytes 2359300
  1164.9 293.9 %reduce-scatter.25.cloned.1.call-start = ((), (), s32[]{:S(2)}) async-start(), calls=%async_computation.35 | async-start | bytes 983040 | tf_op jit(solution)/shard_map/reduce_scatter | solution.py:388
  1165.0 55.5 %copy-start.15 = (bf16[1,2,128,1536]{3,2,1,0:T(8,128)(2,1)S(1)}, bf16[1,2,128,1536]{3,2,1,0:T(8,128)(2,1)}, u32[]{:S(2)}) copy-start(bf16[1,2,128,1536]{3,2,1,0:T(8,128)(2,1)} %copy-done.13) | copy-start | bytes 2359300
  1217.9 240.9 %reduce-scatter.23.cloned.1.call-start = ((), (), s32[]{:S(2)}) async-start(), calls=%async_computation.34 | async-start | bytes 983040 | tf_op jit(solution)/shard_map/reduce_scatter | solution.py:388
  1221.8 238.8 %reduce-scatter.29.cloned.1.call-start = ((), (), s32[]{:S(2)}) async-start(), calls=%async_computation.37 | async-start | bytes 983040 | tf_op jit(solution)/shard_map/reduce_scatter | solution.py:391
  1224.3 236.4 %reduce-scatter.27.cloned.1.call-start = ((), (), s32[]{:S(2)}) async-start(), calls=%async_computation.36 | async-start | bytes 983040 | tf_op jit(solution)/shard_map/reduce_scatter | solution.py:391
  1232.1 230.3 %reduce-scatter.21.cloned.1.call-start = ((), (), s32[]{:S(2)}) async-start(), calls=%async_computation.33 | async-start | bytes 5898240 | tf_op jit(solution)/shard_map/reduce_scatter | solution.py:385
  1256.6 234.9 %reduce-scatter.19.cloned.1.call-start = ((), (), s32[]{:S(2)}) async-start(), calls=%async_computation.32 | async-start | bytes 5898240 | tf_op jit(solution)/shard_map/reduce_scatter | solution.py:385
  1262.1 317.3 %reduce-scatter.33.cloned.1.call-start = ((), (), s32[]{:S(2)}) async-start(), calls=%async_computation.39 | async-start | bytes 5898240 | tf_op jit(solution)/shard_map/reduce_scatter | solution.py:394
  1267.5 399.8 %reduce-scatter.31.cloned.1.call-start = ((), (), s32[]{:S(2)}) async-start(), calls=%async_computation.38 | async-start | bytes 5898240 | tf_op jit(solution)/shard_map/reduce_scatter | solution.py:394
  1272.8 559.3 %reduce-scatter.41.cloned.1.call-start = ((), (), s32[]{:S(2)}) async-start(), calls=%async_computation.43 | async-start | bytes 11796480 | tf_op jit(solution)/shard_map/reduce_scatter | solution.py:400
  1284.8 711.7 %reduce-scatter.39.cloned.1.call-start = ((), (), s32[]{:S(2)}) async-start(), calls=%async_computation.42 | async-start | bytes 11796480 | tf_op jit(solution)/shard_map/reduce_scatter | solution.py:400
  1296.7 1016.8 %reduce-scatter.37.cloned.1.call-start = ((), (), s32[]{:S(2)}) async-start(), calls=%async_computation.41 | async-start | bytes 23592960 | tf_op jit(solution)/shard_map/reduce_scatter | solution.py:397
  1315.3 1315.6 %reduce-scatter.35.cloned.1.call-start = ((), (), s32[]{:S(2)}) async-start(), calls=%async_computation.40 | async-start | bytes 23592960 | tf_op jit(solution)/shard_map/reduce_scatter | solution.py:397
  1348.2 51.0 %all-to-all-start.1 = ((bf16[2,8,4,20,1536]{4,2,3,0,1:T(4,128)(2,1)}), bf16[2,8,4,20,1536]{4,2,3,0,1:T(4,128)(2,1)}, u32[]{:S(2)}, u32[]{:S(2)}) async-start(bf16[2,8,4,20,1536]{4,2,3,0,1:T(4,128)(2,1)} %copy.299), calls=%async_computation.1 | async-start | bytes 7864320 | tf_op jit(solution)/shard_map/all_to_all | solution.py:216
  1352.9 1380.0 %all-reduce.9.cloned.1.call-start = ((), (), s32[]{:S(2)}) async-start(), calls=%async_computation.44 | async-start | bytes 11010048 | tf_op jit(solution)/shard_map/psum | solution.py:405
  1354.6 50.8 %copy-start.69 = (f32[2,128,1536]{2,1,0:T(8,128)S(1)}, f32[2,128,1536]{2,1,0:T(8,128)}, u32[]{:S(2)}) copy-start(f32[2,128,1536]{2,1,0:T(8,128)} %get-tuple-element.64) | copy-start | bytes 4718596
  1354.6 50.8 %copy-start.106 = (s32[2,128,4]{1,2,0:T(4,128)S(1)}, s32[2,128,4]{1,2,0:T(4,128)}, u32[]{:S(2)}) copy-start(s32[2,128,4]{1,2,0:T(4,128)} %copy-done.105) | copy-start | bytes 12292
  1354.6 50.8 %copy-start.112 = (f32[2,128,4]{1,2,0:T(4,128)S(1)}, f32[2,128,4]{1,2,0:T(4,128)}, u32[]{:S(2)}) copy-start(f32[2,128,4]{1,2,0:T(4,128)} %get-tuple-element.110) | copy-start | bytes 12292
  1354.6 50.8 %copy-start.139 = (pred[2,128]{1,0:T(4,128)(4,1)S(1)}, pred[2,128]{1,0:T(4,128)(4,1)}, u32[]{:S(2)}) copy-start(pred[2,128]{1,0:T(4,128)(4,1)} %copy-done.138) | copy-start | bytes 772
  (152 other events, 1075.4 us)
Sparse Core Ops, SparseCore 0:
  9.6 116.0 all-gather.10
  127.6 36.5 all-gather.22
  166.1 25.6 all-gather.24
  193.2 89.4 all-gather.16
  285.0 22.0 all-gather.12
  309.3 26.4 all-gather.14
  337.5 327.8 all-gather.18
  666.9 165.2 all-gather.20
  1111.2 47.7 reduce-scatter.14
  1165.0 49.4 reduce-scatter.16
  1218.0 23.2 reduce-scatter.24
  1243.5 22.5 reduce-scatter.22
  1268.4 22.5 reduce-scatter.28
  1293.1 22.6 reduce-scatter.26
  1318.5 84.4 reduce-scatter.20
  1405.2 86.2 reduce-scatter.18
  1493.7 85.6 reduce-scatter.32
  1581.5 85.7 reduce-scatter.30
  1670.3 161.8 reduce-scatter.40
  1834.3 162.1 reduce-scatter.38
  1998.9 314.5 reduce-scatter.36
  2316.0 314.8 reduce-scatter.34
  2635.7 97.1 all-reduce.8
where the time goes:
time: 2750 us
  waiting for transfers between devices  1920 us (70%)
  matrix products  341 us (12%)
  local copies, waits for them, and re-layouts  203 us (7%)
  blocking collectives  118 us (4%)
  other arithmetic  104 us (4%)
  starting transfers between devices  40.1 us (1%)
    reduce_scatter x2, waiting for transfers between devices, local(): lax.psum_scatter(grads[6].astype(jnp.bfloat16), 'fsdp', scatter_dimension...  629 us
    reduce_scatter x2, waiting for transfers between devices, local(): lax.psum_scatter(grads[7].astype(jnp.bfloat16), 'fsdp', scatter_dimension...  319 us
    all_gather x1, waiting for transfers between devices, local(): lax.all_gather(up_weight, 'fsdp', axis=1, tiled=True)  291 us
    reduce_scatter x2, waiting for transfers between devices, local(): lax.psum_scatter(grads[5].astype(jnp.bfloat16), 'fsdp', scatter_dimension...  172 us
    all_gather x1, waiting for transfers between devices, local(): lax.all_gather(down_weight, 'fsdp', axis=1, tiled=True)  150 us
    psum x1, waiting for transfers between devices, local(): lax.psum((totals[0], totals[1], totals[2], totals[3], totals[4], totals[5...  93 us
    all_gather x1, waiting for transfers between devices, local(): lax.all_gather(output_weight, 'fsdp', axis=0, tiled=True)  62.5 us
  transfers between devices with their start and end apart: 31, of which 20 were waited for; matrix products, arithmetic and copies ran while one was open for 20% of the time, Pallas kernels for 0%

commit v1 on v0

v1 whole, which is shorter than its diff:
```python
import jax
import jax.numpy as jnp
from jax import lax
from jax.experimental import pallas as pl
from jax.experimental.pallas import tpu as pltpu
from jax.sharding import PartitionSpec as P

H = 12
KV = 2
HD = 128
TOP = 4
EXPERTS = 32
EPSILON = 1e-06
ROPE_BASE = 10000.0
NEGATIVE = -1e30
F32 = jnp.float32
BF16 = jnp.bfloat16


def angle_tables(positions):
    half_dim = HD // 2
    frequency = ROPE_BASE ** (-(jnp.arange(half_dim, dtype=F32) * 2.0 / HD))
    angles = positions.astype(F32)[:, None] * frequency[None, :]
    return jnp.cos(angles), jnp.sin(angles)


def rotate(vectors, cosine, sine):
    half_dim = HD // 2
    leading = vectors[..., :half_dim]
    trailing = vectors[..., half_dim:]
    cosine, sine = cosine[:, None, :], sine[:, None, :]
    return jnp.concatenate(
        [leading * cosine - trailing * sine, trailing * cosine + leading * sine], axis=-1
    )


def norm_forward(values, gain_row):
    inverse = lax.rsqrt(jnp.mean(values * values, axis=-1, keepdims=True) + EPSILON)
    return values * inverse * gain_row, inverse


def norm_backward(values, inverse, gain_row, upstream):
    gain_grad = jnp.sum(upstream * values * inverse, axis=0)
    scaled = upstream * gain_row
    projected = jnp.mean(scaled * values, axis=-1, keepdims=True)
    return inverse * scaled - values * inverse**3 * projected, gain_grad


def mm(a, b):
    return jnp.dot(a, b, preferred_element_type=F32)


def mm_nt(a, b):
    return lax.dot_general(a, b, (((1,), (1,)), ((), ())), preferred_element_type=F32)


def mm_tn(a, b):
    return lax.dot_general(a, b, (((0,), (0,)), ((), ())), preferred_element_type=F32)


VMEM_LIMIT = 60 * 1024 * 1024


def stack_heads(block, groups):
    return jnp.concatenate([block[:, h * HD : (h + 1) * HD] for h in range(groups)], axis=0)


def masked_scores(stacked, keys, first, length, groups):
    tl = stacked.shape[0] // groups
    total = keys.shape[0]
    scores = mm_nt(stacked, keys) * HD ** (-0.5)
    key_at = lax.broadcasted_iota(jnp.int32, (tl, total), 1)
    query_at = lax.broadcasted_iota(jnp.int32, (tl, total), 0) + first
    allowed = (key_at <= query_at) & (key_at < length)
    scores = scores.reshape(groups, tl, total)
    return jnp.where(allowed[None], scores, NEGATIVE).reshape(groups * tl, total)


def attend_kernel(groups, info, q_ref, kv_ref, att_ref, lse_ref):
    tl = q_ref.shape[1]
    stacked = stack_heads(q_ref[0], groups)
    scores = masked_scores(
        stacked, kv_ref[0, :, :HD], info[0], info[1 + pl.program_id(0)], groups
    )
    top = jnp.max(scores, axis=-1, keepdims=True)
    shares = jnp.exp(scores - top)
    total = jnp.sum(shares, axis=-1, keepdims=True)
    out = mm(shares.astype(BF16), kv_ref[0, :, HD:]) / total
    lse = top + jnp.log(total)
    for h in range(groups):
        at = slice(h * tl, (h + 1) * tl)
        att_ref[0, :, h * HD : (h + 1) * HD] = out[at].astype(BF16)
        lse_ref[0, 0, :, h : h + 1] = lse[at]


def attend_back_kernel(groups, info, q_ref, kv_ref, da_ref, lse_ref, dq_ref, dkv_ref):
    tl = q_ref.shape[1]
    keys, values = kv_ref[0, :, :HD], kv_ref[0, :, HD:]
    stacked = stack_heads(q_ref[0], groups)
    scores = masked_scores(stacked, keys, info[0], info[1 + pl.program_id(0)], groups)
    lse = jnp.concatenate([lse_ref[0, 0, :, h : h + 1] for h in range(groups)], axis=0)
    probs = jnp.exp(scores - lse)
    grads = stack_heads(da_ref[0], groups)
    d_probs = mm_nt(grads, values)
    delta = jnp.sum(probs * d_probs, axis=-1, keepdims=True)
    d_scores = (probs * (d_probs - delta)).astype(BF16)
    dq = mm(d_scores, keys) * HD ** (-0.5)
    for h in range(groups):
        dq_ref[0, :, h * HD : (h + 1) * HD] = dq[h * tl : (h + 1) * tl]
    dk = mm_tn(d_scores, stacked) * HD ** (-0.5)
    dv = mm_tn(probs.astype(BF16), grads)
    shape = dkv_ref.shape[:1] + (tl, HD)
    dkv_ref[:, 0, :, :HD] = dk.reshape(shape).astype(BF16)
    dkv_ref[:, 0, :, HD:] = dv.reshape(shape).astype(BF16)


def attention(queries, kv_all, info):
    nseq, tl, width = queries.shape
    total = kv_all.shape[1]
    groups = H // KV
    return pl.pallas_call(
        lambda *refs: attend_kernel(groups, *refs),
        grid_spec=pltpu.PrefetchScalarGridSpec(
            num_scalar_prefetch=1,
            grid=(nseq, KV),
            in_specs=[
                pl.BlockSpec((1, tl, groups * HD), lambda s, n, info: (s, 0, n)),
                pl.BlockSpec((1, total, 2 * HD), lambda s, n, info: (s, 0, n)),
            ],
            out_specs=[
                pl.BlockSpec((1, tl, groups * HD), lambda s, n, info: (s, 0, n)),
                pl.BlockSpec((1, 1, tl, HD), lambda s, n, info: (s, n, 0, 0)),
            ],
        ),
        out_shape=[
            jax.ShapeDtypeStruct((nseq, tl, width), BF16),
            jax.ShapeDtypeStruct((nseq, KV, tl, HD), F32),
        ],
        compiler_params=pltpu.CompilerParams(vmem_limit_bytes=VMEM_LIMIT),
        cost_estimate=pl.CostEstimate(
            flops=28 * nseq * tl * width * total,
            bytes_accessed=4 * queries.size * 2 + 2 * kv_all.size,
            transcendentals=nseq * H * tl * total,
        ),
    )(info, queries, kv_all)


def attention_back(queries, kv_all, d_att, lse, info, ctx_count):
    nseq, tl, width = queries.shape
    total = kv_all.shape[1]
    groups = H // KV
    return pl.pallas_call(
        lambda *refs: attend_back_kernel(groups, *refs),
        grid_spec=pltpu.PrefetchScalarGridSpec(
            num_scalar_prefetch=1,
            grid=(nseq, KV),
            in_specs=[
                pl.BlockSpec((1, tl, groups * HD), lambda s, n, info: (s, 0, n)),
                pl.BlockSpec((1, total, 2 * HD), lambda s, n, info: (s, 0, n)),
                pl.BlockSpec((1, tl, groups * HD), lambda s, n, info: (s, 0, n)),
                pl.BlockSpec((1, 1, tl, HD), lambda s, n, info: (s, n, 0, 0)),
            ],
            out_specs=[
                pl.BlockSpec((1, tl, groups * HD), lambda s, n, info: (s, 0, n)),
                pl.BlockSpec((ctx_count, 1, tl, 2 * HD), lambda s, n, info: (0, s, 0, n)),
            ],
        ),
        out_shape=[
            jax.ShapeDtypeStruct((nseq, tl, width), F32),
            jax.ShapeDtypeStruct((ctx_count, nseq, tl, KV * 2 * HD), BF16),
        ],
        compiler_params=pltpu.CompilerParams(vmem_limit_bytes=VMEM_LIMIT),
        cost_estimate=pl.CostEstimate(
            flops=36 * nseq * tl * width * total,
            bytes_accessed=6 * queries.size * 2 + 4 * kv_all.size,
            transcendentals=nseq * H * tl * total,
        ),
    )(info, queries, kv_all, d_att, lse)


def expert_kernel(sides, merged, *refs):
    info = refs[0]
    xs = refs[1 : 1 + sides]
    gs = refs[1 + sides : 1 + 2 * sides]
    count = 11 if merged else 2
    weights = refs[1 + 2 * sides : 1 + 2 * sides + count]
    at = 1 + 2 * sides + count
    din_ref, wy_ref = refs[at : at + 2]
    at = at + 2
    out_refs = refs[at : at + (1 if merged else 2)]
    at = at + (1 if merged else 2)
    up, down, x_t, act_t, dgu, dy, act_s, pre, wide, gup, gdn, sems = refs[at:]
    step, steps = pl.program_id(0), pl.num_programs(0)
    D, W = up.shape[0], down.shape[0]
    tile = wide.shape[0]
    tw = 256 if W % 256 == 0 else 128
    td = 256

    wl = W // 4

    def shard_rows(source, chunk):
        if chunk == 2:
            return down, gdn, pl.ds(pl.multiple_of(source * wl, 16), wl)
        return up, gup, pl.ds(pl.multiple_of((2 * source + chunk) * wl, 16), wl)

    def loads():
        if not merged:
            pairs = [(weights[0].at[info[2]], up), (weights[1].at[info[2]], down)]
        else:
            pairs = []
            for k in range(4):
                for chunk in range(3):
                    to, _, at = shard_rows(lax.rem(info[0] + 4 - k, 4), chunk)
                    if k:
                        block = weights[2 + 3 * (k - 1) + chunk]
                    elif chunk < 2:
                        block = weights[0].at[info[2], pl.ds(chunk * wl, wl)]
                    else:
                        block = weights[1].at[info[2]]
                    pairs.append((block, to.at[at]))
        return [pltpu.make_async_copy(a, b, sems.at[i]) for i, (a, b) in enumerate(pairs)]

    def put(ref, columns, block):
        per = tile // sides
        shape = (ref.shape[0], ref.shape[2], block.shape[1])
        for i in range(sides):
            ref[:, i, :, columns] = block[i * per : (i + 1) * per].reshape(shape)

    @pl.when(step == 0)
    def _():
        copies = loads()
        for copy in copies:
            copy.start()
        for copy in copies:
            copy.wait()

    rows = pl.ds(pl.multiple_of(step * tile, 128), tile)
    x = jnp.concatenate([r[...].reshape(-1, D) for r in xs], axis=0)
    g_aug = jnp.concatenate([r[...].reshape(-1, D + HD) for r in gs], axis=0)
    x_t[:, rows] = x.T
    lane = lax.broadcasted_iota(jnp.int32, (tile, HD), 1)
    picked = (lane == info[1]) | (lane == info[1] + HD // 2)
    w = jnp.sum(jnp.where(picked, g_aug[:, D:].astype(F32), 0.0), axis=1, keepdims=True)
    wide[...] = g_aug[:, :D]
    dy[rows, :] = (g_aug[:, :D].astype(F32) * w).astype(BF16)

    @pl.loop(0, W // tw)
    def _(t):
        a = pl.ds(pl.multiple_of(t * tw, 128), tw)
        b = pl.ds(pl.multiple_of(W + t * tw, 128), tw)
        gate = mm(x, up[:, a])
        lift = mm(x, up[:, b])
        pre[:, a] = gate
        pre[:, b] = lift
        act = gate / (1.0 + jnp.exp(-gate)) * lift
        act = act.astype(BF16)
        act_s[:, a] = act
        act_t[a, rows] = act.T

    def out_step(t, total):
        a = pl.ds(pl.multiple_of(t * td, 128), td)
        y = mm(act_s[...], down[:, a])
        put(wy_ref, a, (y * w).astype(BF16))
        return total + jnp.sum(y * wide[:, a].astype(F32), axis=1, keepdims=True)

    router = lax.fori_loop(0, D // td, out_step, jnp.zeros((tile, 1), F32))
    extra = jnp.where(lane == info[1], router, 0.0).astype(BF16)
    put(wy_ref, pl.ds(D, HD), extra)

    @pl.loop(0, W // tw)
    def _(t):
        a = pl.ds(pl.multiple_of(t * tw, 128), tw)
        b = pl.ds(pl.multiple_of(W + t * tw, 128), tw)
        d_act = mm_nt(dy[rows, :], down[a, :])
        gate, lift = pre[:, a], pre[:, b]
        sig = 1.0 / (1.0 + jnp.exp(-gate))
        dgu[rows, a] = (d_act * lift * sig * (1.0 + gate * (1.0 - sig))).astype(BF16)
        dgu[rows, b] = (d_act * gate * sig).astype(BF16)

    @pl.loop(0, D // td)
    def _(t):
        a = pl.ds(pl.multiple_of(t * td, 128), td)
        put(din_ref, a, mm_nt(dgu[rows, :], up[a, :]).astype(BF16))

    @pl.when(step == steps - 1)
    def _():
        @pl.loop(0, D // td)
        def _(t):
            a = pl.ds(pl.multiple_of(t * td, 128), td)
            gup[a, :] = mm(x_t[a, :], dgu[...]).astype(BF16)

        @pl.loop(0, W // tw)
        def _(t):
            a = pl.ds(pl.multiple_of(t * tw, 128), tw)
            gdn[a, :] = mm(act_t[a, :], dy[...]).astype(BF16)

        if merged:
            pairs = []
            for k in range(4):
                for chunk in range(3):
                    _, block, at = shard_rows(lax.rem(info[0] + k, 4), chunk)
                    pairs.append((block.at[at], out_refs[0].at[k, chunk]))
        else:
            pairs = [(gup, out_refs[0]), (gdn, out_refs[1])]
        copies = [pltpu.make_async_copy(a, b, sems.at[i]) for i, (a, b) in enumerate(pairs)]
        for copy in copies:
            copy.start()
        for copy in copies:
            copy.wait()


def run_expert(piece, xs, gs, weights, info, merged):
    C, mine, slots, D = xs[0].shape
    sides = len(xs)
    W = weights[0].shape[2] // 2
    per_step = C
    while per_step > 1 and (per_step * sides * slots > 640 or C % per_step):
        per_step -= 1
    tile = per_step * sides * slots
    rows = C * sides * slots

    def spec(width, at):
        return pl.BlockSpec((per_step, 1, slots, width), lambda i, info: (i, at, 0, 0))

    def out_spec(width):
        return pl.BlockSpec((per_step, sides, slots, width), lambda i, info: (i, 0, 0, 0))

    any_spec = pl.BlockSpec(memory_space=pl.ANY)
    if merged:
        grads = [jax.ShapeDtypeStruct((4, 3) + weights[2].shape, BF16)]
    else:
        grads = [jax.ShapeDtypeStruct((D, 2 * W), BF16), jax.ShapeDtypeStruct((W, D), BF16)]
    return pl.pallas_call(
        lambda *refs: expert_kernel(sides, merged, *refs),
        grid_spec=pltpu.PrefetchScalarGridSpec(
            num_scalar_prefetch=1,
            grid=(C // per_step,),
            in_specs=[spec(D, piece)] * sides
            + [spec(D + HD, piece)] * sides
            + [any_spec] * len(weights),
            out_specs=[out_spec(D), out_spec(D + HD)] + [any_spec] * len(grads),
            scratch_shapes=[
                pltpu.VMEM((D, 2 * W), BF16),
                pltpu.VMEM((W, D), BF16),
                pltpu.VMEM((D, rows), BF16),
                pltpu.VMEM((W, rows), BF16),
                pltpu.VMEM((rows, 2 * W), BF16),
                pltpu.VMEM((rows, D), BF16),
                pltpu.VMEM((tile, W), BF16),
                pltpu.VMEM((tile, 2 * W), F32),
                pltpu.VMEM((tile, D), BF16),
                pltpu.VMEM((D, 2 * W), BF16),
                pltpu.VMEM((W, D), BF16),
                pltpu.SemaphoreType.DMA((12,)),
            ],
        ),
        out_shape=[jax.ShapeDtypeStruct((C, sides, slots, n), BF16) for n in (D, D + HD)]
        + grads,
        compiler_params=pltpu.CompilerParams(vmem_limit_bytes=VMEM_LIMIT),
        cost_estimate=pl.CostEstimate(
            flops=38 * rows * D * W,
            bytes_accessed=8 * rows * D + 24 * D * W,
            transcendentals=2 * rows * W,
        ),
    )(info, *xs, *gs, *weights)


def local(
    tokens,
    lengths,
    expert_picks,
    router_weights,
    first_gain,
    second_gain,
    query_weight,
    key_weight,
    value_weight,
    output_weight,
    up_weight,
    down_weight,
    cotangent,
):
    batches, seqs_here, tl, D = tokens.shape
    C = lax.axis_size("ctx")
    F = lax.axis_size("fsdp")
    c = lax.axis_index("ctx")
    f = lax.axis_index("fsdp")
    split = max(1, C // EXPERTS)
    pieces = up_weight.shape[0]
    W = up_weight.shape[2] // 2
    merged = pieces % 2 == 0 and F == 4 and 2 * W == D
    share = 2 if merged else 1
    mine = pieces // share
    role = f % share
    nseq = batches * seqs_here
    cap = max(2, (5 * tl * TOP + 4 * EXPERTS - 1) // (4 * EXPERTS))
    while nseq * cap % 16:
        cap += 1
    slots = nseq * cap
    rows = nseq * tl
    L = C * tl
    width = H * HD
    Dl = query_weight.shape[0]
    cut = Dl // C

    positions = c * tl + jnp.arange(tl, dtype=jnp.int32)
    cosine, sine = angle_tables(positions)
    lens = lengths.reshape(nseq)
    live = (positions[None, :] < lens[:, None]).reshape(rows)
    live_rows = live.astype(F32)[:, None]

    def gate(*values):
        return lax.optimization_barrier(values)

    def shift(block, k):
        return lax.ppermute(block, "fsdp", [(i, (i + k) % F) for i in range(F)])

    def fsdp_gather(block):
        got = [shift(block, k) for k in range(F - 1, 0, -1)]
        ring = jnp.stack(got + [block] + got)
        return lax.dynamic_slice_in_dim(ring, F - 1 - f, F, 0)

    def fsdp_scatter_sum(parts):
        total = lax.dynamic_index_in_dim(parts, f, 0, keepdims=False).astype(F32)
        for k in range(1, F):
            block = lax.dynamic_index_in_dim(parts, (f + k) % F, 0, keepdims=False)
            total = total + shift(block, k).astype(F32)
        return total

    def swap(block):
        return lax.ppermute(block, "fsdp", [(i, i ^ 1) for i in range(F)])

    def exchange(blocks):
        return lax.all_to_all(blocks, "ctx", 0, 0, tiled=True)

    def ctx_gather(lines):
        return lax.all_gather(lines, "ctx", axis=1, tiled=True).reshape(D, -1)

    def part_of(weight):
        return lax.dynamic_slice_in_dim(weight, c * cut, cut, 0)

    key_value = jnp.concatenate(
        [
            w[:, h * HD : (h + 1) * HD]
            for h in range(KV)
            for w in (key_weight, value_weight)
        ],
        axis=1,
    )
    query_part, out_part = part_of(query_weight), part_of(output_weight)
    gains = fsdp_gather(jnp.stack([first_gain, second_gain]))
    first_scale = gains[:, 0].reshape(D).astype(F32)
    second_scale = gains[:, 1].reshape(D).astype(F32)
    kv_lines, query_lines = fsdp_gather(part_of(key_value)), fsdp_gather(query_part)

    messages = {}
    grads_out = []

    def operand(name):
        kind, j, chunk, k = name
        if kind == "g":
            return grads_out[j][k, chunk]
        at = ((f + k) % share) * mine + j
        size = (1, W // F, up_weight.shape[2])
        if chunk == 2:
            return lax.dynamic_slice(down_weight, (at, 0, 0), size)[0]
        return lax.dynamic_slice(up_weight, (at, chunk * (W // F), 0), size)[0]

    def step(need, values, go):
        if not merged:
            return lax.optimization_barrier(values)
        fresh = tuple(operand(name) for name in go)
        got, values, fresh = lax.optimization_barrier(
            (tuple(messages[name] for name in need), values, fresh)
        )
        messages.update(zip(need, got))
        messages.update((name, shift(block, name[3])) for name, block in zip(go, fresh))
        return values

    def names(kind, j, *codes):
        return [(kind, j, "abc".index(code[0]), int(code[1])) for code in codes]

    picks = expert_picks.reshape(rows, TOP)
    gates = router_weights.reshape(rows, TOP)
    cot = cotangent.reshape(rows, D)
    expert_ids = jnp.arange(EXPERTS, dtype=jnp.int32)
    hit = picks[:, :, None] == expert_ids
    by_expert = jnp.sum(jnp.where(hit, gates[:, :, None], 0.0), axis=1) * live_rows
    high = by_expert.astype(BF16)
    low = (by_expert - high.astype(F32)).astype(BF16)
    gap = jnp.zeros((rows, HD // 2 - EXPERTS), BF16)
    cot_wide = jnp.concatenate([cot, high, gap, low, gap], axis=1)
    number = jnp.arange(C)[:, None] * pieces + role * mine + jnp.arange(mine)[None, :]
    expert_of = (number // split).reshape(C * mine)
    earlier = jnp.tril(jnp.ones((tl, tl), BF16), -1)
    pick_map = (expert_ids[:, None] == expert_of[None, :]).astype(BF16)

    def route(wide):
        match = wide[:, D : D + EXPERTS] > 0
        ranks = jnp.einsum(
            "ab,sbe->sae",
            earlier,
            match.astype(BF16).reshape(nseq, tl, -1),
            preferred_element_type=F32,
        )
        base = (jnp.arange(nseq) * cap)[:, None, None]
        code = jnp.where(match, (ranks + base).reshape(rows, -1), -1.0).astype(BF16)
        code = mm_tn(pick_map, code.T)
        chosen = code[:, None, :] == jnp.arange(slots, dtype=F32)[None, :, None]
        return chosen.astype(BF16).reshape(C, mine, slots, rows)

    def to_slots(sel, source):
        out = mm(sel.reshape(C * mine * slots, rows), source)
        return out.astype(BF16).reshape(C, mine, slots, -1)

    sels = [route(cot_wide)]

    inputs = tokens.reshape(rows, D).astype(F32)
    normed, inverse_one = norm_forward(inputs, first_scale)
    normed_low = normed.astype(BF16)
    now = names("w", 0, "a1", "b1")
    kv_lines, query_lines = step([], (kv_lines, query_lines), now)
    kv_full = ctx_gather(kv_lines)
    then, now = now, names("w", 0, "c1", "a3")
    kv_full, query_lines, out_part, cot_wide = step(
        then, (kv_full, query_lines, out_part, cot_wide), now
    )
    query_full = ctx_gather(query_lines)
    out_lines = fsdp_gather(out_part)
    g_in = [exchange(to_slots(sels[0], cot_wide))]
    kv_pre = mm(normed_low, kv_full).reshape(nseq, tl, KV, 2, HD)
    turned_key = rotate(kv_pre[..., 0, :], cosine, sine).astype(BF16)
    kv_low = jnp.stack([turned_key, kv_pre[..., 1, :].astype(BF16)], axis=3)
    kv_low = kv_low.reshape(nseq, tl, KV * 2 * HD)
    then, now = now, names("w", 0, "a2")
    query_full, kv_low, out_lines, cot_wide = step(
        then, (query_full, kv_low, out_lines, cot_wide), now
    )
    kv_all = lax.all_gather(kv_low, "ctx", axis=1, tiled=True)
    far_cot = swap(cot_wide) if share == 2 else cot_wide
    query_pre = mm(normed_low, query_full).reshape(nseq, tl, H, HD)
    queries = rotate(query_pre, cosine, sine).astype(BF16).reshape(nseq, tl, width)
    info = jnp.concatenate([(c * tl)[None], lens])
    then, now = now, names("w", 0, "b2")
    kv_all, queries, far_cot, g_in[0], out_lines = step(
        then, (kv_all, queries, far_cot, g_in[0], out_lines), now
    )
    out_full = ctx_gather(out_lines)
    attended, lse = attention(queries, kv_all, info)
    then, now = now, names("w", 0, "b3", "c3")
    attended, far_cot = step(then, (attended, far_cot), now)
    if share == 2:
        sels.append(route(far_cot))
        g_in.append(exchange(to_slots(sels[1], far_cot)))
    attended_low = attended.reshape(rows, width)
    hidden = inputs + live_rows * mm(attended_low, out_full)
    second, inverse_two = norm_forward(hidden, second_scale)
    second_low = second.astype(BF16)

    then, now = now, names("w", 0, "c2") + names("w", 1, "a2")
    (second_low,) = step(then, (second_low,), now)
    x_in = [exchange(to_slots(sels[0], second_low))]
    if share == 2:
        far = swap(second_low)
        then, now = now, names("w", 1, "a1", "b1", "c1")
        x_in[0], g_in[1], far = step(then, (x_in[0], g_in[1], far), now)
        x_in.append(exchange(to_slots(sels[1], far)))

    def expert(j):
        number_here = c * pieces + role * mine + j
        at = role * mine + j
        expert_info = jnp.stack([f, number_here // split, at])
        if merged:
            weights = [up_weight, down_weight]
            weights += [messages["w", j, chunk, k] for k in range(1, F) for chunk in range(3)]
        else:
            weights = [up_full, down_full]
        out = run_expert(j, x_in, g_in, weights, expert_info, merged)
        if merged:
            grads_out.append(out[2])
        return out

    if merged:
        then, now = now, names("w", 1, "b2", "c2")
        (x_in[1],) = step(then, (x_in[1],), now)
        outs = [expert(0)]
        then, now = now, names("w", 1, "a3", "b3", "c3")
        d_in, mixed = [outs[0][0]], [outs[0][1]]
        d_in[0], mixed[0], grads_out[0] = step(then, (d_in[0], mixed[0], grads_out[0]), now)
        d_in[0] = exchange(d_in[0])
        then, now = now, names("g", 0, "a2", "b2")
        d_in[0], mixed[0], x_in[0] = step(then, (d_in[0], mixed[0], x_in[0]), now)
        mixed[0] = exchange(mixed[0])
        outs.append(expert(1))
        then, now = now, names("g", 0, "c2", "a1")
        last, mixed[0], later, grads_out[1] = step(
            then, (outs[1][0], mixed[0], outs[1][1], grads_out[1]), now
        )
        d_in.append(exchange(last))
        mixed.append(later)
    else:
        up_full = lax.all_gather(up_weight, "fsdp", axis=1, tiled=True)
        down_full = lax.all_gather(down_weight, "fsdp", axis=1, tiled=True)
        outs = [expert(j) for j in range(mine)]
        d_in = [exchange(out[0]) for out in outs]
        mixed = [exchange(out[1]) for out in outs]

    def collect(backs):
        sums = []
        for i, sel in enumerate(sels):
            total = 0.0
            for j, back in enumerate(backs):
                total = total + mm_tn(
                    sel[:, j].reshape(C * slots, rows), back[:, i].reshape(C * slots, -1)
                )
            sums.append(total)
        return sums

    sums = collect(d_in)
    dispatch_grad = sums[0]
    if share == 2:
        then, now = now, names("g", 1, "a2")
        (far,) = step(then, (sums[1].astype(BF16),), now)
        dispatch_grad = dispatch_grad + swap(far).astype(F32)
        then, now = now, names("g", 0, "b1")
        dispatch_grad, mixed[1] = step(then, (dispatch_grad, mixed[1]), now)
        mixed[1] = exchange(mixed[1])

    upstream = cot.astype(F32)
    norm_grad, second_grads = norm_backward(hidden, inverse_two, second_scale, dispatch_grad)
    hidden_grad = upstream + norm_grad
    branch_grad = (live_rows * hidden_grad).astype(BF16)
    d_att = mm_nt(branch_grad, out_full).astype(BF16)
    then, now = now, names("g", 0, "c1", "a3")
    (d_att,) = step(then, (d_att,), now)
    query_grad, terms = attention_back(
        queries, kv_all, d_att.reshape(nseq, tl, width), lse, info, C
    )
    then, now = now, names("g", 0, "b3", "c3") + names("g", 1, "b2")
    (terms,) = step(then, (terms,), now)
    own_terms = lax.psum_scatter(terms, "ctx", scatter_dimension=0, tiled=False).astype(F32)
    own_terms = own_terms.reshape(nseq, tl, KV, 2, HD)

    def by_target(grad):
        return grad.astype(BF16).reshape(F, C, cut, -1).transpose(1, 0, 2, 3)

    def over_ctx(blocks):
        return jnp.sum(exchange(blocks).astype(F32), axis=0).astype(BF16)

    query_back = (
        rotate(query_grad.reshape(nseq, tl, H, HD), cosine, -sine)
        .astype(BF16)
        .reshape(rows, width)
    )
    projection_blocks = by_target(mm_tn(attended_low, branch_grad))
    query_blocks = by_target(mm_tn(normed_low, query_back))
    then, now = now, names("g", 1, "c2", "a1", "b1")
    own_terms, mixed, projection_blocks, query_blocks = step(
        then, (own_terms, mixed, projection_blocks, query_blocks), now
    )
    projection_rows = lax.psum_scatter(projection_blocks, "ctx", scatter_dimension=0, tiled=True)
    query_rows = over_ctx(query_blocks)
    key_back = rotate(own_terms[..., 0, :], cosine, -sine)
    kv_back = (
        jnp.stack([key_back, own_terms[..., 1, :]], axis=3).astype(BF16).reshape(rows, KV * 2 * HD)
    )
    normed_grad = mm_nt(query_back, query_full) + mm_nt(kv_back, kv_full)
    entry_grad, first_grads = norm_backward(inputs, inverse_one, first_scale, normed_grad)
    grad_tokens = hidden_grad + entry_grad
    gains_wide = jnp.pad(
        jnp.stack([first_grads, second_grads], axis=1), ((0, 0), (0, 2 * HD - 2))
    )
    kv_blocks = by_target(jnp.concatenate([mm_tn(normed_low, kv_back), gains_wide], axis=1))
    sums = collect(mixed)
    mixed_rows = sums[0]
    then, now = now, names("g", 1, "c1", "a3")
    far, query_rows, kv_blocks = step(then, (sums[-1].astype(BF16), query_rows, kv_blocks), now)
    if share == 2:
        mixed_rows = mixed_rows + swap(far).astype(F32)
    kv_rows = over_ctx(kv_blocks)
    query_rows = fsdp_scatter_sum(query_rows)
    then, now = now, []
    kv_rows, projection_rows = step(then, (kv_rows, projection_rows.reshape(F, cut, -1)), now)
    kv_rows, projection_rows = fsdp_scatter_sum(kv_rows), fsdp_scatter_sum(projection_rows)
    now = names("g", 1, "b3", "c3")
    query_rows, projection_rows, kv_rows = step([], (query_rows, projection_rows, kv_rows), now)
    wide = jnp.concatenate([query_rows, projection_rows, kv_rows], axis=1).astype(BF16)
    wide = lax.all_gather(wide, "ctx", axis=0, tiled=True).astype(F32)
    grad_query, grad_projection = wide[:, :width], wide[:, width : width + D]
    small = wide[:, width + D :]
    pair_width = 2 * KV * HD
    grad_pairs = small[:, :pair_width].reshape(Dl, KV, 2, HD)
    grad_first, grad_second = small[:, pair_width], small[:, pair_width + 1]

    block_rows = (hidden + mixed_rows[:, :D]).astype(BF16)
    router_by_expert = mixed_rows[:, D : D + EXPERTS]
    grad_router = jnp.sum(jnp.where(hit, router_by_expert[:, None, :], 0.0), axis=2)

    if merged:
        def both(k, own):
            parts = []
            for j in range(mine):
                first = grads_out[j][0] if own else jnp.stack(
                    [messages["g", j, chunk, 1] for chunk in range(3)]
                )
                other = jnp.stack([messages["g", j, chunk, k] for chunk in range(3)])
                parts.append(first.astype(F32) + other.astype(F32))
            return jnp.stack(parts).reshape(mine, -1, D)

        same, other = both(2, True), both(3, False)
        low_part = jnp.where(role == 0, same, other)
        high_part = jnp.where(role == 0, other, same)
        grad_both = jnp.concatenate([low_part, high_part], axis=0)
        grad_up, grad_down = grad_both[:, :Dl], grad_both[:, Dl:]
    else:
        grad_up, grad_down = [
            lax.psum_scatter(
                jnp.stack([out[2 + i] for out in outs]), "fsdp", scatter_dimension=1, tiled=True
            ).astype(F32)
            for i in range(2)
        ]

    shape = (batches, seqs_here, tl)
    return (
        block_rows.reshape(shape + (D,)),
        grad_tokens.reshape(shape + (D,)),
        grad_router.reshape(shape + (TOP,)),
        grad_first,
        grad_second,
        grad_query,
        grad_pairs[:, :, 0].reshape(Dl, KV * HD),
        grad_pairs[:, :, 1].reshape(Dl, KV * HD),
        grad_projection,
        grad_up,
        grad_down,
    )


def solution(mesh):
    rows = P(None, "fsdp", "ctx", None)
    weight = P("fsdp", None)
    expert = P("ctx", "fsdp", None)
    placed = (rows, P(None, "fsdp"), rows, rows, P("fsdp"), P("fsdp"))
    placed = placed + (weight,) * 4 + (expert,) * 2 + (rows,)
    outs = (rows, rows, rows, P("fsdp"), P("fsdp")) + (weight,) * 4 + (expert,) * 2
    return jax.shard_map(local, mesh=mesh, in_specs=placed, out_specs=outs, check_vma=False)
```

time: 2750 us -> 1080 us (0.39)
  waiting for transfers between devices: 1920 us -> 515 us
  matrix products: 341 us -> 91.5 us
  Pallas kernels: 0 us -> 151 us
  blocking collectives: 118 us -> 0 us
  local copies, waits for them, and re-layouts: 203 us -> 85.1 us
  starting transfers between devices: 40.1 us -> 150 us
  other arithmetic: 104 us -> 64.6 us
    reduce_scatter x14 -> x2, waiting for transfers between devices: 1200 us -> 43.4 us  [the longest x1 43.3 us: local(): lax.psum_scatter(terms, 'ctx', scatter_dimension=0, tiled=False).astype(F32)]
    all_gather x8 -> x5, waiting for transfers between devices: 518 us -> 0.02 us  [the longest x1 0.01 us: local(): kv_all = lax.all_gather(kv_low, 'ctx', axis=1, tiled=True)]
    ppermute x0 -> x61, waiting for transfers between devices: none -> 328 us  [the longest x57 287 us: shift(): return lax.ppermute(block, 'fsdp', [(i, (i + k) % F) for i in range(F)])]
    dot_general x68 -> x25, matrix products: 341 us -> 91.5 us  [the longest x13 42 us: mm_tn(): lax.dot_general(a, b, (((0,), (0,)), ((), ())), preferred_element_type=F32)]
    pallas_call x0 -> x4, Pallas kernels: none -> 151 us  [the longest x2 103 us: run_expert(): pl.pallas_call(lambda *refs: expert_kernel(sides, merged, *refs), grid_sp...]
    ppermute x0 -> x61, starting transfers between devices: none -> 98 us  [the longest x57 89.2 us: shift(): return lax.ppermute(block, 'fsdp', [(i, (i + k) % F) for i in range(F)])]
    psum x1 -> x0, waiting for transfers between devices: 93 us -> none  [local(): lax.psum((totals[0], totals[1], totals[2], totals[3], totals[4], totals[5...]
    all_gather x4 -> x0, blocking collectives: 85.3 us -> none  [the longest x1 30.7 us: local(): lax.all_gather(value_weight, 'fsdp', axis=0, tiled=True)]
  transfers between devices with their start and end apart: 31 -> 78, of which waited for: 20 -> 36; matrix products, arithmetic and copies ran while one was open for 20% -> 19% of each run, Pallas kernels for 0% -> 14%
where the time goes in v1:
time: 1080 us; the launch traced here: 1070 us
  waiting for transfers between devices  515 us (48%)
  Pallas kernels  151 us (14%)
  starting transfers between devices  150 us (14%)
  matrix products  91.5 us (8%)
  local copies, waits for them, and re-layouts  85.1 us (8%)
  other arithmetic  64.6 us (6%)
  between operations  16 us (1%)
    ppermute x57, waiting for transfers between devices, shift(): return lax.ppermute(block, 'fsdp', [(i, (i + k) % F) for i in range(F)])  287 us
    all_to_all x10, waiting for transfers between devices, exchange(): return lax.all_to_all(blocks, 'ctx', 0, 0, tiled=True)  144 us
    pallas_call x2, Pallas kernels, run_expert(): pl.pallas_call(lambda *refs: expert_kernel(sides, merged, *refs), grid_sp...  103 us
    ppermute x57, starting transfers between devices, shift(): return lax.ppermute(block, 'fsdp', [(i, (i + k) % F) for i in range(F)])  89.2 us
    all_to_all x10, starting transfers between devices, exchange(): return lax.all_to_all(blocks, 'ctx', 0, 0, tiled=True)  50.7 us
    reduce_scatter x1, waiting for transfers between devices, local(): lax.psum_scatter(terms, 'ctx', scatter_dimension=0, tiled=False).astype(F32)  43.3 us
    dot_general x13, matrix products, mm_tn(): lax.dot_general(a, b, (((0,), (0,)), ((), ())), preferred_element_type=F32)  42 us
    ppermute x4, waiting for transfers between devices, swap(): return lax.ppermute(block, 'fsdp', [(i, i ^ 1) for i in range(F)])  41.1 us
  transfers between devices with their start and end apart: 78, of which 36 were waited for; matrix products, arithmetic and copies ran while one was open for 19% of the time, Pallas kernels for 14%

profile of v1, /device:TPU:0, one launch (start us, length us, event | category | flops | bytes accessed | tf_op | source)
XLA Modules:
  0.0 1072.5 jit_solution(11831688735515340724)
XLA Ops:
  8.4 5.1 collective-permute-start
  19.5 5.9 dynamic-slice_bitcast_fusion.1
  43.6 10.8 %collective-permute-done.6.refs_7_ = bf16[192,1536]{1,0:T(8,128)(2,1)} collective-permute-done((bf16[192,1536]{1,0:T(8,128)(2,1)}, bf16[192,1536]{1,0:T(8,128)(2,1)}, u32[]{:S(2)}, u32[]{:S(2)}) %collective-permute-start.6) | collective-permute-done | bytes 589856 | tf_op jit(solution)/shard_map/ppermute | solution.py:416
  54.4 9.5 collective-permute-done.7.refs_8_
  86.6 11.4 %collective-permute-done.14 = bf16[48,1536]{1,0:T(8,128)(2,1)S(1)} collective-permute-done((bf16[48,1536]{1,0:T(8,128)(2,1)S(1)}, bf16[48,1536]{1,0:T(8,128)(2,1)S(1)}, u32[]{:S(2)}, u32[]{:S(2)}) %collective-permute-start.14) | collective-permute-done | bytes 147488 | tf_op jit(solution)/shard_map/ppermute | solution.py:416
  101.0 9.1 collective-permute-done.9.refs_13_
  111.1 6.0 convolution_convert_fusion.3
  123.3 6.6 copy.97
  131.0 5.0 fusion.96
  137.7 46.4 %all-to-all-done.refs_3_ = bf16[8,2,80,1664]{3,2,1,0:T(8,128)(2,1)} async-done(((bf16[8,2,80,1664]{3,2,1,0:T(8,128)(2,1)}), bf16[8,2,80,1664]{3,2,1,0:T(8,128)(2,1)}, u32[]{:S(2)}, u32[]{:S(2)}) %all-to-all-start) | async-done | bytes 4259872 | tf_op jit(solution)/shard_map/all_to_all | solution.py:434
  189.8 20.6 %shard_map.212 = (bf16[4,128,1536]{2,1,0:T(8,128)(2,1)}, f32[4,2,128,128]{3,2,1,0:T(8,128)}) custom-call(s32[5]{0:T(128)} %pad_add_fusion.refs_0_, bf16[4,128,1536]{2,1,0:T(8,128)(2,1)} %copy.101.refs_1_, bf16[4,1024,512]{2,1,0:T(8,128)(2,1)} %all-gather.10.cloned.1.call-done.refs_2_), custom_call_target="tpu_custom_call" | custom-call | flops 22548578304 | bytes 10485760 | tf_op jit(solution)/shard_map/pallas_call | solution.py:121
  216.1 6.1 convolution_convert_fusion.2
  222.2 6.7 all-to-all-start.2
  232.3 5.2 multiply_reduce_fusion.2
  239.6 6.7 collective-permute-done.19.refs_14_
  246.2 12.3 %collective-permute-done.20.refs_15_ = bf16[192,1536]{1,0:T(8,128)(2,1)} collective-permute-done((bf16[192,1536]{1,0:T(8,128)(2,1)}, bf16[192,1536]{1,0:T(8,128)(2,1)}, u32[]{:S(2)}, u32[]{:S(2)}) %collective-permute-start.20) | collective-permute-done | bytes 589856 | tf_op jit(solution)/shard_map/ppermute | solution.py:416
  262.6 16.2 %all-to-all-done.2.refs_4_ = bf16[8,2,80,1664]{3,2,1,0:T(8,128)(2,1)} async-done(((bf16[8,2,80,1664]{3,2,1,0:T(8,128)(2,1)}), bf16[8,2,80,1664]{3,2,1,0:T(8,128)(2,1)}, u32[]{:S(2)}, u32[]{:S(2)}) %all-to-all-start.2) | async-done | bytes 4259872 | tf_op jit(solution)/shard_map/all_to_all | solution.py:434
  278.8 4.9 all-to-all-start.1
  287.9 43.9 %collective-permute-done.21.refs_12_ = bf16[192,1536]{1,0:T(8,128)(2,1)S(1)} collective-permute-done((bf16[192,1536]{1,0:T(8,128)(2,1)S(1)}, bf16[192,1536]{1,0:T(8,128)(2,1)S(1)}, u32[]{:S(2)}, u32[]{:S(2)}) %collective-permute-start.21) | collective-permute-done | bytes 589856 | tf_op jit(solution)/shard_map/ppermute | solution.py:416
  332.5 11.5 %collective-permute-done.22.refs_10_ = bf16[192,1536]{1,0:T(8,128)(2,1)} collective-permute-done((bf16[192,1536]{1,0:T(8,128)(2,1)}, bf16[192,1536]{1,0:T(8,128)(2,1)}, u32[]{:S(2)}, u32[]{:S(2)}) %collective-permute-start.22) | collective-permute-done | bytes 589856 | tf_op jit(solution)/shard_map/ppermute | solution.py:416
  345.9 5.5 convolution_convert_fusion.4
  361.6 12.7 %collective-permute-done.24.refs_7_ = bf16[192,1536]{1,0:T(8,128)(2,1)S(1)} collective-permute-done((bf16[192,1536]{1,0:T(8,128)(2,1)S(1)}, bf16[192,1536]{1,0:T(8,128)(2,1)S(1)}, u32[]{:S(2)}, u32[]{:S(2)}) %collective-permute-start.24) | collective-permute-done | bytes 589856 | tf_op jit(solution)/shard_map/ppermute | solution.py:416
  374.3 12.7 %collective-permute-done.25.refs_8_ = bf16[192,1536]{1,0:T(8,128)(2,1)} collective-permute-done((bf16[192,1536]{1,0:T(8,128)(2,1)S(1)}, bf16[192,1536]{1,0:T(8,128)(2,1)}, u32[]{:S(2)}, u32[]{:S(2)}) %collective-permute-start.25) | collective-permute-done | bytes 589856 | tf_op jit(solution)/shard_map/ppermute | solution.py:416
  387.0 12.0 %collective-permute-done.26.refs_9_ = bf16[192,1536]{1,0:T(8,128)(2,1)} collective-permute-done((bf16[192,1536]{1,0:T(8,128)(2,1)S(1)}, bf16[192,1536]{1,0:T(8,128)(2,1)}, u32[]{:S(2)}, u32[]{:S(2)}) %collective-permute-start.26) | collective-permute-done | bytes 589856 | tf_op jit(solution)/shard_map/ppermute | solution.py:416
  405.5 51.5 %shard_map.213 = (bf16[8,2,80,1536]{3,2,1,0:T(8,128)(2,1)}, bf16[8,2,80,1664]{3,2,1,0:T(8,128)(2,1)}, bf16[4,3,192,1536]{3,2,1,0:T(8,128)(2,1)}) custom-call(s32[3]{0:T(128)} %get-tuple-element.354.refs_0_, bf16[8,2,80,1536]{3,2,1,0:T(8,128)(2,1)} %all-to-all-done.1.refs_1_, bf16[8,2,80,1536]{3,2,1,0:T(8,128)(2,1)} %all-to-all-done.3.refs_2_, ...), custom_call_target="tpu_custom_call" | custom-call | flops 57378078720 | bytes 44040192 | tf_op jit(solution)/shard_map/pallas_call | solution.py:333
  472.5 7.6 collective-permute-done.29.refs_13_
  480.0 12.6 %collective-permute-done.30.refs_14_ = bf16[192,1536]{1,0:T(8,128)(2,1)S(1)} collective-permute-done((bf16[192,1536]{1,0:T(8,128)(2,1)S(1)}, bf16[192,1536]{1,0:T(8,128)(2,1)S(1)}, u32[]{:S(2)}, u32[]{:S(2)}) %collective-permute-start.30) | collective-permute-done | bytes 589856 | tf_op jit(solution)/shard_map/ppermute | solution.py:416
  493.5 11.2 %collective-permute-done.31.refs_15_ = bf16[192,1536]{1,0:T(8,128)(2,1)} collective-permute-done((bf16[192,1536]{1,0:T(8,128)(2,1)S(1)}, bf16[192,1536]{1,0:T(8,128)(2,1)}, u32[]{:S(2)}, u32[]{:S(2)}) %collective-permute-start.31) | collective-permute-done | bytes 589856 | tf_op jit(solution)/shard_map/ppermute | solution.py:416
  516.6 51.5 %shard_map.214 = (bf16[8,2,80,1536]{3,2,1,0:T(8,128)(2,1)}, bf16[8,2,80,1664]{3,2,1,0:T(8,128)(2,1)}, bf16[4,3,192,1536]{3,2,1,0:T(8,128)(2,1)}) custom-call(s32[3]{0:T(128)} %get-tuple-element.355.refs_0_, bf16[8,2,80,1536]{3,2,1,0:T(8,128)(2,1)} %all-to-all-done.1.refs_1_, bf16[8,2,80,1536]{3,2,1,0:T(8,128)(2,1)} %all-to-all-done.3.refs_2_, ...), custom_call_target="tpu_custom_call" | custom-call | flops 57378078720 | bytes 44040192 | tf_op jit(solution)/shard_map/pallas_call | solution.py:333
  578.7 4.9 slice_bitcast_fusion.16
  583.6 36.5 %all-to-all-done.6 = bf16[8,2,80,1536]{3,2,1,0:T(8,128)(2,1)} async-done(((bf16[8,2,80,1536]{3,2,1,0:T(8,128)(2,1)}), bf16[8,2,80,1536]{3,2,1,0:T(8,128)(2,1)}, u32[]{:S(2)}, u32[]{:S(2)}) %all-to-all-start.6) | async-done | bytes 3932192 | tf_op jit(solution)/shard_map/all_to_all | solution.py:434
  634.8 39.2 %collective-permute-done.37 = bf16[512,1536]{1,0:T(8,128)(2,1)} collective-permute-done((bf16[512,1536]{1,0:T(8,128)(2,1)}, bf16[512,1536]{1,0:T(8,128)(2,1)}, u32[]{:S(2)}, u32[]{:S(2)}) %collective-permute-start.37) | collective-permute-done | bytes 1572896 | tf_op jit(solution)/shard_map/ppermute | solution.py:431
  684.8 9.1 collective-permute-done.38
  697.9 26.9 %shard_map.215 = (f32[4,128,1536]{2,1,0:T(8,128)}, bf16[8,4,128,512]{3,2,1,0:T(8,128)(2,1)}) custom-call(s32[5]{0:T(128)} %pad_add_fusion.refs_0_, bf16[4,128,1536]{2,1,0:T(8,128)(2,1)} %copy.101.refs_1_, bf16[4,1024,512]{2,1,0:T(8,128)(2,1)} %all-gather.10.cloned.1.call-done.refs_2_, bf16[4,128,1536]{2,1,0:T(8,128)(2,1)} %bitcast.470, ...), custom_call_target="tpu_custom_call" | custom-call | flops 28991029248 | bytes 17825792 | tf_op jit(solution)/shard_map/pallas_call | solution.py:152
  725.6 6.6 all-to-all-start.7
  732.3 5.6 convolution_convert_fusion.1
  756.8 43.3 %reduce-scatter.3.cloned.1.call-done = bf16[1,4,128,512]{3,2,1,0:T(8,128)(2,1)} async-done(((bf16[8,4,128,512]{3,2,1,0:T(8,128)(2,1)}), bf16[1,4,128,512]{3,2,1,0:T(8,128)(2,1)}) %reduce-scatter.3.cloned.1.call-update) | async-done | bytes 524304 | tf_op jit(solution)/shard_map/reduce_scatter | solution.py:641
  801.8 4.8 all-to-all-start.8
  813.5 7.8 fusion.17
  837.5 36.6 %all-to-all-done.8 = bf16[8,4,48,1536]{3,2,1,0:T(8,128)(2,1)} async-done(((bf16[8,4,48,1536]{3,2,1,0:T(8,128)(2,1)}), bf16[8,4,48,1536]{3,2,1,0:T(8,128)(2,1)}, u32[]{:S(2)}, u32[]{:S(2)}) %all-to-all-start.8) | async-done | bytes 4718624 | tf_op jit(solution)/shard_map/all_to_all | solution.py:434
  889.6 5.2 fusion.26
  906.3 22.6 %collective-permute-done.48 = bf16[48,1536]{1,0:T(8,128)(2,1)S(1)} collective-permute-done((bf16[48,1536]{1,0:T(8,128)(2,1)S(1)}, bf16[48,1536]{1,0:T(8,128)(2,1)S(1)}, u32[]{:S(2)}, u32[]{:S(2)}) %collective-permute-start.48) | collective-permute-done | bytes 147488 | tf_op jit(solution)/shard_map/ppermute | solution.py:416
  945.3 30.6 %collective-permute-done.56 = bf16[48,768]{1,0:T(8,128)(2,1)S(1)} collective-permute-done((bf16[48,768]{1,0:T(8,128)(2,1)S(1)}, bf16[48,768]{1,0:T(8,128)(2,1)S(1)}, u32[]{:S(2)}, u32[]{:S(2)}) %collective-permute-start.56) | collective-permute-done | bytes 73760 | tf_op jit(solution)/shard_map/ppermute | solution.py:416
  980.6 4.8 collective-permute-done.54
  987.3 5.4 fusion.16
  1013.0 8.8 collective-permute-done.59
  1021.8 11.2 %collective-permute-done.60 = bf16[192,1536]{1,0:T(8,128)(2,1)S(1)} collective-permute-done((bf16[192,1536]{1,0:T(8,128)(2,1)S(1)}, bf16[192,1536]{1,0:T(8,128)(2,1)S(1)}, u32[]{:S(2)}, u32[]{:S(2)}) %collective-permute-start.60) | collective-permute-done | bytes 589856 | tf_op jit(solution)/shard_map/ppermute | solution.py:416
  1046.5 5.8 fusion
  (453 shorter events, 313.5 us)
Async XLA Ops:
  7.2 56.7 %all-gather.6.cloned.1.call-start = ((), (), s32[]{:S(2)}) async-start(), calls=%async_computation.12 | async-start | bytes 1769472 | tf_op jit(solution)/shard_map/all_gather | solution.py:437
  34.3 75.8 %all-gather.8.cloned.1.call-start = ((), (), s32[]{:S(2)}) async-start(), calls=%async_computation.13 | async-start | bytes 5308416 | tf_op jit(solution)/shard_map/all_gather | solution.py:437
  63.9 120.2 %all-gather.10.cloned.1.call-start = ((), (), s32[]{:S(2)}) async-start(), calls=%async_computation.14 | async-start | bytes 4718592 | tf_op jit(solution)/shard_map/all_gather | solution.py:539
  117.1 67.0 %all-to-all-start = ((bf16[8,2,80,1664]{3,2,1,0:T(8,128)(2,1)}), bf16[8,2,80,1664]{3,2,1,0:T(8,128)(2,1)}, u32[]{:S(2)}, u32[]{:S(2)}) async-start(bf16[8,2,80,1664]{3,2,1,0:T(8,128)(2,1)} %bitcast.430), calls=%async_computation | async-start | bytes 8519680 | tf_op jit(solution)/shard_map/all_to_all | solution.py:434
  121.7 110.6 %all-gather.12.cloned.1.call-start = ((), (), s32[]{:S(2)}) async-start(), calls=%async_computation.15 | async-start | bytes 5308416 | tf_op jit(solution)/shard_map/all_gather | solution.py:437
  121.9 62.2 %collective-permute-start.17 = (bf16[512,1664]{1,0:T(8,128)(2,1)}, bf16[512,1664]{1,0:T(8,128)(2,1)}, u32[]{:S(2)}, u32[]{:S(2)}) collective-permute-start(bf16[512,1664]{1,0:T(8,128)(2,1)} %concatenate.69), channel_id=1, source_target_pairs={{0,1},{1,0},{2,3},{3,2},{4,5},{5,4},{6,7},{7,6},{8,9},{9,8},{10,11... | collective-permute-start | bytes 5111816 | tf_op jit(solution)/shard_map/ppermute | solution.py:431
  129.9 54.2 %collective-permute-start.16 = (bf16[192,1536]{1,0:T(8,128)(2,1)}, bf16[192,1536]{1,0:T(8,128)(2,1)}, u32[]{:S(2)}, u32[]{:S(2)}) collective-permute-start(bf16[192,1536]{1,0:T(8,128)(2,1)} %get-tuple-element.151), channel_id=1, source_target_pairs={{0,2},{1,3},{2,0},{3,1},{4,6},{5,7},{6,4},{7,5},{8,10},{9,11},{10,... | collective-permute-start | bytes 1769480 | tf_op jit(solution)/shard_map/ppermute | solution.py:416
  222.2 56.6 %all-to-all-start.2 = ((bf16[8,2,80,1664]{3,2,1,0:T(8,128)(2,1)}), bf16[8,2,80,1664]{3,2,1,0:T(8,128)(2,1)}, u32[]{:S(2)}, u32[]{:S(2)}) async-start(bf16[8,2,80,1664]{3,2,1,0:T(8,128)(2,1)} %bitcast.429), calls=%async_computation.2 | async-start | bytes 8519680 | tf_op jit(solution)/shard_map/all_to_all | solution.py:434
  278.8 67.1 %all-to-all-start.1 = ((bf16[8,2,80,1536]{3,2,1,0:T(8,128)(2,1)}), bf16[8,2,80,1536]{3,2,1,0:T(8,128)(2,1)}, u32[]{:S(2)}, u32[]{:S(2)}) async-start(bf16[8,2,80,1536]{3,2,1,0:T(8,128)(2,1)} %bitcast.432), calls=%async_computation.1 | async-start | bytes 7864320 | tf_op jit(solution)/shard_map/all_to_all | solution.py:434
  283.7 62.2 %collective-permute-start.23 = (bf16[512,1536]{1,0:T(8,128)(2,1)S(1)}, bf16[512,1536]{1,0:T(8,128)(2,1)}, u32[]{:S(2)}, u32[]{:S(2)}) collective-permute-start(bf16[512,1536]{1,0:T(8,128)(2,1)S(1)} %multiply_convert_fusion.1), channel_id=1, source_target_pairs={{0,1},{1,0},{2,3},{3,2},{4,5},{5,4},{6,7},{7,6},{8,9},{9,8},{10,11... | collective-permute-start | bytes 4718600 | tf_op jit(solution)/shard_map/ppermute | solution.py:431
  284.4 47.4 %collective-permute-start.21 = (bf16[192,1536]{1,0:T(8,128)(2,1)S(1)}, bf16[192,1536]{1,0:T(8,128)(2,1)S(1)}, u32[]{:S(2)}, u32[]{:S(2)}) collective-permute-start(bf16[192,1536]{1,0:T(8,128)(2,1)S(1)} %copy-done.36), channel_id=1, source_target_pairs={{0,2},{1,3},{2,0},{3,1},{4,6},{5,7},{6,4},{7,5},{8,10},{9,11},{10,... | collective-permute-start | bytes 1769480 | tf_op jit(solution)/shard_map/ppermute | solution.py:416
  287.8 56.2 %collective-permute-start.22 = (bf16[192,1536]{1,0:T(8,128)(2,1)}, bf16[192,1536]{1,0:T(8,128)(2,1)}, u32[]{:S(2)}, u32[]{:S(2)}) collective-permute-start(bf16[192,1536]{1,0:T(8,128)(2,1)} %get-tuple-element.166), channel_id=1, source_target_pairs={{0,2},{1,3},{2,0},{3,1},{4,6},{5,7},{6,4},{7,5},{8,10},{9,11},{10,... | collective-permute-start | bytes 1769480 | tf_op jit(solution)/shard_map/ppermute | solution.py:416
  351.5 51.1 %all-to-all-start.3 = ((bf16[8,2,80,1536]{3,2,1,0:T(8,128)(2,1)}), bf16[8,2,80,1536]{3,2,1,0:T(8,128)(2,1)}, u32[]{:S(2)}, u32[]{:S(2)}) async-start(bf16[8,2,80,1536]{3,2,1,0:T(8,128)(2,1)} %bitcast.431), calls=%async_computation.3 | async-start | bytes 7864320 | tf_op jit(solution)/shard_map/all_to_all | solution.py:434
  358.7 40.4 %collective-permute-start.26 = (bf16[192,1536]{1,0:T(8,128)(2,1)S(1)}, bf16[192,1536]{1,0:T(8,128)(2,1)}, u32[]{:S(2)}, u32[]{:S(2)}) collective-permute-start(bf16[192,1536]{1,0:T(8,128)(2,1)S(1)} %copy-done.35), channel_id=1, source_target_pairs={{0,1},{1,2},{2,3},{3,0},{4,5},{5,6},{6,7},{7,4},{8,9},{9,10},{10,1... | collective-permute-start | bytes 1769480 | tf_op jit(solution)/shard_map/ppermute | solution.py:416
  402.6 54.5 %collective-permute-start.27 = (bf16[192,1536]{1,0:T(8,128)(2,1)S(1)}, bf16[192,1536]{1,0:T(8,128)(2,1)S(1)}, u32[]{:S(2)}, u32[]{:S(2)}) collective-permute-start(bf16[192,1536]{1,0:T(8,128)(2,1)S(1)} %copy-done.39), channel_id=1, source_target_pairs={{0,2},{1,3},{2,0},{3,1},{4,6},{5,7},{6,4},{7,5},{8,10},{9,11},{10,... | collective-permute-start | bytes 1769480 | tf_op jit(solution)/shard_map/ppermute | solution.py:416
  404.1 53.0 %collective-permute-start.28 = (bf16[192,1536]{1,0:T(8,128)(2,1)S(1)}, bf16[192,1536]{1,0:T(8,128)(2,1)S(1)}, u32[]{:S(2)}, u32[]{:S(2)}) collective-permute-start(bf16[192,1536]{1,0:T(8,128)(2,1)S(1)} %copy-done.34), channel_id=1, source_target_pairs={{0,2},{1,3},{2,0},{3,1},{4,6},{5,7},{6,4},{7,5},{8,10},{9,11},{10,... | collective-permute-start | bytes 1769480 | tf_op jit(solution)/shard_map/ppermute | solution.py:416
  458.1 51.0 %all-to-all-start.4 = ((bf16[8,2,80,1536]{3,2,1,0:T(8,128)(2,1)}), bf16[8,2,80,1536]{3,2,1,0:T(8,128)(2,1)}, u32[]{:S(2)}, u32[]{:S(2)}) async-start(bf16[8,2,80,1536]{3,2,1,0:T(8,128)(2,1)} %get-tuple-element.194), calls=%async_computation.4 | async-start | bytes 7864320 | tf_op jit(solution)/shard_map/all_to_all | solution.py:434
  466.4 38.3 %collective-permute-start.31 = (bf16[192,1536]{1,0:T(8,128)(2,1)S(1)}, bf16[192,1536]{1,0:T(8,128)(2,1)}, u32[]{:S(2)}, u32[]{:S(2)}) collective-permute-start(bf16[192,1536]{1,0:T(8,128)(2,1)S(1)} %copy-done.33), channel_id=1, source_target_pairs={{0,3},{1,0},{2,1},{3,2},{4,7},{5,4},{6,5},{7,6},{8,11},{9,8},{10,9... | collective-permute-start | bytes 1769480 | tf_op jit(solution)/shard_map/ppermute | solution.py:416
  509.1 59.0 %collective-permute-start.32 = (bf16[192,1536]{1,0:T(8,128)(2,1)}, bf16[192,1536]{1,0:T(8,128)(2,1)S(1)}, u32[]{:S(2)}, u32[]{:S(2)}) collective-permute-start(bf16[192,1536]{1,0:T(8,128)(2,1)} %get-tuple-element.197), channel_id=1, source_target_pairs={{0,2},{1,3},{2,0},{3,1},{4,6},{5,7},{6,4},{7,5},{8,10},{9,11},{10,... | collective-permute-start | bytes 1769480 | tf_op jit(solution)/shard_map/ppermute | solution.py:416
  510.6 57.6 %collective-permute-start.33 = (bf16[192,1536]{1,0:T(8,128)(2,1)S(1)}, bf16[192,1536]{1,0:T(8,128)(2,1)S(1)}, u32[]{:S(2)}, u32[]{:S(2)}) collective-permute-start(bf16[192,1536]{1,0:T(8,128)(2,1)S(1)} %get-tuple-element.198), channel_id=1, source_target_pairs={{0,2},{1,3},{2,0},{3,1},{4,6},{5,7},{6,4},{7,5},{8,10},{9,11},{10,... | collective-permute-start | bytes 1769480 | tf_op jit(solution)/shard_map/ppermute | solution.py:416
  512.0 56.1 %all-to-all-start.5 = ((bf16[8,2,80,1664]{3,2,1,0:T(8,128)(2,1)}), bf16[8,2,80,1664]{3,2,1,0:T(8,128)(2,1)}, u32[]{:S(2)}, u32[]{:S(2)}) async-start(bf16[8,2,80,1664]{3,2,1,0:T(8,128)(2,1)} %get-tuple-element.210), calls=%async_computation.5 | async-start | bytes 8519680 | tf_op jit(solution)/shard_map/all_to_all | solution.py:434
  569.2 50.9 %all-to-all-start.6 = ((bf16[8,2,80,1536]{3,2,1,0:T(8,128)(2,1)}), bf16[8,2,80,1536]{3,2,1,0:T(8,128)(2,1)}, u32[]{:S(2)}, u32[]{:S(2)}) async-start(bf16[8,2,80,1536]{3,2,1,0:T(8,128)(2,1)} %get-tuple-element.216), calls=%async_computation.6 | async-start | bytes 7864320 | tf_op jit(solution)/shard_map/all_to_all | solution.py:434
  573.7 226.4 %reduce-scatter.3.cloned.1.call-start = ((), (), s32[]{:S(2)}) async-start(), calls=%async_computation.16 | async-start | bytes 4718592 | tf_op jit(solution)/shard_map/reduce_scatter | solution.py:641
  574.2 53.0 %collective-permute-start.34 = (bf16[192,1536]{1,0:T(8,128)(2,1)S(1)}, bf16[192,1536]{1,0:T(8,128)(2,1)S(1)}, u32[]{:S(2)}, u32[]{:S(2)}) collective-permute-start(bf16[192,1536]{1,0:T(8,128)(2,1)S(1)} %get-tuple-element.213), channel_id=1, source_target_pairs={{0,2},{1,3},{2,0},{3,1},{4,6},{5,7},{6,4},{7,5},{8,10},{9,11},{10,... | collective-permute-start | bytes 1769480 | tf_op jit(solution)/shard_map/ppermute | solution.py:416
  575.7 51.5 %collective-permute-start.35 = (bf16[192,1536]{1,0:T(8,128)(2,1)S(1)}, bf16[192,1536]{1,0:T(8,128)(2,1)S(1)}, u32[]{:S(2)}, u32[]{:S(2)}) collective-permute-start(bf16[192,1536]{1,0:T(8,128)(2,1)S(1)} %get-tuple-element.214), channel_id=1, source_target_pairs={{0,1},{1,2},{2,3},{3,0},{4,5},{5,6},{6,7},{7,4},{8,9},{9,10},{10,1... | collective-permute-start | bytes 1769480 | tf_op jit(solution)/shard_map/ppermute | solution.py:416
  627.2 46.8 %collective-permute-start.37 = (bf16[512,1536]{1,0:T(8,128)(2,1)}, bf16[512,1536]{1,0:T(8,128)(2,1)}, u32[]{:S(2)}, u32[]{:S(2)}) collective-permute-start(bf16[512,1536]{1,0:T(8,128)(2,1)} %fusion.18), channel_id=1, source_target_pairs={{0,1},{1,0},{2,3},{3,2},{4,5},{5,4},{6,7},{7,6},{8,9},{9,8},{10,11... | collective-permute-start | bytes 4718600 | tf_op jit(solution)/shard_map/ppermute | solution.py:431
  630.0 47.6 %collective-permute-start.36 = (bf16[192,1536]{1,0:T(8,128)(2,1)}, bf16[192,1536]{1,0:T(8,128)(2,1)S(1)}, u32[]{:S(2)}, u32[]{:S(2)}) collective-permute-start(bf16[192,1536]{1,0:T(8,128)(2,1)} %get-tuple-element.218), channel_id=1, source_target_pairs={{0,2},{1,3},{2,0},{3,1},{4,6},{5,7},{6,4},{7,5},{8,10},{9,11},{10,... | collective-permute-start | bytes 1769480 | tf_op jit(solution)/shard_map/ppermute | solution.py:416
  693.9 30.9 %collective-permute-start.39 = (bf16[192,1536]{1,0:T(8,128)(2,1)S(1)}, bf16[192,1536]{1,0:T(8,128)(2,1)S(1)}, u32[]{:S(2)}, u32[]{:S(2)}) collective-permute-start(bf16[192,1536]{1,0:T(8,128)(2,1)S(1)} %copy-done.46), channel_id=1, source_target_pairs={{0,1},{1,2},{2,3},{3,0},{4,5},{5,6},{6,7},{7,4},{8,9},{9,10},{10,1... | collective-permute-start | bytes 1769480 | tf_op jit(solution)/shard_map/ppermute | solution.py:416
  725.6 76.2 %all-to-all-start.7 = ((bf16[8,2,80,1664]{3,2,1,0:T(8,128)(2,1)}), bf16[8,2,80,1664]{3,2,1,0:T(8,128)(2,1)}, u32[]{:S(2)}, u32[]{:S(2)}) async-start(bf16[8,2,80,1664]{3,2,1,0:T(8,128)(2,1)} %get-tuple-element.233), calls=%async_computation.8 | async-start | bytes 8519680 | tf_op jit(solution)/shard_map/all_to_all | solution.py:434
  732.2 204.5 %reduce-scatter.5.cloned.1.call-start = ((), (), s32[]{:S(2)}) async-start(), calls=%async_computation.17 | async-start | bytes 5308416 | tf_op jit(solution)/shard_map/reduce_scatter | solution.py:661
  746.4 55.4 %collective-permute-start.41 = (bf16[192,1536]{1,0:T(8,128)(2,1)}, bf16[192,1536]{1,0:T(8,128)(2,1)}, u32[]{:S(2)}, u32[]{:S(2)}) collective-permute-start(bf16[192,1536]{1,0:T(8,128)(2,1)} %get-tuple-element.228), channel_id=1, source_target_pairs={{0,3},{1,0},{2,1},{3,2},{4,7},{5,4},{6,5},{7,6},{8,11},{9,8},{10,9... | collective-permute-start | bytes 1769480 | tf_op jit(solution)/shard_map/ppermute | solution.py:416
  746.4 55.4 %collective-permute-start.42 = (bf16[192,1536]{1,0:T(8,128)(2,1)}, bf16[192,1536]{1,0:T(8,128)(2,1)}, u32[]{:S(2)}, u32[]{:S(2)}) collective-permute-start(bf16[192,1536]{1,0:T(8,128)(2,1)} %get-tuple-element.229), channel_id=1, source_target_pairs={{0,3},{1,0},{2,1},{3,2},{4,7},{5,4},{6,5},{7,6},{8,11},{9,8},{10,9... | collective-permute-start | bytes 1769480 | tf_op jit(solution)/shard_map/ppermute | solution.py:416
  746.5 55.3 %collective-permute-start.43 = (bf16[192,1536]{1,0:T(8,128)(2,1)}, bf16[192,1536]{1,0:T(8,128)(2,1)}, u32[]{:S(2)}, u32[]{:S(2)}) collective-permute-start(bf16[192,1536]{1,0:T(8,128)(2,1)} %get-tuple-element.230), channel_id=1, source_target_pairs={{0,2},{1,3},{2,0},{3,1},{4,6},{5,7},{6,4},{7,5},{8,10},{9,11},{10,... | collective-permute-start | bytes 1769480 | tf_op jit(solution)/shard_map/ppermute | solution.py:416
  801.8 72.2 %all-to-all-start.8 = ((bf16[8,4,48,1536]{3,2,1,0:T(8,128)(2,1)}), bf16[8,4,48,1536]{3,2,1,0:T(8,128)(2,1)}, u32[]{:S(2)}, u32[]{:S(2)}) async-start(bf16[8,4,48,1536]{3,2,1,0:T(8,128)(2,1)} %bitcast.409), calls=%async_computation.9 | async-start | bytes 9437184 | tf_op jit(solution)/shard_map/all_to_all | solution.py:434
  821.7 55.5 %collective-permute-start.44 = (bf16[192,1536]{1,0:T(8,128)(2,1)}, bf16[192,1536]{1,0:T(8,128)(2,1)}, u32[]{:S(2)}, u32[]{:S(2)}) collective-permute-start(bf16[192,1536]{1,0:T(8,128)(2,1)} %get-tuple-element.237), channel_id=1, source_target_pairs={{0,2},{1,3},{2,0},{3,1},{4,6},{5,7},{6,4},{7,5},{8,10},{9,11},{10,... | collective-permute-start | bytes 1769480 | tf_op jit(solution)/shard_map/ppermute | solution.py:416
  824.1 53.1 %collective-permute-start.45 = (bf16[192,1536]{1,0:T(8,128)(2,1)}, bf16[192,1536]{1,0:T(8,128)(2,1)}, u32[]{:S(2)}, u32[]{:S(2)}) collective-permute-start(bf16[192,1536]{1,0:T(8,128)(2,1)} %get-tuple-element.238), channel_id=1, source_target_pairs={{0,1},{1,2},{2,3},{3,0},{4,5},{5,6},{6,7},{7,4},{8,9},{9,10},{10,1... | collective-permute-start | bytes 1769480 | tf_op jit(solution)/shard_map/ppermute | solution.py:416
  825.5 51.6 %collective-permute-start.46 = (bf16[192,1536]{1,0:T(8,128)(2,1)}, bf16[192,1536]{1,0:T(8,128)(2,1)}, u32[]{:S(2)}, u32[]{:S(2)}) collective-permute-start(bf16[192,1536]{1,0:T(8,128)(2,1)} %get-tuple-element.239), channel_id=1, source_target_pairs={{0,1},{1,2},{2,3},{3,0},{4,5},{5,6},{6,7},{7,4},{8,9},{9,10},{10,1... | collective-permute-start | bytes 1769480 | tf_op jit(solution)/shard_map/ppermute | solution.py:416
  880.5 54.2 %all-to-all-start.9 = ((bf16[8,4,48,768]{3,2,1,0:T(8,128)(2,1)}), bf16[8,4,48,768]{3,2,1,0:T(8,128)(2,1)}, u32[]{:S(2)}, u32[]{:S(2)}) async-start(bf16[8,4,48,768]{3,2,1,0:T(8,128)(2,1)} %copy.118), calls=%async_computation.10 | async-start | bytes 4718592 | tf_op jit(solution)/shard_map/all_to_all | solution.py:434
  885.0 167.3 %all-gather.14.cloned.1.call-start = ((), (), s32[]{:S(2)}) async-start(), calls=%async_computation.18 | async-start | bytes 3317760 | tf_op jit(solution)/shard_map/all_gather | solution.py:688
  894.8 42.0 %collective-permute-start.51 = (bf16[192,1536]{1,0:T(8,128)(2,1)}, bf16[192,1536]{1,0:T(8,128)(2,1)}, u32[]{:S(2)}, u32[]{:S(2)}) collective-permute-start(bf16[192,1536]{1,0:T(8,128)(2,1)} %get-tuple-element.244), channel_id=1, source_target_pairs={{0,1},{1,2},{2,3},{3,0},{4,5},{5,6},{6,7},{7,4},{8,9},{9,10},{10,1... | collective-permute-start | bytes 1769480 | tf_op jit(solution)/shard_map/ppermute | solution.py:416
  896.3 40.5 %collective-permute-start.52 = (bf16[192,1536]{1,0:T(8,128)(2,1)}, bf16[192,1536]{1,0:T(8,128)(2,1)}, u32[]{:S(2)}, u32[]{:S(2)}) collective-permute-start(bf16[192,1536]{1,0:T(8,128)(2,1)} %get-tuple-element.245), channel_id=1, source_target_pairs={{0,3},{1,0},{2,1},{3,2},{4,7},{5,4},{6,5},{7,6},{8,11},{9,8},{10,9... | collective-permute-start | bytes 1769480 | tf_op jit(solution)/shard_map/ppermute | solution.py:416
  898.7 35.9 %collective-permute-start.49 = (bf16[48,1536]{1,0:T(8,128)(2,1)S(1)}, bf16[48,1536]{1,0:T(8,128)(2,1)S(1)}, u32[]{:S(2)}, u32[]{:S(2)}) collective-permute-start(bf16[48,1536]{1,0:T(8,128)(2,1)S(1)} %get-tuple-element.332), channel_id=1, source_target_pairs={{0,2},{1,3},{2,0},{3,1},{4,6},{5,7},{6,4},{7,5},{8,10},{9,11},{10,... | collective-permute-start | bytes 442376 | tf_op jit(solution)/shard_map/ppermute | solution.py:416
  900.8 33.8 %collective-permute-start.50 = (bf16[48,1536]{1,0:T(8,128)(2,1)S(1)}, bf16[48,1536]{1,0:T(8,128)(2,1)S(1)}, u32[]{:S(2)}, u32[]{:S(2)}) collective-permute-start(bf16[48,1536]{1,0:T(8,128)(2,1)S(1)} %get-tuple-element.331), channel_id=1, source_target_pairs={{0,3},{1,0},{2,1},{3,2},{4,7},{5,4},{6,5},{7,6},{8,11},{9,8},{10,9... | collective-permute-start | bytes 442376 | tf_op jit(solution)/shard_map/ppermute | solution.py:416
  928.9 68.2 %collective-permute-start.47 = (bf16[512,1664]{1,0:T(8,128)(2,1)}, bf16[512,1664]{1,0:T(8,128)(2,1)}, u32[]{:S(2)}, u32[]{:S(2)}) collective-permute-start(bf16[512,1664]{1,0:T(8,128)(2,1)} %fusion.3), channel_id=1, source_target_pairs={{0,1},{1,0},{2,3},{3,2},{4,5},{5,4},{6,7},{7,6},{8,9},{9,8},{10,11... | collective-permute-start | bytes 5111816 | tf_op jit(solution)/shard_map/ppermute | solution.py:431
  936.8 39.1 %collective-permute-start.56 = (bf16[48,768]{1,0:T(8,128)(2,1)S(1)}, bf16[48,768]{1,0:T(8,128)(2,1)S(1)}, u32[]{:S(2)}, u32[]{:S(2)}) collective-permute-start(bf16[48,768]{1,0:T(8,128)(2,1)S(1)} %get-tuple-element.337), channel_id=1, source_target_pairs={{0,1},{1,2},{2,3},{3,0},{4,5},{5,6},{6,7},{7,4},{8,9},{9,10},{10,1... | collective-permute-start | bytes 221192 | tf_op jit(solution)/shard_map/ppermute | solution.py:416
  940.5 38.2 %collective-permute-start.57 = (bf16[48,768]{1,0:T(8,128)(2,1)S(1)}, bf16[48,768]{1,0:T(8,128)(2,1)S(1)}, u32[]{:S(2)}, u32[]{:S(2)}) collective-permute-start(bf16[48,768]{1,0:T(8,128)(2,1)S(1)} %get-tuple-element.339), channel_id=1, source_target_pairs={{0,2},{1,3},{2,0},{3,1},{4,6},{5,7},{6,4},{7,5},{8,10},{9,11},{10,... | collective-permute-start | bytes 221192 | tf_op jit(solution)/shard_map/ppermute | solution.py:416
  942.1 38.5 %collective-permute-start.58 = (bf16[48,768]{1,0:T(8,128)(2,1)S(1)}, bf16[48,768]{1,0:T(8,128)(2,1)S(1)}, u32[]{:S(2)}, u32[]{:S(2)}) collective-permute-start(bf16[48,768]{1,0:T(8,128)(2,1)S(1)} %get-tuple-element.338), channel_id=1, source_target_pairs={{0,3},{1,0},{2,1},{3,2},{4,7},{5,4},{6,5},{7,6},{8,11},{9,8},{10,9... | collective-permute-start | bytes 221192 | tf_op jit(solution)/shard_map/ppermute | solution.py:416
  944.0 36.6 %collective-permute-start.53 = (bf16[48,1536]{1,0:T(8,128)(2,1)S(1)}, bf16[48,1536]{1,0:T(8,128)(2,1)S(1)}, u32[]{:S(2)}, u32[]{:S(2)}) collective-permute-start(bf16[48,1536]{1,0:T(8,128)(2,1)S(1)} %get-tuple-element.327), channel_id=1, source_target_pairs={{0,1},{1,2},{2,3},{3,0},{4,5},{5,6},{6,7},{7,4},{8,9},{9,10},{10,1... | collective-permute-start | bytes 442376 | tf_op jit(solution)/shard_map/ppermute | solution.py:416
  (109 other events, 1751.2 us)
Sparse Core Ops, SparseCore 0:
  34.4 24.8 all-gather.5
  64.1 38.2 all-gather.7
  110.3 64.3 all-gather.9
  184.3 41.2 all-gather.11
  725.0 75.0 reduce-scatter.2
  804.4 79.1 reduce-scatter.4
  987.4 32.9 all-gather.13

commit v2 on v1

v2 whole, which is shorter than its diff:
```python
import jax
import jax.numpy as jnp
from jax import lax
from jax.experimental import pallas as pl
from jax.experimental.pallas import tpu as pltpu
from jax.sharding import PartitionSpec as P

H = 12
KV = 2
HD = 128
TOP = 4
EXPERTS = 32
EPSILON = 1e-06
ROPE_BASE = 10000.0
NEGATIVE = -1e30
F32 = jnp.float32
BF16 = jnp.bfloat16


def angle_tables(positions):
    frequency = ROPE_BASE ** (-(jnp.arange(HD // 2, dtype=F32) * 2.0 / HD))
    angles = positions.astype(F32)[:, None] * frequency[None, :]
    cosine, sine = jnp.cos(angles), jnp.sin(angles)
    return jnp.concatenate([cosine, cosine], 1), jnp.concatenate([-sine, sine], 1)


def turn(vectors, cosine, sine):
    return vectors * cosine + pltpu.roll(vectors, HD // 2, 1) * sine


def norm_forward(values, gain_row):
    inverse = lax.rsqrt(jnp.mean(values * values, axis=-1, keepdims=True) + EPSILON)
    return values * inverse * gain_row, inverse


def norm_backward(values, inverse, gain_row, upstream):
    gain_grad = jnp.sum(upstream * values * inverse, axis=0)
    scaled = upstream * gain_row
    projected = jnp.mean(scaled * values, axis=-1, keepdims=True)
    return inverse * scaled - values * inverse**3 * projected, gain_grad


def mm(a, b):
    return jnp.dot(a, b, preferred_element_type=F32)


def mm_nt(a, b):
    return lax.dot_general(a, b, (((1,), (1,)), ((), ())), preferred_element_type=F32)


def mm_tn(a, b):
    return lax.dot_general(a, b, (((0,), (0,)), ((), ())), preferred_element_type=F32)


VMEM_LIMIT = 60 * 1024 * 1024


def stack_heads(block, groups):
    return jnp.concatenate([block[:, h * HD : (h + 1) * HD] for h in range(groups)], axis=0)


def masked_scores(stacked, keys, first, length, groups):
    tl = stacked.shape[0] // groups
    total = keys.shape[0]
    scores = mm_nt(stacked, keys) * HD ** (-0.5)
    key_at = lax.broadcasted_iota(jnp.int32, (tl, total), 1)
    query_at = lax.broadcasted_iota(jnp.int32, (tl, total), 0) + first
    allowed = (key_at <= query_at) & (key_at < length)
    scores = scores.reshape(groups, tl, total)
    return jnp.where(allowed[None], scores, NEGATIVE).reshape(groups * tl, total)


def key_value_kernel(x_ref, w_ref, cos_ref, sin_ref, out_ref):
    both = mm(x_ref[...], w_ref[...])
    cosine, sine = cos_ref[...], sin_ref[...]
    for h in range(KV):
        key = turn(both[:, 2 * h * HD : (2 * h + 1) * HD], cosine, sine)
        out_ref[0, :, 2 * h * HD : (2 * h + 1) * HD] = key.astype(BF16)
        value = both[:, (2 * h + 1) * HD : (2 * h + 2) * HD]
        out_ref[0, :, (2 * h + 1) * HD : (2 * h + 2) * HD] = value.astype(BF16)


def key_values(normed_low, qkv_full, tables, nseq):
    rows, D = normed_low.shape
    tl, wide = rows // nseq, 2 * KV * HD
    return pl.pallas_call(
        key_value_kernel,
        grid=(nseq,),
        in_specs=[
            pl.BlockSpec((tl, D), lambda s: (s, 0)),
            pl.BlockSpec((D, wide), lambda s: (0, H * HD // wide)),
            pl.BlockSpec((tl, HD), lambda s: (0, 0)),
            pl.BlockSpec((tl, HD), lambda s: (0, 0)),
        ],
        out_specs=pl.BlockSpec((1, tl, wide), lambda s: (s, 0, 0)),
        out_shape=jax.ShapeDtypeStruct((nseq, tl, wide), BF16),
        compiler_params=pltpu.CompilerParams(vmem_limit_bytes=VMEM_LIMIT),
        cost_estimate=pl.CostEstimate(
            flops=4 * rows * D * wide, bytes_accessed=2 * D * wide, transcendentals=0
        ),
    )(normed_low, qkv_full, *tables)


def attend_kernel(groups, info, q_ref, kv_ref, cos_ref, sin_ref, att_ref, lse_ref, turned_ref):
    tl = q_ref.shape[1]
    cosine, sine = cos_ref[...], sin_ref[...]
    for h in range(groups):
        at = slice(h * HD, (h + 1) * HD)
        turned_ref[0, :, at] = turn(q_ref[0, :, at], cosine, sine).astype(BF16)
    stacked = stack_heads(turned_ref[0], groups)
    scores = masked_scores(
        stacked, kv_ref[0, :, :HD], info[0], info[1 + pl.program_id(0)], groups
    )
    top = jnp.max(scores, axis=-1, keepdims=True)
    shares = jnp.exp(scores - top)
    total = jnp.sum(shares, axis=-1, keepdims=True)
    out = mm(shares.astype(BF16), kv_ref[0, :, HD:]) / total
    lse = top + jnp.log(total)
    for h in range(groups):
        at = slice(h * tl, (h + 1) * tl)
        att_ref[0, :, h * HD : (h + 1) * HD] = out[at].astype(BF16)
        lse_ref[0, 0, :, h : h + 1] = lse[at]


def attend_back_kernel(
    groups, info, q_ref, kv_ref, da_ref, lse_ref, cos_ref, sin_ref, dq_ref, dkv_ref
):
    tl = q_ref.shape[1]
    keys, values = kv_ref[0, :, :HD], kv_ref[0, :, HD:]
    stacked = stack_heads(q_ref[0], groups)
    scores = masked_scores(stacked, keys, info[0], info[1 + pl.program_id(0)], groups)
    lse = jnp.concatenate([lse_ref[0, 0, :, h : h + 1] for h in range(groups)], axis=0)
    probs = jnp.exp(scores - lse)
    grads = stack_heads(da_ref[0], groups)
    d_probs = mm_nt(grads, values)
    delta = jnp.sum(probs * d_probs, axis=-1, keepdims=True)
    d_scores = (probs * (d_probs - delta)).astype(BF16)
    dq = mm(d_scores, keys) * HD ** (-0.5)
    here = pl.ds(pl.multiple_of(info[0], 8), tl)
    cosine, sine = cos_ref[here, :], -sin_ref[here, :]
    for h in range(groups):
        turned = turn(dq[h * tl : (h + 1) * tl], cosine, sine)
        dq_ref[0, :, h * HD : (h + 1) * HD] = turned.astype(BF16)
    dk = mm_tn(d_scores, stacked) * HD ** (-0.5)
    dk = turn(dk, cos_ref[...], -sin_ref[...])
    dv = mm_tn(probs.astype(BF16), grads)
    shape = dkv_ref.shape[:1] + (tl, HD)
    dkv_ref[:, 0, :, :HD] = dk.reshape(shape).astype(BF16)
    dkv_ref[:, 0, :, HD:] = dv.reshape(shape).astype(BF16)


def attention(queries, kv_all, info, tables):
    nseq, tl, width = queries.shape
    total = kv_all.shape[1]
    groups = H // KV
    return pl.pallas_call(
        lambda *refs: attend_kernel(groups, *refs),
        grid_spec=pltpu.PrefetchScalarGridSpec(
            num_scalar_prefetch=1,
            grid=(nseq, KV),
            in_specs=[
                pl.BlockSpec((1, tl, groups * HD), lambda s, n, info: (s, 0, n)),
                pl.BlockSpec((1, total, 2 * HD), lambda s, n, info: (s, 0, n)),
                pl.BlockSpec((tl, HD), lambda s, n, info: (0, 0)),
                pl.BlockSpec((tl, HD), lambda s, n, info: (0, 0)),
            ],
            out_specs=[
                pl.BlockSpec((1, tl, groups * HD), lambda s, n, info: (s, 0, n)),
                pl.BlockSpec((1, 1, tl, HD), lambda s, n, info: (s, n, 0, 0)),
                pl.BlockSpec((1, tl, groups * HD), lambda s, n, info: (s, 0, n)),
            ],
        ),
        out_shape=[
            jax.ShapeDtypeStruct((nseq, tl, width), BF16),
            jax.ShapeDtypeStruct((nseq, KV, tl, HD), F32),
            jax.ShapeDtypeStruct((nseq, tl, width), BF16),
        ],
        compiler_params=pltpu.CompilerParams(vmem_limit_bytes=VMEM_LIMIT),
        cost_estimate=pl.CostEstimate(
            flops=28 * nseq * tl * width * total,
            bytes_accessed=4 * queries.size * 2 + 2 * kv_all.size,
            transcendentals=nseq * H * tl * total,
        ),
    )(info, queries, kv_all, *tables)


def attention_back(queries, kv_all, d_att, lse, info, tables, ctx_count):
    nseq, tl, width = queries.shape
    total = kv_all.shape[1]
    groups = H // KV
    return pl.pallas_call(
        lambda *refs: attend_back_kernel(groups, *refs),
        grid_spec=pltpu.PrefetchScalarGridSpec(
            num_scalar_prefetch=1,
            grid=(nseq, KV),
            in_specs=[
                pl.BlockSpec((1, tl, groups * HD), lambda s, n, info: (s, 0, n)),
                pl.BlockSpec((1, total, 2 * HD), lambda s, n, info: (s, 0, n)),
                pl.BlockSpec((1, tl, groups * HD), lambda s, n, info: (s, 0, n)),
                pl.BlockSpec((1, 1, tl, HD), lambda s, n, info: (s, n, 0, 0)),
                pl.BlockSpec((total, HD), lambda s, n, info: (0, 0)),
                pl.BlockSpec((total, HD), lambda s, n, info: (0, 0)),
            ],
            out_specs=[
                pl.BlockSpec((1, tl, groups * HD), lambda s, n, info: (s, 0, n)),
                pl.BlockSpec((ctx_count, 1, tl, 2 * HD), lambda s, n, info: (0, s, 0, n)),
            ],
        ),
        out_shape=[
            jax.ShapeDtypeStruct((nseq, tl, width), BF16),
            jax.ShapeDtypeStruct((ctx_count, nseq, tl, KV * 2 * HD), BF16),
        ],
        compiler_params=pltpu.CompilerParams(vmem_limit_bytes=VMEM_LIMIT),
        cost_estimate=pl.CostEstimate(
            flops=36 * nseq * tl * width * total,
            bytes_accessed=6 * queries.size * 2 + 4 * kv_all.size,
            transcendentals=nseq * H * tl * total,
        ),
    )(info, queries, kv_all, d_att, lse, *tables)


def expert_kernel(sides, w_mode, g_mode, *refs):
    info = refs[0]
    ins = refs[1 : 1 + sides]
    count = MODE_REFS[w_mode]
    weights = refs[1 + sides : 1 + sides + count]
    at = 1 + sides + count
    din_ref, wy_ref = refs[at : at + 2]
    at = at + 2
    out_refs = refs[at : at + GRAD_REFS[g_mode]]
    at = at + GRAD_REFS[g_mode]
    up, down, x_t, act_t, dgu, dy, act_s, pre, wide, gup, gdn, sems = refs[at:]
    step, steps = pl.program_id(0), pl.num_programs(0)
    D, W = up.shape[0], down.shape[0]
    tile = wide.shape[0]
    tw = 256 if W % 256 == 0 else 128
    td = 256

    wl = W // 4
    dl = 2 * wl

    def shard(up_side, down_side, source, block, first=0):
        pairs, count = [], block.shape[0]
        ups = min(count, dl - first)
        if ups > 0:
            at = pl.ds(pl.multiple_of(source * dl + first, 16), ups)
            pairs.append((up_side.at[at], block.at[pl.ds(0, ups)]))
        if ups < count:
            skip = max(0, ups)
            at = pl.ds(pl.multiple_of(source * wl + first + skip - dl, 16), count - skip)
            pairs.append((down_side.at[at], block.at[pl.ds(skip, count - skip)]))
        return pairs

    def by_distance(up_side, down_side, blocks, sign):
        pairs = []
        for block, k, first in zip(blocks, (1, 2, 2, 2, 3), (0, 0, wl, 2 * wl, 0)):
            source = lax.rem(info[0] + 4 + sign * k, 4)
            pairs += shard(up_side, down_side, source, block, first)
        return pairs

    def copies_of(pairs):
        return [pltpu.make_async_copy(a, b, sems.at[i]) for i, (a, b) in enumerate(pairs)]

    def loads():
        if w_mode == "whole":
            return copies_of([(weights[0].at[info[2]], up), (weights[1].at[info[2]], down)])
        pairs = by_distance(up, down, weights[2:], -1)
        own_up = up.at[pl.ds(pl.multiple_of(info[0] * dl, 16), dl)]
        own_down = down.at[pl.ds(pl.multiple_of(info[0] * wl, 16), wl)]
        pairs += [(own_up, weights[0].at[info[2]]), (own_down, weights[1].at[info[2]])]
        return copies_of([(b, a) for a, b in pairs])

    def put(ref, columns, block):
        per = tile // sides
        shape = (ref.shape[0], ref.shape[2], block.shape[1])
        for i in range(sides):
            ref[:, i, :, columns] = block[i * per : (i + 1) * per].reshape(shape)

    @pl.when(step == 0)
    def _():
        copies = loads()
        for copy in copies:
            copy.start()
        for copy in copies:
            copy.wait()

    rows = pl.ds(pl.multiple_of(step * tile, 128), tile)
    x = jnp.concatenate([r[:, :, :, :D].reshape(-1, D) for r in ins], axis=0)
    g_aug = jnp.concatenate([r[:, :, :, D:].reshape(-1, D + HD) for r in ins], axis=0)
    x_t[:, rows] = x.T
    lane = lax.broadcasted_iota(jnp.int32, (tile, HD), 1)
    picked = (lane == info[1]) | (lane == info[1] + HD // 2)
    w = jnp.sum(jnp.where(picked, g_aug[:, D:].astype(F32), 0.0), axis=1, keepdims=True)
    wide[...] = g_aug[:, :D]
    dy[rows, :] = (g_aug[:, :D].astype(F32) * w).astype(BF16)

    @pl.loop(0, W // tw)
    def _(t):
        a = pl.ds(pl.multiple_of(t * tw, 128), tw)
        b = pl.ds(pl.multiple_of(W + t * tw, 128), tw)
        gate = mm(x, up[:, a])
        lift = mm(x, up[:, b])
        pre[:, a] = gate
        pre[:, b] = lift
        act = gate / (1.0 + jnp.exp(-gate)) * lift
        act = act.astype(BF16)
        act_s[:, a] = act
        act_t[a, rows] = act.T

    def out_step(t, total):
        a = pl.ds(pl.multiple_of(t * td, 128), td)
        y = mm(act_s[...], down[:, a])
        put(wy_ref, a, (y * w).astype(BF16))
        return total + jnp.sum(y * wide[:, a].astype(F32), axis=1, keepdims=True)

    router = lax.fori_loop(0, D // td, out_step, jnp.zeros((tile, 1), F32))
    extra = jnp.where(lane == info[1], router, 0.0).astype(BF16)
    put(wy_ref, pl.ds(D, HD), extra)

    @pl.loop(0, W // tw)
    def _(t):
        a = pl.ds(pl.multiple_of(t * tw, 128), tw)
        b = pl.ds(pl.multiple_of(W + t * tw, 128), tw)
        d_act = mm_nt(dy[rows, :], down[a, :])
        gate, lift = pre[:, a], pre[:, b]
        sig = 1.0 / (1.0 + jnp.exp(-gate))
        dgu[rows, a] = (d_act * lift * sig * (1.0 + gate * (1.0 - sig))).astype(BF16)
        dgu[rows, b] = (d_act * gate * sig).astype(BF16)

    @pl.loop(0, D // td)
    def _(t):
        a = pl.ds(pl.multiple_of(t * td, 128), td)
        put(din_ref, a, mm_nt(dgu[rows, :], up[a, :]).astype(BF16))

    @pl.when(step == steps - 1)
    def _():
        @pl.loop(0, D // td)
        def _(t):
            a = pl.ds(pl.multiple_of(t * td, 128), td)
            gup[a, :] = mm(x_t[a, :], dgu[...]).astype(BF16)

        @pl.loop(0, W // tw)
        def _(t):
            a = pl.ds(pl.multiple_of(t * tw, 128), tw)
            gdn[a, :] = mm(act_t[a, :], dy[...]).astype(BF16)

        if g_mode == "whole":
            pairs = [(gup, out_refs[0]), (gdn, out_refs[1])]
        else:
            pairs = shard(gup, gdn, info[0], out_refs[0])
            pairs += by_distance(gup, gdn, out_refs[1:], 1)
        copies = copies_of(pairs)
        for copy in copies:
            copy.start()
        for copy in copies:
            copy.wait()


def weight_grad_kernel(
    planes, att_ref, db_ref, x_ref, dq_ref, all_ref, pair_ref, out_ref, total, grads, sems
):
    step = pl.program_id(0)
    D, width = x_ref.shape[1], dq_ref.shape[1]
    td = 256

    @pl.when(step == 0)
    def _():
        total[...] = jnp.zeros_like(total)

        @pl.loop(0, D // td)
        def _(t):
            a = pl.ds(pl.multiple_of(t * td, 128), td)
            grads[a, :D] = mm_tn(att_ref[:, a], db_ref[...]).astype(BF16)
            grads[a, D : D + width] = mm_tn(x_ref[:, a], dq_ref[...]).astype(BF16)

    total[...] += mm_tn(pair_ref[...], all_ref[...])

    @pl.when(step == pl.num_programs(0) - 1)
    def _():
        @pl.loop(0, D // td)
        def _(t):
            a = pl.ds(pl.multiple_of(t * td, 128), td)
            grads[a, D + width :] = total[:, a].T.astype(BF16)

        ctx = sems.shape[0] // planes
        cut = D // (planes * ctx)
        copies = []
        for f in range(planes):
            for c in range(ctx):
                source = grads.at[pl.ds((f * ctx + c) * cut, cut)]
                target = out_ref.at[pl.ds((c * planes + f) * cut, cut)]
                copies.append(pltpu.make_async_copy(source, target, sems.at[len(copies)]))
        for copy in copies:
            copy.start()
        for copy in copies:
            copy.wait()


def weight_grads(att, db, x, dq, every_x, pairs, ctx_count, planes):
    rows, D = x.shape
    width, wide = dq.shape[1], pairs.shape[1]
    return pl.pallas_call(
        lambda *refs: weight_grad_kernel(planes, *refs),
        grid=(ctx_count,),
        in_specs=[
            pl.BlockSpec((rows, D), lambda i: (0, 0)),
            pl.BlockSpec((rows, D), lambda i: (0, 0)),
            pl.BlockSpec((rows, D), lambda i: (0, 0)),
            pl.BlockSpec((rows, width), lambda i: (0, 0)),
            pl.BlockSpec((rows, D), lambda i: (i, 0)),
            pl.BlockSpec((rows, wide), lambda i: (i, 0)),
        ],
        out_specs=pl.BlockSpec(memory_space=pl.ANY),
        out_shape=jax.ShapeDtypeStruct((D, D + width + wide), BF16),
        scratch_shapes=[
            pltpu.VMEM((wide, D), F32),
            pltpu.VMEM((D, D + width + wide), BF16),
            pltpu.SemaphoreType.DMA((planes * ctx_count,)),
        ],
        compiler_params=pltpu.CompilerParams(vmem_limit_bytes=VMEM_LIMIT),
        cost_estimate=pl.CostEstimate(
            flops=4 * rows * D * (D + width + ctx_count * wide),
            bytes_accessed=2 * ctx_count * rows * D,
            transcendentals=0,
        ),
    )(att, db, x, dq, every_x, pairs)


def blank(shapes):
    return pl.pallas_call(
        lambda *refs: None,
        out_specs=[pl.BlockSpec(memory_space=pl.ANY)] * len(shapes),
        out_shape=[jax.ShapeDtypeStruct(shape, F32) for shape in shapes],
    )()


MODE_REFS = {"whole": 2, "parts": 7}
GRAD_REFS = {"whole": 2, "parts": 6}


def run_expert(piece, W, ins, weights, info, w_mode, g_mode):
    C, mine, slots, wide = ins[0].shape
    D = (wide - HD) // 2
    sides = len(ins)
    per_step = C
    while per_step > 1 and (per_step * sides * slots > 640 or C % per_step):
        per_step -= 1
    tile = per_step * sides * slots
    rows = C * sides * slots

    def spec(width, at):
        return pl.BlockSpec((per_step, 1, slots, width), lambda i, info: (i, at, 0, 0))

    def out_spec(width):
        return pl.BlockSpec((per_step, sides, slots, width), lambda i, info: (i, 0, 0, 0))

    any_spec = pl.BlockSpec(memory_space=pl.ANY)
    if g_mode == "whole":
        grads = [(D, 2 * W), (W, D)]
    else:
        grads = [(n * W // 4, D) for n in (3, 3, 1, 1, 1, 3)]
    grads = [jax.ShapeDtypeStruct(shape, BF16) for shape in grads]
    return pl.pallas_call(
        lambda *refs: expert_kernel(sides, w_mode, g_mode, *refs),
        grid_spec=pltpu.PrefetchScalarGridSpec(
            num_scalar_prefetch=1,
            grid=(C // per_step,),
            in_specs=[spec(wide, piece)] * sides
            + [any_spec] * len(weights),
            out_specs=[out_spec(D), out_spec(D + HD)] + [any_spec] * len(grads),
            scratch_shapes=[
                pltpu.VMEM((D, 2 * W), BF16),
                pltpu.VMEM((W, D), BF16),
                pltpu.VMEM((D, rows), BF16),
                pltpu.VMEM((W, rows), BF16),
                pltpu.VMEM((rows, 2 * W), BF16),
                pltpu.VMEM((rows, D), BF16),
                pltpu.VMEM((tile, W), BF16),
                pltpu.VMEM((tile, 2 * W), F32),
                pltpu.VMEM((tile, D), BF16),
                pltpu.VMEM((D, 2 * W), BF16),
                pltpu.VMEM((W, D), BF16),
                pltpu.SemaphoreType.DMA((12,)),
            ],
        ),
        out_shape=[jax.ShapeDtypeStruct((C, sides, slots, n), BF16) for n in (D, D + HD)]
        + grads,
        compiler_params=pltpu.CompilerParams(vmem_limit_bytes=VMEM_LIMIT),
        cost_estimate=pl.CostEstimate(
            flops=38 * rows * D * W,
            bytes_accessed=8 * rows * D + 24 * D * W,
            transcendentals=2 * rows * W,
        ),
    )(info, *ins, *weights)


def local(
    tokens,
    lengths,
    expert_picks,
    router_weights,
    first_gain,
    second_gain,
    query_weight,
    key_weight,
    value_weight,
    output_weight,
    up_weight,
    down_weight,
    cotangent,
):
    batches, seqs_here, tl, D = tokens.shape
    C = lax.axis_size("ctx")
    F = lax.axis_size("fsdp")
    c = lax.axis_index("ctx")
    f = lax.axis_index("fsdp")
    split = max(1, C // EXPERTS)
    pieces = up_weight.shape[0]
    W = up_weight.shape[2] // 2
    merged = pieces % 2 == 0 and F == 4 and 2 * W == D
    share = 2 if merged else 1
    mine = pieces // share
    role = f % share
    nseq = batches * seqs_here
    cap = max(2, (5 * tl * TOP + 4 * EXPERTS - 1) // (4 * EXPERTS))
    while nseq * cap % 16:
        cap += 1
    slots = nseq * cap
    rows = nseq * tl
    L = C * tl
    width = H * HD
    Dl = query_weight.shape[0]
    cut = Dl // C

    positions = c * tl + jnp.arange(tl, dtype=jnp.int32)
    tables = angle_tables(positions)
    all_tables = angle_tables(jnp.arange(L, dtype=jnp.int32))
    lens = lengths.reshape(nseq)
    live = (positions[None, :] < lens[:, None]).reshape(rows)
    live_rows = live.astype(F32)[:, None]

    def gate(*values):
        return lax.optimization_barrier(values)

    def shift(block, k):
        return lax.ppermute(block, "fsdp", [(i, (i + k) % F) for i in range(F)])

    def fsdp_gather(block):
        got = [shift(block, k) for k in range(F - 1, 0, -1)]
        ring = jnp.stack(got + [block] + got)
        return lax.dynamic_slice_in_dim(ring, F - 1 - f, F, 0)

    def fsdp_scatter_sum(parts):
        total = lax.dynamic_index_in_dim(parts, f, 0, keepdims=False).astype(F32)
        for k in range(1, F):
            block = lax.dynamic_index_in_dim(parts, (f + k) % F, 0, keepdims=False)
            total = total + shift(block, k).astype(F32)
        return total

    def swap(block):
        return lax.ppermute(block, "fsdp", [(i, i ^ 1) for i in range(F)])

    def exchange(blocks):
        return lax.all_to_all(blocks, "ctx", 0, 0, tiled=True)

    def ctx_gather(lines):
        return lax.all_gather(lines, "ctx", axis=1, tiled=True).reshape(D, -1)

    def part_of(weight):
        return lax.dynamic_slice_in_dim(weight, c * cut, cut, 0)

    key_part, value_part = part_of(key_weight), part_of(value_weight)
    qkv_part = [part_of(query_weight)]
    for h in range(KV):
        qkv_part += [part[:, h * HD : (h + 1) * HD] for part in (key_part, value_part)]
    qkv_part = jnp.concatenate(qkv_part, axis=1)
    out_part, gain_parts = part_of(output_weight), jnp.stack([first_gain, second_gain])
    qkv_lines = fsdp_gather(qkv_part)

    messages, operands = {}, {}
    expert_in = [up_weight, down_weight]

    def shard_of(at):
        return jnp.concatenate(
            [lax.dynamic_index_in_dim(x, at, 0, keepdims=False) for x in expert_in]
        )

    def operand(name):
        if name in operands:
            return operands[name]
        j = "wv".index(name[0])
        block = shard_of((role if name[1] == "2" else 1 - role) * mine + j)
        third = block.shape[0] // 3
        at = "abc".find(name[2:]) * third if name[2:] else 0
        return block[at : at + third] if name[2:] else block

    def send(name, block):
        return shift(block, int(name[1]))

    def step(need, values, go):
        if not merged:
            return lax.optimization_barrier(values)
        fresh = tuple(operand(name) for name in go)
        got, values, fresh = lax.optimization_barrier(
            (tuple(messages[name] for name in need), values, fresh)
        )
        messages.update(zip(need, got))
        messages.update((name, send(name, block)) for name, block in zip(go, fresh))
        return values

    picks = expert_picks.reshape(rows, TOP)
    gates = router_weights.reshape(rows, TOP)
    cot = cotangent.reshape(rows, D)
    expert_ids = jnp.arange(EXPERTS, dtype=jnp.int32)
    hit = picks[:, :, None] == expert_ids
    by_expert = jnp.sum(jnp.where(hit, gates[:, :, None], 0.0), axis=1) * live_rows
    high = by_expert.astype(BF16)
    low = (by_expert - high.astype(F32)).astype(BF16)
    gap = jnp.zeros((rows, HD // 2 - EXPERTS), BF16)
    table = jnp.concatenate([high, gap, low, gap], axis=1)
    number = jnp.arange(C)[:, None] * pieces + role * mine + jnp.arange(mine)[None, :]
    expert_of = (number // split).reshape(C * mine)
    earlier = jnp.tril(jnp.ones((tl, tl), BF16), -1)
    pick_map = (expert_ids[:, None] == expert_of[None, :]).astype(BF16)

    def route(table):
        match = table[:, :EXPERTS] > 0
        ranks = jnp.einsum(
            "ab,sbe->sae",
            earlier,
            match.astype(BF16).reshape(nseq, tl, -1),
            preferred_element_type=F32,
        )
        base = (jnp.arange(nseq) * cap)[:, None, None]
        code = jnp.where(match, (ranks + base).reshape(rows, -1), -1.0).astype(BF16)
        code = mm_tn(pick_map, code.T)
        chosen = code[:, None, :] == jnp.arange(slots, dtype=F32)[None, :, None]
        return chosen.astype(BF16).reshape(C, mine, slots, rows)

    def to_slots(sel, source):
        out = mm(sel.reshape(C * mine * slots, rows), source)
        return out.astype(BF16).reshape(C, mine, slots, -1)

    inputs = tokens.reshape(rows, D).astype(F32)
    step([], (qkv_part,), ["w1"])
    _, gain_parts, table, cot, out_part = gate(qkv_lines, gain_parts, table, cot, out_part)
    gains, out_lines = fsdp_gather(gain_parts), fsdp_gather(out_part)
    sels = [route(table)]
    qkv_full, sels[0], table, out_lines, cot_wide, all_tables = step(
        ["w1"],
        (
            ctx_gather(qkv_lines),
            sels[0],
            table,
            out_lines,
            jnp.concatenate([cot, table], axis=1),
            all_tables,
        ),
        ["w3"],
    )
    first_scale = gains[:, 0].reshape(D).astype(F32)
    second_scale = gains[:, 1].reshape(D).astype(F32)
    normed, inverse_one = norm_forward(inputs, first_scale)
    normed_low = normed.astype(BF16)
    kv_low = key_values(normed_low, qkv_full, tables, nseq)
    kv_all = lax.all_gather(kv_low, "ctx", axis=1, tiled=True)
    _, expert_in, qkv_full, table = gate(kv_low, expert_in, qkv_full, table)
    query_pre = mm(normed_low, qkv_full[:, :width]).reshape(nseq, tl, width)
    info = jnp.concatenate([(c * tl)[None], lens])
    kv_all, query_pre, out_lines, table = step(
        ["w3"], (kv_all, query_pre, out_lines, table), ["w2a"]
    )
    far_table = swap(table) if share == 2 else table
    out_full = ctx_gather(out_lines)
    attended, lse, queries = attention(query_pre, kv_all, info, tables)
    attended, cot_wide, far_table = step(["w2a"], (attended, cot_wide, far_table), [])
    attended_low = attended.reshape(rows, width)
    hidden = inputs + live_rows * mm(attended_low, out_full)
    second, inverse_two = norm_forward(hidden, second_scale)
    second_low = second.astype(BF16)

    second_low, cot_wide = step([], (second_low, cot_wide), ["w2b", "w2c"])
    expert_rows = [exchange(to_slots(sels[0], jnp.concatenate([second_low, cot_wide], axis=1)))]
    shards = None
    if merged:
        far, far_cot = swap(second_low), swap(cot_wide[:, :D])
        sels.append(route(far_table))
        shards = list(blank([(pieces, Dl, 2 * W), (pieces, W // F, D)]))
        far, far_cot, expert_rows[0], sels[1], shards = step(
            ["w2b", "w2c"], (far, far_cot, expert_rows[0], sels[1], shards), ["v1", "v3", "v2a"]
        )
        far_rows = jnp.concatenate([far, far_cot, far_table], axis=1)
        expert_rows.append(exchange(to_slots(sels[1], far_rows)))

    def expert(j):
        at = role * mine + j
        expert_info = jnp.stack([f, (c * pieces + at) // split, at])
        if not merged:
            return run_expert(j, W, expert_rows, [up_full, down_full], expert_info, "whole", "whole")
        names = ["wv"[j] + k for k in ("1", "2a", "2b", "2c", "3")]
        weights = [up_weight, down_weight] + [messages[name] for name in names]
        out = run_expert(j, W, expert_rows, weights, expert_info, "parts", "parts")
        for k, grad in zip(("0", "1", "2a", "2b", "2c", "3"), out[2:]):
            operands["pq"[j] + k] = grad
        return out

    if merged:
        expert_rows[1], normed_mine = step(
            ["v1", "v3", "v2a"], (expert_rows[1], normed_low), ["v2b", "v2c"]
        )
        every_normed = lax.all_gather(normed_mine, "ctx", axis=0, tiled=True)
        outs = [expert(0)]
        d_in, mixed = [outs[0][0]], [outs[0][1]]
        d_in[0], expert_rows[0], mixed[0] = step(
            ["v2b", "v2c"], (d_in[0], expert_rows[0], mixed[0]), ["p1", "p2a"]
        )
        d_in[0] = exchange(d_in[0])
        outs.append(expert(1))
        last, d_in[0], later, every_normed = step(
            ["p1", "p2a"], (outs[1][0], d_in[0], outs[1][1], every_normed), ["p3"]
        )
        d_in.append(exchange(last))
        mixed.append(later)
    else:
        up_full = lax.all_gather(up_weight, "fsdp", axis=1, tiled=True)
        down_full = lax.all_gather(down_weight, "fsdp", axis=1, tiled=True)
        outs = [expert(j) for j in range(mine)]
        d_in = [exchange(out[0]) for out in outs]
        mixed = [exchange(out[1]) for out in outs]

    def collect(backs):
        sums = []
        for i, sel in enumerate(sels):
            total = 0.0
            for j, back in enumerate(backs):
                total = total + mm_tn(
                    sel[:, j].reshape(C * slots, rows), back[:, i].reshape(C * slots, -1)
                )
            sums.append(total)
        return sums

    def fill(at, total):
        for i, block in enumerate((total[:Dl], total[Dl:])):
            shards[i] = lax.dynamic_update_slice(shards[i], block[None], (at, 0, 0))

    def pair_sum(first, *others):
        far = jnp.concatenate([messages[name] for name in others])
        return first.astype(F32) + far.astype(F32)

    sums = collect(d_in)
    dispatch_grad = sums[0]
    if share == 2:
        far, mixed[0] = step(["p3"], (sums[1].astype(BF16), mixed[0]), ["p2b"])
        dispatch_grad = dispatch_grad + swap(far).astype(F32)
        mixed[0] = exchange(mixed[0])
        dispatch_grad, mixed[0], mixed[1] = step(["p2b"], (dispatch_grad, mixed[0], mixed[1]), [])
        mixed[1] = exchange(mixed[1])

    upstream = cot.astype(F32)
    norm_grad, second_grads = norm_backward(hidden, inverse_two, second_scale, dispatch_grad)
    hidden_grad = upstream + norm_grad
    branch_grad = (live_rows * hidden_grad).astype(BF16)
    def by_target(grad):
        return grad.astype(BF16).reshape(F, C, cut, -1).transpose(1, 0, 2, 3)

    def over_ctx(blocks):
        return jnp.sum(exchange(blocks).astype(F32), axis=0).astype(BF16)

    def scatter(blocks):
        (blocks,) = gate(blocks.reshape(D, -1))
        total = lax.psum_scatter(blocks, "ctx", scatter_dimension=0, tiled=True)
        return gate(total)[0].reshape(F, cut, -1)

    d_att = mm_nt(branch_grad, out_full).astype(BF16)
    (d_att,) = step([], (d_att,), ["p2c"])
    query_back, terms = attention_back(
        queries, kv_all, d_att.reshape(nseq, tl, width), lse, info, all_tables, C
    )
    query_back = query_back.reshape(rows, width)
    terms, query_back, mixed[-1] = step(["p2c"], (terms, query_back, mixed[-1]), ["q2a"])
    if merged:
        own_terms = over_ctx(terms)
        flat_terms = terms.reshape(C * rows, -1)
        blocks = weight_grads(
            attended_low, branch_grad, normed_low, query_back, every_normed, flat_terms, C, F
        )
        blocks, mixed = step(["q2a"], (blocks, mixed), ["q2b", "q2c"])
        mixed_sums = collect(mixed)
        mixed_rows = mixed_sums[0] + swap(mixed_sums[1].astype(BF16)).astype(F32)
        fill(role * mine, pair_sum(operands["p0"], "p2a", "p2b", "p2c"))
        fill((1 - role) * mine, pair_sum(messages["p1"], "p3"))
        own_terms, shards, mixed_rows = step(
            ["q2b", "q2c"], (own_terms, shards, mixed_rows), ["q1"]
        )
        fill(role * mine + 1, pair_sum(operands["q0"], "q2a", "q2b", "q2c"))
    else:
        own_terms = over_ctx(terms)
        pair_grad = mm_tn(normed_low, own_terms.reshape(rows, 2 * KV * HD))
        query_grad = mm_tn(normed_low, query_back)
        projection_grad = mm_tn(attended_low, branch_grad)
        blocks = by_target(jnp.concatenate([projection_grad, query_grad, pair_grad], axis=1))
        mixed_rows = collect(mixed)[0]
    weight_rows = scatter(blocks)
    kv_back = own_terms.reshape(rows, 2 * KV * HD)
    normed_grad = mm_nt(query_back, qkv_full[:, :width]) + mm_nt(kv_back, qkv_full[:, width:])
    entry_grad, first_grads = norm_backward(inputs, inverse_one, first_scale, normed_grad)
    grad_tokens = hidden_grad + entry_grad
    gain_columns = jnp.stack([first_grads, second_grads]).reshape(2, F, Dl).transpose(1, 0, 2)
    gain_columns = gain_columns.reshape(F, cut, -1)
    gain_count = gain_columns.shape[2]
    gain_columns = jnp.pad(gain_columns, ((0, 0), (0, 0), (0, -gain_count % HD)))
    weight_rows, gain_columns, shards = step(["q1"], (weight_rows, gain_columns, shards), [])
    wide = jnp.concatenate([weight_rows, gain_columns.astype(BF16)], axis=2)
    wide = fsdp_scatter_sum(wide).astype(BF16)
    wide, shards = step([], (wide, shards), ["q3"])
    wide = lax.all_gather(wide, "ctx", axis=0, tiled=False)
    whole = wide[:, :, : D + width + 2 * KV * HD].reshape(Dl, -1).astype(F32)
    grad_projection, grad_query = whole[:, :D], whole[:, D : D + width]
    grad_pairs = whole[:, D + width :].reshape(Dl, KV, 2, HD)
    gain_at = D + width + 2 * KV * HD
    gain_sums = jnp.sum(wide[:, :, gain_at : gain_at + gain_count].astype(F32), axis=0)
    grad_first, grad_second = gain_sums.reshape(2, Dl)

    block_rows = (hidden + mixed_rows[:, :D]).astype(BF16)
    router_by_expert = mixed_rows[:, D : D + EXPERTS]
    grad_router = jnp.sum(jnp.where(hit, router_by_expert[:, None, :], 0.0), axis=2)

    if merged:
        fill((1 - role) * mine + 1, pair_sum(messages["q1"], "q3"))
        grad_up, grad_down = shards
    else:
        grad_up, grad_down = [
            lax.psum_scatter(
                jnp.stack([out[2 + i] for out in outs]), "fsdp", scatter_dimension=1, tiled=True
            ).astype(F32)
            for i in range(2)
        ]

    shape = (batches, seqs_here, tl)
    return (
        block_rows.reshape(shape + (D,)),
        grad_tokens.reshape(shape + (D,)),
        grad_router.reshape(shape + (TOP,)),
        grad_first,
        grad_second,
        grad_query,
        grad_pairs[:, :, 0].reshape(Dl, KV * HD),
        grad_pairs[:, :, 1].reshape(Dl, KV * HD),
        grad_projection,
        grad_up,
        grad_down,
    )


def solution(mesh):
    rows = P(None, "fsdp", "ctx", None)
    weight = P("fsdp", None)
    expert = P("ctx", "fsdp", None)
    placed = (rows, P(None, "fsdp"), rows, rows, P("fsdp"), P("fsdp"))
    placed = placed + (weight,) * 4 + (expert,) * 2 + (rows,)
    outs = (rows, rows, rows, P("fsdp"), P("fsdp")) + (weight,) * 4 + (expert,) * 2
    return jax.shard_map(local, mesh=mesh, in_specs=placed, out_specs=outs, check_vma=False)
```

time: 1080 us -> 1000 us (0.926)
  starting transfers between devices: 150 us -> 85.7 us
  local copies, waits for them, and re-layouts: 85.1 us -> 48.5 us
  Pallas kernels: 151 us -> 182 us
  matrix products: 91.5 us -> 74.1 us
  waiting for transfers between devices: 515 us -> 531 us
    all_to_all x10 -> x7, waiting for transfers between devices: 144 us -> 55.6 us  [exchange(): return lax.all_to_all(blocks, 'ctx', 0, 0, tiled=True)]
    ppermute x57 -> x32, waiting for transfers between devices: 287 us -> 366 us  [shift(): return lax.ppermute(block, 'fsdp', [(i, (i + k) % F) for i in range(F)])]
    ppermute x4 -> x5, waiting for transfers between devices: 41.1 us -> 102 us  [swap(): return lax.ppermute(block, 'fsdp', [(i, i ^ 1) for i in range(F)])]
    reduce_scatter x2 -> x1, waiting for transfers between devices: 43.4 us -> 0.19 us  [scatter(): total = lax.psum_scatter(blocks, 'ctx', scatter_dimension=0, tiled=True)]
    ppermute x57 -> x32, starting transfers between devices: 89.2 us -> 47.2 us  [shift(): return lax.ppermute(block, 'fsdp', [(i, (i + k) % F) for i in range(F)])]
    pallas_call x2 -> x5, Pallas kernels: 103 us -> 134 us  [the longest x2 104 us: run_expert(): pl.pallas_call(lambda *refs: expert_kernel(sides, w_mode, g_mode, *refs),...]
    all_to_all x10 -> x7, starting transfers between devices: 50.7 us -> 33.2 us  [exchange(): return lax.all_to_all(blocks, 'ctx', 0, 0, tiled=True)]
    squeeze x9 -> x4, local copies, waits for them, and re-layouts: 20.4 us -> 4.95 us  [shard_of(): lax.dynamic_index_in_dim(x, at, 0, keepdims=False)]
  transfers between devices with their start and end apart: 78 -> 50, of which waited for: 36 -> 23; matrix products, arithmetic and copies ran while one was open for 19% -> 12% of each run, Pallas kernels for 14% -> 18%
where the time goes in v2:
time: 1000 us; the launch traced here: 993 us
  waiting for transfers between devices  531 us (53%)
  Pallas kernels  182 us (18%)
  starting transfers between devices  85.7 us (9%)
  matrix products  74.1 us (7%)
  other arithmetic  55.9 us (6%)
  local copies, waits for them, and re-layouts  48.5 us (5%)
  between operations  15.7 us (2%)
    ppermute x32, waiting for transfers between devices, shift(): return lax.ppermute(block, 'fsdp', [(i, (i + k) % F) for i in range(F)])  366 us
    pallas_call x2, Pallas kernels, run_expert(): pl.pallas_call(lambda *refs: expert_kernel(sides, w_mode, g_mode, *refs),...  104 us
    ppermute x5, waiting for transfers between devices, swap(): return lax.ppermute(block, 'fsdp', [(i, i ^ 1) for i in range(F)])  102 us
    all_to_all x7, waiting for transfers between devices, exchange(): return lax.all_to_all(blocks, 'ctx', 0, 0, tiled=True)  55.6 us
    ppermute x32, starting transfers between devices, shift(): return lax.ppermute(block, 'fsdp', [(i, (i + k) % F) for i in range(F)])  47.2 us
    all_to_all x7, starting transfers between devices, exchange(): return lax.all_to_all(blocks, 'ctx', 0, 0, tiled=True)  33.2 us
    dot_general x10, matrix products, mm_tn(): lax.dot_general(a, b, (((0,), (0,)), ((), ())), preferred_element_type=F32)  30.8 us
    pallas_call x1, Pallas kernels, attention_back(): pl.pallas_call(lambda *refs: attend_back_kernel(groups, *refs), grid_spec...  27.6 us
  transfers between devices with their start and end apart: 50, of which 23 were waited for; matrix products, arithmetic and copies ran while one was open for 12% of the time, Pallas kernels for 18%

profile of v2, /device:TPU:0, one launch (start us, length us, event | category | flops | bytes accessed | tf_op | source)
XLA Modules:
  0.0 993.3 jit_solution(16626825713563080956)
XLA Ops:
  11.1 5.0 collective-permute-start.1
  17.2 4.3 collective-permute-done.1
  21.5 11.3 %collective-permute-done.2 = bf16[48,2048]{1,0:T(8,128)(2,1)S(1)} collective-permute-done((bf16[48,2048]{1,0:T(8,128)(2,1)S(1)}, bf16[48,2048]{1,0:T(8,128)(2,1)S(1)}, u32[]{:S(2)}, u32[]{:S(2)}) %collective-permute-start.2) | collective-permute-done | bytes 196640 | tf_op jit(solution)/shard_map/ppermute | solution.py:546
  49.2 3.8 collective-permute-start.4
  57.8 20.1 %collective-permute-done.8 = bf16[2,384]{1,0:T(2,128)(2,1)S(1)} collective-permute-done((bf16[2,384]{1,0:T(2,128)(2,1)S(1)}, bf16[2,384]{1,0:T(2,128)(2,1)S(1)}, u32[]{:S(2)}, u32[]{:S(2)}) %collective-permute-start.8) | collective-permute-done | bytes 1568 | tf_op jit(solution)/shard_map/ppermute | solution.py:546
  78.0 4.1 collective-permute-start.5
  86.5 5.9 collective-permute-done.5
  93.4 4.8 shard_map.212
  103.4 4.3 fusion.refs_1_
  107.7 31.7 %collective-permute-done.7.refs_9_ = bf16[576,1536]{1,0:T(8,128)(2,1)} collective-permute-done((bf16[576,1536]{1,0:T(8,128)(2,1)}, bf16[576,1536]{1,0:T(8,128)(2,1)}, u32[]{:S(2)}, u32[]{:S(2)}) %collective-permute-start.7) | collective-permute-done | bytes 1769504 | tf_op jit(solution)/shard_map/ppermute | solution.py:546
  146.5 21.2 %shard_map.213 = (bf16[4,128,1536]{2,1,0:T(8,128)(2,1)}, f32[4,2,128,128]{3,2,1,0:T(8,128)}, bf16[4,128,1536]{2,1,0:T(8,128)(2,1)}) custom-call(s32[5]{0:T(128)} %pad_add_fusion.refs_0_, f32[4,128,1536]{2,1,0:T(8,128)} %fusion.refs_1_, bf16[4,1024,512]{2,1,0:T(8,128)(2,1)} %all-gather.9.cloned.1.call-done.refs_2_, ...), custom_call_target="tpu_custom_call" | custom-call | flops 22548578304 | bytes 10485760 | tf_op jit(solution)/shard_map/pallas_call | solution.py:156
  170.8 7.4 all-gather.11.cloned.1.call-done
  178.2 5.2 multiply_reduce_fusion.2
  186.6 8.2 convolution_convert_fusion.1
  194.8 4.9 all-to-all-start
  209.7 74.1 %collective-permute-done.13.refs_7_ = bf16[192,1536]{1,0:T(8,128)(2,1)S(1)} collective-permute-done((bf16[192,1536]{1,0:T(8,128)(2,1)S(1)}, bf16[192,1536]{1,0:T(8,128)(2,1)S(1)}, u32[]{:S(2)}, u32[]{:S(2)}) %collective-permute-start.13) | collective-permute-done | bytes 589856 | tf_op jit(solution)/shard_map/ppermute | solution.py:546
  283.8 12.1 %collective-permute-done.14.refs_8_ = bf16[192,1536]{1,0:T(8,128)(2,1)} collective-permute-done((bf16[192,1536]{1,0:T(8,128)(2,1)S(1)}, bf16[192,1536]{1,0:T(8,128)(2,1)}, u32[]{:S(2)}, u32[]{:S(2)}) %collective-permute-start.14) | collective-permute-done | bytes 589856 | tf_op jit(solution)/shard_map/ppermute | solution.py:546
  297.1 8.7 convolution_convert_fusion
  305.8 5.1 all-to-all-start.1
  315.9 101.4 %collective-permute-done.19.refs_6_ = bf16[192,1536]{1,0:T(8,128)(2,1)S(1)} collective-permute-done((bf16[192,1536]{1,0:T(8,128)(2,1)}, bf16[192,1536]{1,0:T(8,128)(2,1)S(1)}, u32[]{:S(2)}, u32[]{:S(2)}) %collective-permute-start.19) | collective-permute-done | bytes 589856 | tf_op jit(solution)/shard_map/ppermute | solution.py:546
  423.0 52.7 %shard_map.215 = (bf16[8,2,80,1536]{3,2,1,0:T(8,128)(2,1)}, bf16[8,2,80,1664]{3,2,1,0:T(8,128)(2,1)}, bf16[576,1536]{1,0:T(8,128)(2,1)}, bf16[576,1536]{1,0:T(8,...) custom-call(s32[3]{0:T(128)} %get-tuple-element.296.refs_0_, ...), custom_call_target="tpu_custom_call" | custom-call | flops 57378078720 | bytes 44040192 | tf_op jit(solution)/shard_map/pallas_call | solution.py:463
  478.1 4.5 all-to-all-start.2
  482.6 51.2 %shard_map.216 = (bf16[8,2,80,1536]{3,2,1,0:T(8,128)(2,1)}, bf16[8,2,80,1664]{3,2,1,0:T(8,128)(2,1)}, bf16[576,1536]{1,0:T(8,128)(2,1)}, bf16[576,1536]{1,0:T(8,...) custom-call(s32[3]{0:T(128)} %get-tuple-element.297.refs_0_, ...), custom_call_target="tpu_custom_call" | custom-call | flops 57378078720 | bytes 44040192 | tf_op jit(solution)/shard_map/pallas_call | solution.py:463
  533.8 9.1 collective-permute-done.23
  544.2 4.6 all-to-all-start.3
  549.0 46.1 %all-to-all-done.3 = bf16[8,2,80,1536]{3,2,1,0:T(8,128)(2,1)} async-done(((bf16[8,2,80,1536]{3,2,1,0:T(8,128)(2,1)}), bf16[8,2,80,1536]{3,2,1,0:T(8,128)(2,1)}, u32[]{:S(2)}, u32[]{:S(2)}) %all-to-all-start.3) | async-done | bytes 3932192 | tf_op jit(solution)/shard_map/all_to_all | solution.py:564
  598.0 4.2 fusion.32
  603.5 4.6 all-to-all-start.4
  611.3 46.3 %collective-permute-done.26 = bf16[512,1536]{1,0:T(8,128)(2,1)S(1)} collective-permute-done((bf16[512,1536]{1,0:T(8,128)(2,1)}, bf16[512,1536]{1,0:T(8,128)(2,1)S(1)}, u32[]{:S(2)}, u32[]{:S(2)}) %collective-permute-start.26) | collective-permute-done | bytes 1572896 | tf_op jit(solution)/shard_map/ppermute | solution.py:561
  657.6 4.8 convert_add_fusion.4
  665.1 4.6 all-to-all-start.5
  669.7 5.0 multiply_convert_fusion
  674.8 6.7 convolution_convert_fusion.2
  681.5 27.6 %shard_map.217 = (bf16[4,128,1536]{2,1,0:T(8,128)(2,1)}, bf16[8,4,128,512]{3,2,1,0:T(8,128)(2,1)}) custom-call(s32[5]{0:T(128)} %pad_add_fusion.refs_0_, bf16[4,128,1536]{2,1,0:T(8,128)(2,1)} %get-tuple-element.209.refs_1_, bf16[4,1024,512]{2,1,0:T(8,128)(2,1)} %all-gather.9.cloned.1.call-done.refs_2_, bf16[4,128,1536]{2,1,0:T(8,128)(2,1)} %bitcast.312, ...), custom_call_target="tpu_custom_call" | custom-call | flops 28991029248 | bytes 17825792 | tf_op jit(solution)/shard_map/pallas_call | solution.py:191
  710.0 9.5 all-to-all-done.5
  719.5 24.9 %shard_map.218 = bf16[1536,3584]{1,0:T(8,128)(2,1)} custom-call(bf16[512,1536]{1,0:T(8,128)(2,1)} %bitcast.309, bf16[512,1536]{1,0:T(8,128)(2,1)} %copy-done.21, bf16[512,1536]{1,0:T(8,128)(2,1)} %fusion.25.x_ref.refs_2_, bf16[512,1536]{1,0:T(8,128)(2,1)} %bitcast.310, bf16[4096,1536]{1,0:T(8,128)(2,1)} %all-gather.13.cloned.1.call-done.refs_4_, ...), custom_call_target="tpu_custom_call" | custom-call | flops 22548578304 | bytes 12582912 | tf_op jit(solution)/shard_map/pallas_call | solution.py:402
  744.6 4.3 convert_add_fusion.2
  748.9 5.0 all-to-all-start.6
  758.6 3.7 fusion.40
  776.3 54.6 %collective-permute-done.31 = bf16[512,1664]{1,0:T(8,128)(2,1)S(1)} collective-permute-done((bf16[512,1664]{1,0:T(8,128)(2,1)S(1)}, bf16[512,1664]{1,0:T(8,128)(2,1)S(1)}, u32[]{:S(2)}, u32[]{:S(2)}) %collective-permute-start.31) | collective-permute-done | bytes 1703968 | tf_op jit(solution)/shard_map/ppermute | solution.py:561
  830.9 5.1 fusion.6
  836.0 4.6 reduce_sum.97
  843.4 7.1 fusion.31
  856.0 36.6 %collective-permute-done.32 = bf16[576,1536]{1,0:T(8,128)(2,1)} collective-permute-done((bf16[576,1536]{1,0:T(8,128)(2,1)}, bf16[576,1536]{1,0:T(8,128)(2,1)}, u32[]{:S(2)}, u32[]{:S(2)}) %collective-permute-start.32) | collective-permute-done | bytes 1769504 | tf_op jit(solution)/shard_map/ppermute | solution.py:546
  898.9 9.7 collective-permute-done.33
  908.6 12.9 %collective-permute-done.34 = bf16[48,3712]{1,0:T(8,128)(2,1)} collective-permute-done((bf16[48,3712]{1,0:T(8,128)(2,1)}, bf16[48,3712]{1,0:T(8,128)(2,1)}, u32[]{:S(2)}, u32[]{:S(2)}) %collective-permute-start.34) | collective-permute-done | bytes 356384 | tf_op jit(solution)/shard_map/ppermute | solution.py:546
  923.9 5.2 collective-permute-start.36
  937.0 32.2 %collective-permute-done.36 = bf16[576,1536]{1,0:T(8,128)(2,1)S(1)} collective-permute-done((bf16[576,1536]{1,0:T(8,128)(2,1)}, bf16[576,1536]{1,0:T(8,128)(2,1)S(1)}, u32[]{:S(2)}, u32[]{:S(2)}) %collective-permute-start.36) | collective-permute-done | bytes 1769504 | tf_op jit(solution)/shard_map/ppermute | solution.py:546
  (315 shorter events, 146.5 us)
Async XLA Ops:
  7.2 86.2 %all-gather.7.cloned.1.call-start = ((), (), s32[]{:S(2)}) async-start(), calls=%async_computation.8 | async-start | bytes 7077888 | tf_op jit(solution)/shard_map/all_gather | solution.py:567
  16.2 16.7 %collective-permute-start.2 = (bf16[48,2048]{1,0:T(8,128)(2,1)S(1)}, bf16[48,2048]{1,0:T(8,128)(2,1)S(1)}, u32[]{:S(2)}, u32[]{:S(2)}) collective-permute-start(bf16[48,2048]{1,0:T(8,128)(2,1)S(1)} %constant_dynamic-update-slice_fusion), channel_id=1, source_target_pairs={{0,2},{1,3},{2,0},{3,1},{4,6},{5,7},{6,4},{7,5},{8,10},{9,11},{10,... | collective-permute-start | bytes 589832 | tf_op jit(solution)/shard_map/ppermute | solution.py:546
  16.2 16.7 %collective-permute-start.3 = (bf16[48,2048]{1,0:T(8,128)(2,1)S(1)}, bf16[48,2048]{1,0:T(8,128)(2,1)S(1)}, u32[]{:S(2)}, u32[]{:S(2)}) collective-permute-start(bf16[48,2048]{1,0:T(8,128)(2,1)S(1)} %constant_dynamic-update-slice_fusion), channel_id=1, source_target_pairs={{0,1},{1,2},{2,3},{3,0},{4,5},{5,6},{6,7},{7,4},{8,9},{9,10},{10,1... | collective-permute-start | bytes 589832 | tf_op jit(solution)/shard_map/ppermute | solution.py:546
  34.0 105.4 %all-gather.9.cloned.1.call-start = ((), (), s32[]{:S(2)}) async-start(), calls=%async_computation.9 | async-start | bytes 4718592 | tf_op jit(solution)/shard_map/all_gather | solution.py:666
  37.9 55.5 %collective-permute-start = (bf16[576,1536]{1,0:T(8,128)(2,1)}, bf16[576,1536]{1,0:T(8,128)(2,1)}, u32[]{:S(2)}, u32[]{:S(2)}) collective-permute-start(bf16[576,1536]{1,0:T(8,128)(2,1)} %pad_maximum_fusion), channel_id=1, source_target_pairs={{0,1},{1,2},{2,3},{3,0},{4,5},{5,6},{6,7},{7,4},{8,9},{9,10},{10,1... | collective-permute-start | bytes 5308424 | tf_op jit(solution)/shard_map/ppermute | solution.py:546
  45.2 32.8 %collective-permute-start.8 = (bf16[2,384]{1,0:T(2,128)(2,1)S(1)}, bf16[2,384]{1,0:T(2,128)(2,1)S(1)}, u32[]{:S(2)}, u32[]{:S(2)}) collective-permute-start(bf16[2,384]{1,0:T(2,128)(2,1)S(1)} %pad_maximum_fusion.8), channel_id=1, source_target_pairs={{0,3},{1,0},{2,1},{3,2},{4,7},{5,4},{6,5},{7,6},{8,11},{9,8},{10,9... | collective-permute-start | bytes 4616 | tf_op jit(solution)/shard_map/ppermute | solution.py:546
  48.2 33.9 %collective-permute-start.9 = (bf16[2,384]{1,0:T(2,128)(2,1)S(1)}, bf16[2,384]{1,0:T(2,128)(2,1)S(1)}, u32[]{:S(2)}, u32[]{:S(2)}) collective-permute-start(bf16[2,384]{1,0:T(2,128)(2,1)S(1)} %pad_maximum_fusion.8), channel_id=1, source_target_pairs={{0,2},{1,3},{2,0},{3,1},{4,6},{5,7},{6,4},{7,5},{8,10},{9,11},{10,... | collective-permute-start | bytes 4616 | tf_op jit(solution)/shard_map/ppermute | solution.py:546
  49.2 35.6 %collective-permute-start.10 = (bf16[2,384]{1,0:T(2,128)(2,1)S(1)}, bf16[2,384]{1,0:T(2,128)(2,1)S(1)}, u32[]{:S(2)}, u32[]{:S(2)}) collective-permute-start(bf16[2,384]{1,0:T(2,128)(2,1)S(1)} %pad_maximum_fusion.8), channel_id=1, source_target_pairs={{0,1},{1,2},{2,3},{3,0},{4,5},{5,6},{6,7},{7,4},{8,9},{9,10},{10,1... | collective-permute-start | bytes 4616 | tf_op jit(solution)/shard_map/ppermute | solution.py:546
  49.2 37.3 %collective-permute-start.4 = (bf16[48,1536]{1,0:T(8,128)(2,1)S(1)}, bf16[48,1536]{1,0:T(8,128)(2,1)S(1)}, u32[]{:S(2)}, u32[]{:S(2)}) collective-permute-start(bf16[48,1536]{1,0:T(8,128)(2,1)S(1)} %constant_dynamic-slice_fusion.3), channel_id=1, source_target_pairs={{0,3},{1,0},{2,1},{3,2},{4,7},{5,4},{6,5},{7,6},{8,11},{9,8},{10,9... | collective-permute-start | bytes 442376 | tf_op jit(solution)/shard_map/ppermute | solution.py:546
  78.0 14.4 %collective-permute-start.5 = (bf16[48,1536]{1,0:T(8,128)(2,1)S(1)}, bf16[48,1536]{1,0:T(8,128)(2,1)S(1)}, u32[]{:S(2)}, u32[]{:S(2)}) collective-permute-start(bf16[48,1536]{1,0:T(8,128)(2,1)S(1)} %constant_dynamic-slice_fusion.3), channel_id=1, source_target_pairs={{0,2},{1,3},{2,0},{3,1},{4,6},{5,7},{6,4},{7,5},{8,10},{9,11},{10,... | collective-permute-start | bytes 442376 | tf_op jit(solution)/shard_map/ppermute | solution.py:546
  98.2 80.0 %all-gather.11.cloned.1.call-start = ((), (), s32[]{:S(2)}) async-start(), calls=%async_computation.10 | async-start | bytes 5308416 | tf_op jit(solution)/shard_map/all_gather | solution.py:567
  98.2 41.2 %collective-permute-start.7 = (bf16[576,1536]{1,0:T(8,128)(2,1)}, bf16[576,1536]{1,0:T(8,128)(2,1)}, u32[]{:S(2)}, u32[]{:S(2)}) collective-permute-start(bf16[576,1536]{1,0:T(8,128)(2,1)} %pad_maximum_fusion), channel_id=1, source_target_pairs={{0,3},{1,0},{2,1},{3,2},{4,7},{5,4},{6,5},{7,6},{8,11},{9,8},{10,9... | collective-permute-start | bytes 5308424 | tf_op jit(solution)/shard_map/ppermute | solution.py:546
  143.9 27.0 %collective-permute-start.11 = (bf16[192,1536]{1,0:T(8,128)(2,1)S(1)}, bf16[192,1536]{1,0:T(8,128)(2,1)S(1)}, u32[]{:S(2)}, u32[]{:S(2)}) collective-permute-start(bf16[192,1536]{1,0:T(8,128)(2,1)S(1)} %get-tuple-element.147), channel_id=1, source_target_pairs={{0,2},{1,3},{2,0},{3,1},{4,6},{5,7},{6,4},{7,5},{8,10},{9,11},{10,... | collective-permute-start | bytes 1769480 | tf_op jit(solution)/shard_map/ppermute | solution.py:546
  143.9 23.9 %collective-permute-start.12 = (bf16[512,128]{1,0:T(8,128)(2,1)S(1)}, bf16[512,128]{1,0:T(8,128)(2,1)S(1)}, u32[]{:S(2)}, u32[]{:S(2)}) collective-permute-start(bf16[512,128]{1,0:T(8,128)(2,1)S(1)} %pad_maximum_fusion.5), channel_id=1, source_target_pairs={{0,1},{1,0},{2,3},{3,2},{4,5},{5,4},{6,7},{7,6},{8,9},{9,8},{10,11... | collective-permute-start | bytes 393224 | tf_op jit(solution)/shard_map/ppermute | solution.py:561
  194.8 102.2 %all-to-all-start = ((bf16[8,2,80,3200]{3,2,1,0:T(8,128)(2,1)}), bf16[8,2,80,3200]{3,2,1,0:T(8,128)(2,1)}, u32[]{:S(2)}, u32[]{:S(2)}) async-start(bf16[8,2,80,3200]{3,2,1,0:T(8,128)(2,1)} %bitcast.277), calls=%async_computation | async-start | bytes 16384000 | tf_op jit(solution)/shard_map/all_to_all | solution.py:564
  201.0 96.0 %collective-permute-start.15 = (bf16[512,1536]{1,0:T(8,128)(2,1)}, bf16[512,1536]{1,0:T(8,128)(2,1)}, u32[]{:S(2)}, u32[]{:S(2)}) collective-permute-start(bf16[512,1536]{1,0:T(8,128)(2,1)} %multiply_convert_fusion.1), channel_id=1, source_target_pairs={{0,1},{1,0},{2,3},{3,2},{4,5},{5,4},{6,7},{7,6},{8,9},{9,8},{10,11... | collective-permute-start | bytes 4718600 | tf_op jit(solution)/shard_map/ppermute | solution.py:561
  202.5 94.5 %collective-permute-start.16 = (bf16[512,1536]{1,0:T(8,128)(2,1)}, bf16[512,1536]{1,0:T(8,128)(2,1)}, u32[]{:S(2)}, u32[]{:S(2)}) collective-permute-start(bf16[512,1536]{1,0:T(8,128)(2,1)} %slice.163), channel_id=1, source_target_pairs={{0,1},{1,0},{2,3},{3,2},{4,5},{5,4},{6,7},{7,6},{8,9},{9,8},{10,11... | collective-permute-start | bytes 4718600 | tf_op jit(solution)/shard_map/ppermute | solution.py:561
  206.1 77.7 %collective-permute-start.13 = (bf16[192,1536]{1,0:T(8,128)(2,1)S(1)}, bf16[192,1536]{1,0:T(8,128)(2,1)S(1)}, u32[]{:S(2)}, u32[]{:S(2)}) collective-permute-start(bf16[192,1536]{1,0:T(8,128)(2,1)S(1)} %copy-done.23), channel_id=1, source_target_pairs={{0,2},{1,3},{2,0},{3,1},{4,6},{5,7},{6,4},{7,5},{8,10},{9,11},{10,... | collective-permute-start | bytes 1769480 | tf_op jit(solution)/shard_map/ppermute | solution.py:546
  208.6 87.3 %collective-permute-start.14 = (bf16[192,1536]{1,0:T(8,128)(2,1)S(1)}, bf16[192,1536]{1,0:T(8,128)(2,1)}, u32[]{:S(2)}, u32[]{:S(2)}) collective-permute-start(bf16[192,1536]{1,0:T(8,128)(2,1)S(1)} %copy-done.24), channel_id=1, source_target_pairs={{0,2},{1,3},{2,0},{3,1},{4,6},{5,7},{6,4},{7,5},{8,10},{9,11},{10,... | collective-permute-start | bytes 1769480 | tf_op jit(solution)/shard_map/ppermute | solution.py:546
  305.8 113.6 %all-to-all-start.1 = ((bf16[8,2,80,3200]{3,2,1,0:T(8,128)(2,1)}), bf16[8,2,80,3200]{3,2,1,0:T(8,128)(2,1)}, u32[]{:S(2)}, u32[]{:S(2)}) async-start(bf16[8,2,80,3200]{3,2,1,0:T(8,128)(2,1)} %bitcast.278), calls=%async_computation.1 | async-start | bytes 16384000 | tf_op jit(solution)/shard_map/all_to_all | solution.py:564
  310.9 232.1 %all-gather.13.cloned.1.call-start = ((), (), s32[]{:S(2)}) async-start(), calls=%async_computation.11 | async-start | bytes 14155776 | tf_op jit(solution)/shard_map/all_gather | solution.py:711
  310.9 106.4 %collective-permute-start.17 = (bf16[576,1536]{1,0:T(8,128)(2,1)S(1)}, bf16[576,1536]{1,0:T(8,128)(2,1)S(1)}, u32[]{:S(2)}, u32[]{:S(2)}) collective-permute-start(bf16[576,1536]{1,0:T(8,128)(2,1)S(1)} %copy-done.20), channel_id=1, source_target_pairs={{0,1},{1,2},{2,3},{3,0},{4,5},{5,6},{6,7},{7,4},{8,9},{9,10},{10,1... | collective-permute-start | bytes 5308424 | tf_op jit(solution)/shard_map/ppermute | solution.py:546
  313.9 105.6 %collective-permute-start.18 = (bf16[576,1536]{1,0:T(8,128)(2,1)S(1)}, bf16[576,1536]{1,0:T(8,128)(2,1)}, u32[]{:S(2)}, u32[]{:S(2)}) collective-permute-start(bf16[576,1536]{1,0:T(8,128)(2,1)S(1)} %copy-done.20), channel_id=1, source_target_pairs={{0,3},{1,0},{2,1},{3,2},{4,7},{5,4},{6,5},{7,6},{8,11},{9,8},{10,9... | collective-permute-start | bytes 5308424 | tf_op jit(solution)/shard_map/ppermute | solution.py:546
  315.3 102.0 %collective-permute-start.19 = (bf16[192,1536]{1,0:T(8,128)(2,1)}, bf16[192,1536]{1,0:T(8,128)(2,1)S(1)}, u32[]{:S(2)}, u32[]{:S(2)}) collective-permute-start(bf16[192,1536]{1,0:T(8,128)(2,1)} %get-tuple-element.167), channel_id=1, source_target_pairs={{0,2},{1,3},{2,0},{3,1},{4,6},{5,7},{6,4},{7,5},{8,10},{9,11},{10,... | collective-permute-start | bytes 1769480 | tf_op jit(solution)/shard_map/ppermute | solution.py:546
  420.1 55.6 %collective-permute-start.20 = (bf16[192,1536]{1,0:T(8,128)(2,1)}, bf16[192,1536]{1,0:T(8,128)(2,1)S(1)}, u32[]{:S(2)}, u32[]{:S(2)}) collective-permute-start(bf16[192,1536]{1,0:T(8,128)(2,1)} %get-tuple-element.171), channel_id=1, source_target_pairs={{0,2},{1,3},{2,0},{3,1},{4,6},{5,7},{6,4},{7,5},{8,10},{9,11},{10,... | collective-permute-start | bytes 1769480 | tf_op jit(solution)/shard_map/ppermute | solution.py:546
  420.1 55.7 %collective-permute-start.21 = (bf16[192,1536]{1,0:T(8,128)(2,1)}, bf16[192,1536]{1,0:T(8,128)(2,1)S(1)}, u32[]{:S(2)}, u32[]{:S(2)}) collective-permute-start(bf16[192,1536]{1,0:T(8,128)(2,1)} %get-tuple-element.172), channel_id=1, source_target_pairs={{0,2},{1,3},{2,0},{3,1},{4,6},{5,7},{6,4},{7,5},{8,10},{9,11},{10,... | collective-permute-start | bytes 1769480 | tf_op jit(solution)/shard_map/ppermute | solution.py:546
  476.7 66.2 %collective-permute-start.22 = (bf16[576,1536]{1,0:T(8,128)(2,1)}, bf16[576,1536]{1,0:T(8,128)(2,1)S(1)}, u32[]{:S(2)}, u32[]{:S(2)}) collective-permute-start(bf16[576,1536]{1,0:T(8,128)(2,1)} %get-tuple-element.184), channel_id=1, source_target_pairs={{0,1},{1,2},{2,3},{3,0},{4,5},{5,6},{6,7},{7,4},{8,9},{9,10},{10,1... | collective-permute-start | bytes 5308424 | tf_op jit(solution)/shard_map/ppermute | solution.py:546
  476.7 66.2 %collective-permute-start.23 = (bf16[192,1536]{1,0:T(8,128)(2,1)}, bf16[192,1536]{1,0:T(8,128)(2,1)}, u32[]{:S(2)}, u32[]{:S(2)}) collective-permute-start(bf16[192,1536]{1,0:T(8,128)(2,1)} %get-tuple-element.185), channel_id=1, source_target_pairs={{0,2},{1,3},{2,0},{3,1},{4,6},{5,7},{6,4},{7,5},{8,10},{9,11},{10,... | collective-permute-start | bytes 1769480 | tf_op jit(solution)/shard_map/ppermute | solution.py:546
  478.1 64.8 %all-to-all-start.2 = ((bf16[8,2,80,1536]{3,2,1,0:T(8,128)(2,1)}), bf16[8,2,80,1536]{3,2,1,0:T(8,128)(2,1)}, u32[]{:S(2)}, u32[]{:S(2)}) async-start(bf16[8,2,80,1536]{3,2,1,0:T(8,128)(2,1)} %get-tuple-element.193), calls=%async_computation.2 | async-start | bytes 7864320 | tf_op jit(solution)/shard_map/all_to_all | solution.py:564
  544.2 50.9 %all-to-all-start.3 = ((bf16[8,2,80,1536]{3,2,1,0:T(8,128)(2,1)}), bf16[8,2,80,1536]{3,2,1,0:T(8,128)(2,1)}, u32[]{:S(2)}, u32[]{:S(2)}) async-start(bf16[8,2,80,1536]{3,2,1,0:T(8,128)(2,1)} %get-tuple-element.199), calls=%async_computation.3 | async-start | bytes 7864320 | tf_op jit(solution)/shard_map/all_to_all | solution.py:564
  548.7 53.5 %collective-permute-start.24 = (bf16[576,1536]{1,0:T(8,128)(2,1)}, bf16[576,1536]{1,0:T(8,128)(2,1)S(1)}, u32[]{:S(2)}, u32[]{:S(2)}) collective-permute-start(bf16[576,1536]{1,0:T(8,128)(2,1)} %get-tuple-element.197), channel_id=1, source_target_pairs={{0,3},{1,0},{2,1},{3,2},{4,7},{5,4},{6,5},{7,6},{8,11},{9,8},{10,9... | collective-permute-start | bytes 5308424 | tf_op jit(solution)/shard_map/ppermute | solution.py:546
  603.5 58.9 %all-to-all-start.4 = ((bf16[8,2,80,1664]{3,2,1,0:T(8,128)(2,1)}), bf16[8,2,80,1664]{3,2,1,0:T(8,128)(2,1)}, u32[]{:S(2)}, u32[]{:S(2)}) async-start(bf16[8,2,80,1664]{3,2,1,0:T(8,128)(2,1)} %get-tuple-element.204), calls=%async_computation.4 | async-start | bytes 8519680 | tf_op jit(solution)/shard_map/all_to_all | solution.py:564
  608.1 49.5 %collective-permute-start.26 = (bf16[512,1536]{1,0:T(8,128)(2,1)}, bf16[512,1536]{1,0:T(8,128)(2,1)S(1)}, u32[]{:S(2)}, u32[]{:S(2)}) collective-permute-start(bf16[512,1536]{1,0:T(8,128)(2,1)} %fusion.32), channel_id=1, source_target_pairs={{0,1},{1,0},{2,3},{3,2},{4,5},{5,4},{6,7},{7,6},{8,9},{9,8},{10,11... | collective-permute-start | bytes 4718600 | tf_op jit(solution)/shard_map/ppermute | solution.py:561
  608.2 54.2 %collective-permute-start.25 = (bf16[192,1536]{1,0:T(8,128)(2,1)}, bf16[192,1536]{1,0:T(8,128)(2,1)}, u32[]{:S(2)}, u32[]{:S(2)}) collective-permute-start(bf16[192,1536]{1,0:T(8,128)(2,1)} %get-tuple-element.202), channel_id=1, source_target_pairs={{0,2},{1,3},{2,0},{3,1},{4,6},{5,7},{6,4},{7,5},{8,10},{9,11},{10,... | collective-permute-start | bytes 1769480 | tf_op jit(solution)/shard_map/ppermute | solution.py:546
  665.1 54.4 %all-to-all-start.5 = ((bf16[8,2,80,1664]{3,2,1,0:T(8,128)(2,1)}), bf16[8,2,80,1664]{3,2,1,0:T(8,128)(2,1)}, u32[]{:S(2)}, u32[]{:S(2)}) async-start(bf16[8,2,80,1664]{3,2,1,0:T(8,128)(2,1)} %get-tuple-element.216), calls=%async_computation.5 | async-start | bytes 8519680 | tf_op jit(solution)/shard_map/all_to_all | solution.py:564
  669.7 186.4 %reduce-scatter.2.cloned.1.call-start = ((), (), s32[]{:S(2)}) async-start(), calls=%async_computation.12 | async-start | bytes 12386304 | tf_op jit(solution)/shard_map/reduce_scatter | solution.py:771
  681.5 28.5 %collective-permute-start.27 = (bf16[192,1536]{1,0:T(8,128)(2,1)}, bf16[192,1536]{1,0:T(8,128)(2,1)}, u32[]{:S(2)}, u32[]{:S(2)}) collective-permute-start(bf16[192,1536]{1,0:T(8,128)(2,1)} %get-tuple-element.208), channel_id=1, source_target_pairs={{0,2},{1,3},{2,0},{3,1},{4,6},{5,7},{6,4},{7,5},{8,10},{9,11},{10,... | collective-permute-start | bytes 1769480 | tf_op jit(solution)/shard_map/ppermute | solution.py:546
  719.5 25.0 %collective-permute-start.28 = (bf16[192,1536]{1,0:T(8,128)(2,1)}, bf16[192,1536]{1,0:T(8,128)(2,1)}, u32[]{:S(2)}, u32[]{:S(2)}) collective-permute-start(bf16[192,1536]{1,0:T(8,128)(2,1)} %get-tuple-element.218), channel_id=1, source_target_pairs={{0,2},{1,3},{2,0},{3,1},{4,6},{5,7},{6,4},{7,5},{8,10},{9,11},{10,... | collective-permute-start | bytes 1769480 | tf_op jit(solution)/shard_map/ppermute | solution.py:546
  748.9 87.1 %all-to-all-start.6 = ((bf16[8,4,128,512]{3,2,1,0:T(8,128)(2,1)}), bf16[8,4,128,512]{3,2,1,0:T(8,128)(2,1)}, u32[]{:S(2)}, u32[]{:S(2)}) async-start(bf16[8,4,128,512]{3,2,1,0:T(8,128)(2,1)} %get-tuple-element.221), calls=%async_computation.6 | async-start | bytes 8388608 | tf_op jit(solution)/shard_map/all_to_all | solution.py:564
  753.9 219.9 %all-gather.15.cloned.1.call-start = ((), (), s32[]{:S(2)}) async-start(), calls=%async_computation.13 | async-start | bytes 3207168 | tf_op jit(solution)/shard_map/all_gather | solution.py:816
  765.8 65.0 %collective-permute-start.31 = (bf16[512,1664]{1,0:T(8,128)(2,1)S(1)}, bf16[512,1664]{1,0:T(8,128)(2,1)S(1)}, u32[]{:S(2)}, u32[]{:S(2)}) collective-permute-start(bf16[512,1664]{1,0:T(8,128)(2,1)S(1)} %fusion.5), channel_id=1, source_target_pairs={{0,1},{1,0},{2,3},{3,2},{4,5},{5,4},{6,7},{7,6},{8,9},{9,8},{10,11... | collective-permute-start | bytes 5111816 | tf_op jit(solution)/shard_map/ppermute | solution.py:561
  770.1 70.5 %collective-permute-start.29 = (bf16[192,1536]{1,0:T(8,128)(2,1)}, bf16[192,1536]{1,0:T(8,128)(2,1)}, u32[]{:S(2)}, u32[]{:S(2)}) collective-permute-start(bf16[192,1536]{1,0:T(8,128)(2,1)} %get-tuple-element.226), channel_id=1, source_target_pairs={{0,2},{1,3},{2,0},{3,1},{4,6},{5,7},{6,4},{7,5},{8,10},{9,11},{10,... | collective-permute-start | bytes 1769480 | tf_op jit(solution)/shard_map/ppermute | solution.py:546
  772.5 68.1 %collective-permute-start.30 = (bf16[192,1536]{1,0:T(8,128)(2,1)}, bf16[192,1536]{1,0:T(8,128)(2,1)}, u32[]{:S(2)}, u32[]{:S(2)}) collective-permute-start(bf16[192,1536]{1,0:T(8,128)(2,1)} %get-tuple-element.227), channel_id=1, source_target_pairs={{0,2},{1,3},{2,0},{3,1},{4,6},{5,7},{6,4},{7,5},{8,10},{9,11},{10,... | collective-permute-start | bytes 1769480 | tf_op jit(solution)/shard_map/ppermute | solution.py:546
  850.5 42.2 %collective-permute-start.32 = (bf16[576,1536]{1,0:T(8,128)(2,1)}, bf16[576,1536]{1,0:T(8,128)(2,1)}, u32[]{:S(2)}, u32[]{:S(2)}) collective-permute-start(bf16[576,1536]{1,0:T(8,128)(2,1)} %get-tuple-element.241), channel_id=1, source_target_pairs={{0,1},{1,2},{2,3},{3,0},{4,5},{5,6},{6,7},{7,4},{8,9},{9,10},{10,1... | collective-permute-start | bytes 5308424 | tf_op jit(solution)/shard_map/ppermute | solution.py:546
  894.8 13.7 %collective-permute-start.33 = (bf16[48,3712]{1,0:T(8,128)(2,1)}, bf16[48,3712]{1,0:T(8,128)(2,1)}, u32[]{:S(2)}, u32[]{:S(2)}) collective-permute-start(bf16[48,3712]{1,0:T(8,128)(2,1)} %get-tuple-element.278), channel_id=1, source_target_pairs={{0,1},{1,2},{2,3},{3,0},{4,5},{5,6},{6,7},{7,4},{8,9},{9,10},{10,1... | collective-permute-start | bytes 1069064 | tf_op jit(solution)/shard_map/ppermute | solution.py:546
  895.1 26.4 %collective-permute-start.34 = (bf16[48,3712]{1,0:T(8,128)(2,1)}, bf16[48,3712]{1,0:T(8,128)(2,1)}, u32[]{:S(2)}, u32[]{:S(2)}) collective-permute-start(bf16[48,3712]{1,0:T(8,128)(2,1)} %get-tuple-element.279), channel_id=1, source_target_pairs={{0,2},{1,3},{2,0},{3,1},{4,6},{5,7},{6,4},{7,5},{8,10},{9,11},{10,... | collective-permute-start | bytes 1069064 | tf_op jit(solution)/shard_map/ppermute | solution.py:546
  895.3 26.2 %collective-permute-start.35 = (bf16[48,3712]{1,0:T(8,128)(2,1)}, bf16[48,3712]{1,0:T(8,128)(2,1)}, u32[]{:S(2)}, u32[]{:S(2)}) collective-permute-start(bf16[48,3712]{1,0:T(8,128)(2,1)} %get-tuple-element.280), channel_id=1, source_target_pairs={{0,3},{1,0},{2,1},{3,2},{4,7},{5,4},{6,5},{7,6},{8,11},{9,8},{10,9... | collective-permute-start | bytes 1069064 | tf_op jit(solution)/shard_map/ppermute | solution.py:546
  923.9 45.3 %collective-permute-start.36 = (bf16[576,1536]{1,0:T(8,128)(2,1)}, bf16[576,1536]{1,0:T(8,128)(2,1)S(1)}, u32[]{:S(2)}, u32[]{:S(2)}) collective-permute-start(bf16[576,1536]{1,0:T(8,128)(2,1)} %get-tuple-element.257), channel_id=1, source_target_pairs={{0,3},{1,0},{2,1},{3,2},{4,7},{5,4},{6,5},{7,6},{8,11},{9,8},{10,9... | collective-permute-start | bytes 5308424 | tf_op jit(solution)/shard_map/ppermute | solution.py:546
  (54 other events, 1182.1 us)
Sparse Core Ops, SparseCore 0:
  34.1 45.9 all-gather.6
  98.3 35.3 all-gather.8
  139.5 38.6 all-gather.10
  419.6 74.4 all-gather.12
  744.7 111.2 reduce-scatter.1
  923.9 35.3 all-gather.14

commit v3 on v2

--- a/solution.py
+++ b/solution.py
@@ -424,6 +424,54 @@
             transcendentals=0,
         ),
     )(att, db, x, dq, every_x, pairs)
+
+
+def input_back_kernel(
+    dq_ref, terms_ref, w_ref, x_ref, inverse_ref, gain_ref, upstream_ref, out_ref, gain_out
+):
+    width = dq_ref.shape[1]
+    pairs = jnp.sum(terms_ref[:, 0].astype(F32), axis=0).astype(BF16)
+    grad = mm_nt(dq_ref[...], w_ref[:, :width]) + mm_nt(pairs, w_ref[:, width:])
+    values, inverse = x_ref[...].astype(F32), inverse_ref[...]
+
+    @pl.when(pl.program_id(0) == 0)
+    def _():
+        gain_out[...] = jnp.zeros_like(gain_out)
+
+    gain_out[...] += jnp.sum(grad * values * inverse, axis=0, keepdims=True)
+    scaled = grad * gain_ref[...]
+    projected = jnp.mean(scaled * values, axis=-1, keepdims=True)
+    out_ref[...] = upstream_ref[...] + inverse * scaled - values * inverse**3 * projected
+
+
+def input_back(dq, terms, w, x, inverse, gain, upstream):
+    ctx_count, nseq, tl, wide = terms.shape
+    rows, D = x.shape
+    return pl.pallas_call(
+        input_back_kernel,
+        grid=(nseq,),
+        in_specs=[
+            pl.BlockSpec((tl, dq.shape[1]), lambda i: (i, 0)),
+            pl.BlockSpec((ctx_count, 1, tl, wide), lambda i: (0, i, 0, 0)),
+            pl.BlockSpec(w.shape, lambda i: (0, 0)),
+            pl.BlockSpec((tl, D), lambda i: (i, 0)),
+            pl.BlockSpec((tl, 1), lambda i: (i, 0)),
+            pl.BlockSpec((1, D), lambda i: (0, 0)),
+            pl.BlockSpec((tl, D), lambda i: (i, 0)),
+        ],
+        out_specs=[
+            pl.BlockSpec((tl, D), lambda i: (i, 0)),
+            pl.BlockSpec((1, D), lambda i: (0, 0)),
+        ],
+        out_shape=[
+            jax.ShapeDtypeStruct((rows, D), F32),
+            jax.ShapeDtypeStruct((1, D), F32),
+        ],
+        compiler_params=pltpu.CompilerParams(vmem_limit_bytes=VMEM_LIMIT),
+        cost_estimate=pl.CostEstimate(
+            flops=8 * rows * w.size, bytes_accessed=16 * rows * D, transcendentals=0
+        ),
+    )(dq, terms, w, x, inverse, gain, upstream)
 
 
 def blank(shapes):
@@ -680,16 +728,16 @@
     second_low = second.astype(BF16)
 
     second_low, cot_wide = step([], (second_low, cot_wide), ["w2b", "w2c"])
-    expert_rows = [exchange(to_slots(sels[0], jnp.concatenate([second_low, cot_wide], axis=1)))]
+    wide_rows = jnp.concatenate([second_low, cot_wide], axis=1)
+    expert_rows = [exchange(to_slots(sels[0], wide_rows))]
     shards = None
     if merged:
-        far, far_cot = swap(second_low), swap(cot_wide[:, :D])
+        far_rows = swap(wide_rows)
         sels.append(route(far_table))
         shards = list(blank([(pieces, Dl, 2 * W), (pieces, W // F, D)]))
-        far, far_cot, expert_rows[0], sels[1], shards = step(
-            ["w2b", "w2c"], (far, far_cot, expert_rows[0], sels[1], shards), ["v1", "v3", "v2a"]
+        far_rows, expert_rows[0], sels[1], shards = step(
+            ["w2b", "w2c"], (far_rows, expert_rows[0], sels[1], shards), ["v1", "v3", "v2a"]
         )
-        far_rows = jnp.concatenate([far, far_cot, far_table], axis=1)
         expert_rows.append(exchange(to_slots(sels[1], far_rows)))
 
     def expert(j):
@@ -753,8 +801,7 @@
         far, mixed[0] = step(["p3"], (sums[1].astype(BF16), mixed[0]), ["p2b"])
         dispatch_grad = dispatch_grad + swap(far).astype(F32)
         mixed[0] = exchange(mixed[0])
-        dispatch_grad, mixed[0], mixed[1] = step(["p2b"], (dispatch_grad, mixed[0], mixed[1]), [])
-        mixed[1] = exchange(mixed[1])
+        (dispatch_grad,) = step(["p2b"], (dispatch_grad,), [])
 
     upstream = cot.astype(F32)
     norm_grad, second_grads = norm_backward(hidden, inverse_two, second_scale, dispatch_grad)
@@ -772,27 +819,24 @@
         return gate(total)[0].reshape(F, cut, -1)
 
     d_att = mm_nt(branch_grad, out_full).astype(BF16)
-    (d_att,) = step([], (d_att,), ["p2c"])
+    if merged:
+        d_att, mixed[0], mixed[1] = step([], (d_att, mixed[0], mixed[1]), ["p2c"])
+        mixed[1] = exchange(mixed[1])
     query_back, terms = attention_back(
         queries, kv_all, d_att.reshape(nseq, tl, width), lse, info, all_tables, C
     )
     query_back = query_back.reshape(rows, width)
-    terms, query_back, mixed[-1] = step(["p2c"], (terms, query_back, mixed[-1]), ["q2a"])
+    terms, query_back = step(["p2c"], (terms, query_back), ["q2a"])
     if merged:
-        own_terms = over_ctx(terms)
+        own_terms = exchange(terms)
         flat_terms = terms.reshape(C * rows, -1)
         blocks = weight_grads(
             attended_low, branch_grad, normed_low, query_back, every_normed, flat_terms, C, F
         )
         blocks, mixed = step(["q2a"], (blocks, mixed), ["q2b", "q2c"])
         mixed_sums = collect(mixed)
-        mixed_rows = mixed_sums[0] + swap(mixed_sums[1].astype(BF16)).astype(F32)
-        fill(role * mine, pair_sum(operands["p0"], "p2a", "p2b", "p2c"))
-        fill((1 - role) * mine, pair_sum(messages["p1"], "p3"))
-        own_terms, shards, mixed_rows = step(
-            ["q2b", "q2c"], (own_terms, shards, mixed_rows), ["q1"]
-        )
-        fill(role * mine + 1, pair_sum(operands["q0"], "q2a", "q2b", "q2c"))
+        far = swap(mixed_sums[1].astype(BF16))
+        own_terms, shards, far = step(["q2b", "q2c"], (own_terms, shards, far), ["q1"])
     else:
         own_terms = over_ctx(terms)
         pair_grad = mm_tn(normed_low, own_terms.reshape(rows, 2 * KV * HD))
@@ -801,18 +845,33 @@
         blocks = by_target(jnp.concatenate([projection_grad, query_grad, pair_grad], axis=1))
         mixed_rows = collect(mixed)[0]
     weight_rows = scatter(blocks)
-    kv_back = own_terms.reshape(rows, 2 * KV * HD)
-    normed_grad = mm_nt(query_back, qkv_full[:, :width]) + mm_nt(kv_back, qkv_full[:, width:])
-    entry_grad, first_grads = norm_backward(inputs, inverse_one, first_scale, normed_grad)
-    grad_tokens = hidden_grad + entry_grad
+    if not merged:
+        own_terms = own_terms.reshape((1,) + terms.shape[1:])
+    grad_tokens, first_grads = input_back(
+        query_back,
+        own_terms,
+        qkv_full,
+        tokens.reshape(rows, D),
+        inverse_one,
+        first_scale[None],
+        hidden_grad,
+    )
+    first_grads = first_grads[0]
+    if merged:
+        first_grads, mixed_sums[0] = step(["q1"], (first_grads, mixed_sums[0]), [])
+        fill(role * mine, pair_sum(operands["p0"], "p2a", "p2b", "p2c"))
+        fill((1 - role) * mine, pair_sum(messages["p1"], "p3"))
     gain_columns = jnp.stack([first_grads, second_grads]).reshape(2, F, Dl).transpose(1, 0, 2)
     gain_columns = gain_columns.reshape(F, cut, -1)
     gain_count = gain_columns.shape[2]
     gain_columns = jnp.pad(gain_columns, ((0, 0), (0, 0), (0, -gain_count % HD)))
-    weight_rows, gain_columns, shards = step(["q1"], (weight_rows, gain_columns, shards), [])
+    weight_rows, gain_columns = gate(weight_rows, gain_columns)
     wide = jnp.concatenate([weight_rows, gain_columns.astype(BF16)], axis=2)
     wide = fsdp_scatter_sum(wide).astype(BF16)
-    wide, shards = step([], (wide, shards), ["q3"])
+    if merged:
+        wide, far = step([], (wide, far), ["q3"])
+        mixed_rows = mixed_sums[0] + far.astype(F32)
+        fill(role * mine + 1, pair_sum(operands["q0"], "q2a", "q2b", "q2c"))
     wide = lax.all_gather(wide, "ctx", axis=0, tiled=False)
     whole = wide[:, :, : D + width + 2 * KV * HD].reshape(Dl, -1).astype(F32)
     grad_projection, grad_query = whole[:, :D], whole[:, D : D + width]
@@ -821,6 +880,9 @@
     gain_sums = jnp.sum(wide[:, :, gain_at : gain_at + gain_count].astype(F32), axis=0)
     grad_first, grad_second = gain_sums.reshape(2, Dl)
 
+    grads = (grad_projection, grad_query, grad_pairs, grad_first, grad_second)
+    grads = step(["q3"], grads, [])
+    grad_projection, grad_query, grad_pairs, grad_first, grad_second = grads
     block_rows = (hidden + mixed_rows[:, :D]).astype(BF16)
     router_by_expert = mixed_rows[:, D : D + EXPERTS]
     grad_router = jnp.sum(jnp.where(hit, router_by_expert[:, None, :], 0.0), axis=2)

time: 1000 us -> 953 us (0.953)
  waiting for transfers between devices: 531 us -> 474 us
  Pallas kernels: 182 us -> 199 us
  matrix products: 74.1 us -> 63.3 us
    ppermute x5 -> x4, waiting for transfers between devices: 102 us -> 40.4 us  [swap(): return lax.ppermute(block, 'fsdp', [(i, i ^ 1) for i in range(F)])]
    ppermute x32, waiting for transfers between devices: 366 us -> 322 us  [shift(): return lax.ppermute(block, 'fsdp', [(i, (i + k) % F) for i in range(F)])]
    all_to_all x7, waiting for transfers between devices: 55.6 us -> 93.8 us  [exchange(): return lax.all_to_all(blocks, 'ctx', 0, 0, tiled=True)]
    pallas_call x0 -> x1, Pallas kernels: none -> 16.1 us  [input_back(): pl.pallas_call(input_back_kernel, grid=(nseq,), in_specs=[pl.BlockSpec((t...]
    dot_general x3 -> x1, matrix products: 16.5 us -> 3.75 us  [mm_nt(): lax.dot_general(a, b, (((1,), (1,)), ((), ())), preferred_element_type=F32)]
  transfers between devices with their start and end apart: 50 -> 49, of which waited for: 23 -> 23; matrix products, arithmetic and copies ran while one was open for 12% -> 13% of each run, Pallas kernels for 18% -> 20%
where the time goes in v3:
time: 953 us; the launch traced here: 946 us
  waiting for transfers between devices  474 us (50%)
  Pallas kernels  199 us (21%)
  starting transfers between devices  91.6 us (10%)
  matrix products  63.3 us (7%)
  local copies, waits for them, and re-layouts  56.7 us (6%)
  other arithmetic  46.6 us (5%)
  between operations  15.6 us (2%)
    ppermute x32, waiting for transfers between devices, shift(): return lax.ppermute(block, 'fsdp', [(i, (i + k) % F) for i in range(F)])  322 us
    pallas_call x2, Pallas kernels, run_expert(): pl.pallas_call(lambda *refs: expert_kernel(sides, w_mode, g_mode, *refs),...  104 us
    all_to_all x7, waiting for transfers between devices, exchange(): return lax.all_to_all(blocks, 'ctx', 0, 0, tiled=True)  93.8 us
    ppermute x32, starting transfers between devices, shift(): return lax.ppermute(block, 'fsdp', [(i, (i + k) % F) for i in range(F)])  53.4 us
    ppermute x4, waiting for transfers between devices, swap(): return lax.ppermute(block, 'fsdp', [(i, i ^ 1) for i in range(F)])  40.4 us
    dot_general x10, matrix products, mm_tn(): lax.dot_general(a, b, (((0,), (0,)), ((), ())), preferred_element_type=F32)  34.3 us
    all_to_all x7, starting transfers between devices, exchange(): return lax.all_to_all(blocks, 'ctx', 0, 0, tiled=True)  33.1 us
    pallas_call x1, Pallas kernels, attention_back(): pl.pallas_call(lambda *refs: attend_back_kernel(groups, *refs), grid_spec...  27.6 us
  transfers between devices with their start and end apart: 49, of which 23 were waited for; matrix products, arithmetic and copies ran while one was open for 13% of the time, Pallas kernels for 20%

profile of v3, /device:TPU:0, one launch (start us, length us, event | category | flops | bytes accessed | tf_op | source)
XLA Modules:
  0.0 946.1 jit_solution(13897122521240318720)
XLA Ops:
  11.1 5.0 collective-permute-start.1
  17.2 4.3 collective-permute-done.1
  21.5 11.3 %collective-permute-done.2 = bf16[48,2048]{1,0:T(8,128)(2,1)S(1)} collective-permute-done((bf16[48,2048]{1,0:T(8,128)(2,1)S(1)}, bf16[48,2048]{1,0:T(8,128)(2,1)S(1)}, u32[]{:S(2)}, u32[]{:S(2)}) %collective-permute-start.2) | collective-permute-done | bytes 196640 | tf_op jit(solution)/shard_map/ppermute | solution.py:594
  49.2 3.8 collective-permute-start.4
  57.8 20.2 %collective-permute-done.8 = bf16[2,384]{1,0:T(2,128)(2,1)S(1)} collective-permute-done((bf16[2,384]{1,0:T(2,128)(2,1)S(1)}, bf16[2,384]{1,0:T(2,128)(2,1)S(1)}, u32[]{:S(2)}, u32[]{:S(2)}) %collective-permute-start.8) | collective-permute-done | bytes 1568 | tf_op jit(solution)/shard_map/ppermute | solution.py:594
  78.0 4.1 collective-permute-start.5
  87.0 5.4 collective-permute-done.5
  93.4 4.8 shard_map.212
  103.4 4.3 fusion.refs_1_
  107.7 31.7 %collective-permute-done.7.refs_9_ = bf16[576,1536]{1,0:T(8,128)(2,1)} collective-permute-done((bf16[576,1536]{1,0:T(8,128)(2,1)}, bf16[576,1536]{1,0:T(8,128)(2,1)}, u32[]{:S(2)}, u32[]{:S(2)}) %collective-permute-start.7) | collective-permute-done | bytes 1769504 | tf_op jit(solution)/shard_map/ppermute | solution.py:594
  146.5 21.2 %shard_map.213 = (bf16[4,128,1536]{2,1,0:T(8,128)(2,1)}, f32[4,2,128,128]{3,2,1,0:T(8,128)}, bf16[4,128,1536]{2,1,0:T(8,128)(2,1)}) custom-call(s32[5]{0:T(128)} %pad_add_fusion.refs_0_, f32[4,128,1536]{2,1,0:T(8,128)} %fusion.refs_1_, bf16[4,1024,512]{2,1,0:T(8,128)(2,1)} %all-gather.9.cloned.1.call-done.refs_2_, ...), custom_call_target="tpu_custom_call" | custom-call | flops 22548578304 | bytes 10485760 | tf_op jit(solution)/shard_map/pallas_call | solution.py:156
  170.9 7.3 all-gather.11.cloned.1.call-done
  178.2 5.2 multiply_reduce_fusion.2
  186.3 6.8 convolution_convert_fusion.1
  193.1 4.9 all-to-all-start
  205.0 78.8 %collective-permute-done.13.refs_7_ = bf16[192,1536]{1,0:T(8,128)(2,1)} collective-permute-done((bf16[192,1536]{1,0:T(8,128)(2,1)}, bf16[192,1536]{1,0:T(8,128)(2,1)}, u32[]{:S(2)}, u32[]{:S(2)}) %collective-permute-start.13) | collective-permute-done | bytes 589856 | tf_op jit(solution)/shard_map/ppermute | solution.py:594
  283.8 12.0 %collective-permute-done.14.refs_8_ = bf16[192,1536]{1,0:T(8,128)(2,1)} collective-permute-done((bf16[192,1536]{1,0:T(8,128)(2,1)}, bf16[192,1536]{1,0:T(8,128)(2,1)}, u32[]{:S(2)}, u32[]{:S(2)}) %collective-permute-start.14) | collective-permute-done | bytes 589856 | tf_op jit(solution)/shard_map/ppermute | solution.py:594
  296.9 8.7 convolution_convert_fusion
  305.7 4.9 all-to-all-start.1
  315.5 101.4 %collective-permute-done.18.refs_6_ = bf16[192,1536]{1,0:T(8,128)(2,1)S(1)} collective-permute-done((bf16[192,1536]{1,0:T(8,128)(2,1)}, bf16[192,1536]{1,0:T(8,128)(2,1)S(1)}, u32[]{:S(2)}, u32[]{:S(2)}) %collective-permute-start.18) | collective-permute-done | bytes 589856 | tf_op jit(solution)/shard_map/ppermute | solution.py:594
  422.7 52.7 %shard_map.215 = (bf16[8,2,80,1536]{3,2,1,0:T(8,128)(2,1)}, bf16[8,2,80,1664]{3,2,1,0:T(8,128)(2,1)}, bf16[576,1536]{1,0:T(8,128)(2,1)}, bf16[576,1536]{1,0:T(8,...) custom-call(s32[3]{0:T(128)} %get-tuple-element.304.refs_0_, ...), custom_call_target="tpu_custom_call" | custom-call | flops 57378078720 | bytes 44040192 | tf_op jit(solution)/shard_map/pallas_call | solution.py:511
  477.7 4.5 all-to-all-start.2
  482.3 51.2 %shard_map.216 = (bf16[8,2,80,1536]{3,2,1,0:T(8,128)(2,1)}, bf16[8,2,80,1664]{3,2,1,0:T(8,128)(2,1)}, bf16[576,1536]{1,0:T(8,128)(2,1)}, bf16[576,1536]{1,0:T(8,...) custom-call(s32[3]{0:T(128)} %get-tuple-element.305.refs_0_, ...), custom_call_target="tpu_custom_call" | custom-call | flops 57378078720 | bytes 44040192 | tf_op jit(solution)/shard_map/pallas_call | solution.py:511
  533.5 9.1 collective-permute-done.22
  543.8 4.5 all-to-all-start.3
  548.6 46.1 %all-to-all-done.3 = bf16[8,2,80,1536]{3,2,1,0:T(8,128)(2,1)} async-done(((bf16[8,2,80,1536]{3,2,1,0:T(8,128)(2,1)}), bf16[8,2,80,1536]{3,2,1,0:T(8,128)(2,1)}, u32[]{:S(2)}, u32[]{:S(2)}) %all-to-all-start.3) | async-done | bytes 3932192 | tf_op jit(solution)/shard_map/all_to_all | solution.py:612
  597.7 4.2 fusion.11
  603.1 4.6 all-to-all-start.4
  610.9 37.2 %collective-permute-done.25 = bf16[512,1536]{1,0:T(8,128)(2,1)} collective-permute-done((bf16[512,1536]{1,0:T(8,128)(2,1)}, bf16[512,1536]{1,0:T(8,128)(2,1)}, u32[]{:S(2)}, u32[]{:S(2)}) %collective-permute-start.25) | collective-permute-done | bytes 1572896 | tf_op jit(solution)/shard_map/ppermute | solution.py:609
  656.9 3.7 convolution_convert_fusion.2
  660.6 5.0 all-to-all-start.5
  665.9 27.6 %shard_map.217 = (bf16[4,128,1536]{2,1,0:T(8,128)(2,1)}, bf16[8,4,128,512]{3,2,1,0:T(8,128)(2,1)}) custom-call(s32[5]{0:T(128)} %pad_add_fusion.refs_0_, bf16[4,128,1536]{2,1,0:T(8,128)(2,1)} %get-tuple-element.213.refs_1_, bf16[4,1024,512]{2,1,0:T(8,128)(2,1)} %all-gather.9.cloned.1.call-done.refs_2_, bf16[4,128,1536]{2,1,0:T(8,128)(2,1)} %bitcast.291, ...), custom_call_target="tpu_custom_call" | custom-call | flops 28991029248 | bytes 17825792 | tf_op jit(solution)/shard_map/pallas_call | solution.py:191
  696.5 24.9 %shard_map.218 = bf16[1536,3584]{1,0:T(8,128)(2,1)} custom-call(bf16[512,1536]{1,0:T(8,128)(2,1)} %bitcast.288, bf16[512,1536]{1,0:T(8,128)(2,1)} %copy-done.23, bf16[512,1536]{1,0:T(8,128)(2,1)} %fusion.7.x_ref.refs_2_, bf16[512,1536]{1,0:T(8,128)(2,1)} %bitcast.289, bf16[4096,1536]{1,0:T(8,128)(2,1)} %all-gather.13.cloned.1.call-done.refs_4_, ...), custom_call_target="tpu_custom_call" | custom-call | flops 22548578304 | bytes 12582912 | tf_op jit(solution)/shard_map/pallas_call | solution.py:402
  722.5 4.6 all-to-all-start.6
  728.1 3.8 fusion.22
  731.9 5.3 fusion.3
  742.9 4.4 convert_add_fusion.4
  747.2 5.0 fusion.19
  752.2 47.7 %all-to-all-done.6.terms_ref = bf16[8,4,128,512]{3,2,1,0:T(8,128)(2,1)} async-done(((bf16[8,4,128,512]{3,2,1,0:T(8,128)(2,1)}), bf16[8,4,128,512]{3,2,1,0:T(8,128)(2,1)}, u32[]{:S(2)}, u32[]{:S(2)}) %all-to-all-start.6) | async-done | bytes 4194336 | tf_op jit(solution)/shard_map/all_to_all | solution.py:612
  804.0 6.3 bitcast_add_fusion
  810.3 16.1 %shard_map.219 = (f32[512,1536]{1,0:T(8,128)}, f32[1,1536]{1,0:T(1,128)}) custom-call(bf16[512,1536]{1,0:T(8,128)(2,1)} %bitcast.290, bf16[8,4,128,512]{3,2,1,0:T(8,128)(2,1)} %all-to-all-done.6.terms_ref, bf16[1536,2048]{1,0:T(8,128)(2,1)} %bitcast.258, bf16[512,1536]{1,0:T(8,128)(2,1)} %bitcast.251, f32[512,1]{1,0:T(8,128)} %copy.67.inverse_ref, ...), custom_call_target="tpu_custom_call" | custom-call | flops 12884901888 | bytes 12582912 | tf_op jit(solution)/shard_map/pallas_call | solution.py:450
  827.1 17.4 %collective-permute-done.31 = bf16[576,1536]{1,0:T(8,128)(2,1)} collective-permute-done((bf16[576,1536]{1,0:T(8,128)(2,1)}, bf16[576,1536]{1,0:T(8,128)(2,1)}, u32[]{:S(2)}, u32[]{:S(2)}) %collective-permute-start.31) | collective-permute-done | bytes 1769504 | tf_op jit(solution)/shard_map/ppermute | solution.py:594
  852.4 7.0 collective-permute-done.32
  859.3 12.9 %collective-permute-done.33 = bf16[48,3712]{1,0:T(8,128)(2,1)S(1)} collective-permute-done((bf16[48,3712]{1,0:T(8,128)(2,1)S(1)}, bf16[48,3712]{1,0:T(8,128)(2,1)S(1)}, u32[]{:S(2)}, u32[]{:S(2)}) %collective-permute-start.33) | collective-permute-done | bytes 356384 | tf_op jit(solution)/shard_map/ppermute | solution.py:594
  883.9 6.9 collective-permute-start.35
  899.5 9.9 %all-gather.15.cloned.1.call-done = bf16[384,3712]{1,0:T(8,128)(2,1)} async-done(((bf16[48,3712]{1,0:T(8,128)(2,1)}), bf16[384,3712]{1,0:T(8,128)(2,1)}) %all-gather.15.cloned.1.call-update) | async-done | bytes 2850832 | tf_op jit(solution)/shard_map/all_gather | solution.py:875
  918.6 4.9 fusion.100
  923.5 6.1 collective-permute-done.35
  (304 shorter events, 150.6 us)
Async XLA Ops:
  7.2 86.2 %all-gather.7.cloned.1.call-start = ((), (), s32[]{:S(2)}) async-start(), calls=%async_computation.8 | async-start | bytes 7077888 | tf_op jit(solution)/shard_map/all_gather | solution.py:615
  11.1 10.4 %collective-permute-start.1 = (bf16[48,2048]{1,0:T(8,128)(2,1)S(1)}, bf16[48,2048]{1,0:T(8,128)(2,1)S(1)}, u32[]{:S(2)}, u32[]{:S(2)}) collective-permute-start(bf16[48,2048]{1,0:T(8,128)(2,1)S(1)} %constant_dynamic-update-slice_fusion), channel_id=1, source_target_pairs={{0,3},{1,0},{2,1},{3,2},{4,7},{5,4},{6,5},{7,6},{8,11},{9,8},{10,9... | collective-permute-start | bytes 589832 | tf_op jit(solution)/shard_map/ppermute | solution.py:594
  16.2 16.7 %collective-permute-start.2 = (bf16[48,2048]{1,0:T(8,128)(2,1)S(1)}, bf16[48,2048]{1,0:T(8,128)(2,1)S(1)}, u32[]{:S(2)}, u32[]{:S(2)}) collective-permute-start(bf16[48,2048]{1,0:T(8,128)(2,1)S(1)} %constant_dynamic-update-slice_fusion), channel_id=1, source_target_pairs={{0,2},{1,3},{2,0},{3,1},{4,6},{5,7},{6,4},{7,5},{8,10},{9,11},{10,... | collective-permute-start | bytes 589832 | tf_op jit(solution)/shard_map/ppermute | solution.py:594
  16.2 16.7 %collective-permute-start.3 = (bf16[48,2048]{1,0:T(8,128)(2,1)S(1)}, bf16[48,2048]{1,0:T(8,128)(2,1)S(1)}, u32[]{:S(2)}, u32[]{:S(2)}) collective-permute-start(bf16[48,2048]{1,0:T(8,128)(2,1)S(1)} %constant_dynamic-update-slice_fusion), channel_id=1, source_target_pairs={{0,1},{1,2},{2,3},{3,0},{4,5},{5,6},{6,7},{7,4},{8,9},{9,10},{10,1... | collective-permute-start | bytes 589832 | tf_op jit(solution)/shard_map/ppermute | solution.py:594
  34.0 105.4 %all-gather.9.cloned.1.call-start = ((), (), s32[]{:S(2)}) async-start(), calls=%async_computation.9 | async-start | bytes 4718592 | tf_op jit(solution)/shard_map/all_gather | solution.py:714
  37.9 55.5 %collective-permute-start = (bf16[576,1536]{1,0:T(8,128)(2,1)}, bf16[576,1536]{1,0:T(8,128)(2,1)}, u32[]{:S(2)}, u32[]{:S(2)}) collective-permute-start(bf16[576,1536]{1,0:T(8,128)(2,1)} %pad_maximum_fusion), channel_id=1, source_target_pairs={{0,1},{1,2},{2,3},{3,0},{4,5},{5,6},{6,7},{7,4},{8,9},{9,10},{10,1... | collective-permute-start | bytes 5308424 | tf_op jit(solution)/shard_map/ppermute | solution.py:594
  45.2 32.8 %collective-permute-start.8 = (bf16[2,384]{1,0:T(2,128)(2,1)S(1)}, bf16[2,384]{1,0:T(2,128)(2,1)S(1)}, u32[]{:S(2)}, u32[]{:S(2)}) collective-permute-start(bf16[2,384]{1,0:T(2,128)(2,1)S(1)} %pad_maximum_fusion.8), channel_id=1, source_target_pairs={{0,3},{1,0},{2,1},{3,2},{4,7},{5,4},{6,5},{7,6},{8,11},{9,8},{10,9... | collective-permute-start | bytes 4616 | tf_op jit(solution)/shard_map/ppermute | solution.py:594
  48.2 33.9 %collective-permute-start.9 = (bf16[2,384]{1,0:T(2,128)(2,1)S(1)}, bf16[2,384]{1,0:T(2,128)(2,1)S(1)}, u32[]{:S(2)}, u32[]{:S(2)}) collective-permute-start(bf16[2,384]{1,0:T(2,128)(2,1)S(1)} %pad_maximum_fusion.8), channel_id=1, source_target_pairs={{0,2},{1,3},{2,0},{3,1},{4,6},{5,7},{6,4},{7,5},{8,10},{9,11},{10,... | collective-permute-start | bytes 4616 | tf_op jit(solution)/shard_map/ppermute | solution.py:594
  49.2 35.6 %collective-permute-start.10 = (bf16[2,384]{1,0:T(2,128)(2,1)S(1)}, bf16[2,384]{1,0:T(2,128)(2,1)S(1)}, u32[]{:S(2)}, u32[]{:S(2)}) collective-permute-start(bf16[2,384]{1,0:T(2,128)(2,1)S(1)} %pad_maximum_fusion.8), channel_id=1, source_target_pairs={{0,1},{1,2},{2,3},{3,0},{4,5},{5,6},{6,7},{7,4},{8,9},{9,10},{10,1... | collective-permute-start | bytes 4616 | tf_op jit(solution)/shard_map/ppermute | solution.py:594
  49.2 37.8 %collective-permute-start.4 = (bf16[48,1536]{1,0:T(8,128)(2,1)S(1)}, bf16[48,1536]{1,0:T(8,128)(2,1)S(1)}, u32[]{:S(2)}, u32[]{:S(2)}) collective-permute-start(bf16[48,1536]{1,0:T(8,128)(2,1)S(1)} %constant_dynamic-slice_fusion.3), channel_id=1, source_target_pairs={{0,3},{1,0},{2,1},{3,2},{4,7},{5,4},{6,5},{7,6},{8,11},{9,8},{10,9... | collective-permute-start | bytes 442376 | tf_op jit(solution)/shard_map/ppermute | solution.py:594
  78.0 14.4 %collective-permute-start.5 = (bf16[48,1536]{1,0:T(8,128)(2,1)S(1)}, bf16[48,1536]{1,0:T(8,128)(2,1)S(1)}, u32[]{:S(2)}, u32[]{:S(2)}) collective-permute-start(bf16[48,1536]{1,0:T(8,128)(2,1)S(1)} %constant_dynamic-slice_fusion.3), channel_id=1, source_target_pairs={{0,2},{1,3},{2,0},{3,1},{4,6},{5,7},{6,4},{7,5},{8,10},{9,11},{10,... | collective-permute-start | bytes 442376 | tf_op jit(solution)/shard_map/ppermute | solution.py:594
  98.2 80.0 %all-gather.11.cloned.1.call-start = ((), (), s32[]{:S(2)}) async-start(), calls=%async_computation.10 | async-start | bytes 5308416 | tf_op jit(solution)/shard_map/all_gather | solution.py:615
  98.2 41.2 %collective-permute-start.7 = (bf16[576,1536]{1,0:T(8,128)(2,1)}, bf16[576,1536]{1,0:T(8,128)(2,1)}, u32[]{:S(2)}, u32[]{:S(2)}) collective-permute-start(bf16[576,1536]{1,0:T(8,128)(2,1)} %pad_maximum_fusion), channel_id=1, source_target_pairs={{0,3},{1,0},{2,1},{3,2},{4,7},{5,4},{6,5},{7,6},{8,11},{9,8},{10,9... | collective-permute-start | bytes 5308424 | tf_op jit(solution)/shard_map/ppermute | solution.py:594
  143.8 27.1 %collective-permute-start.11 = (bf16[192,1536]{1,0:T(8,128)(2,1)S(1)}, bf16[192,1536]{1,0:T(8,128)(2,1)}, u32[]{:S(2)}, u32[]{:S(2)}) collective-permute-start(bf16[192,1536]{1,0:T(8,128)(2,1)S(1)} %get-tuple-element.152), channel_id=1, source_target_pairs={{0,2},{1,3},{2,0},{3,1},{4,6},{5,7},{6,4},{7,5},{8,10},{9,11},{10,... | collective-permute-start | bytes 1769480 | tf_op jit(solution)/shard_map/ppermute | solution.py:594
  143.8 23.9 %collective-permute-start.12 = (bf16[512,128]{1,0:T(8,128)(2,1)S(1)}, bf16[512,128]{1,0:T(8,128)(2,1)S(1)}, u32[]{:S(2)}, u32[]{:S(2)}) collective-permute-start(bf16[512,128]{1,0:T(8,128)(2,1)S(1)} %pad_maximum_fusion.5), channel_id=1, source_target_pairs={{0,1},{1,0},{2,3},{3,2},{4,5},{5,4},{6,7},{7,6},{8,9},{9,8},{10,11... | collective-permute-start | bytes 393224 | tf_op jit(solution)/shard_map/ppermute | solution.py:609
  193.1 103.7 %all-to-all-start = ((bf16[8,2,80,3200]{3,2,1,0:T(8,128)(2,1)}), bf16[8,2,80,3200]{3,2,1,0:T(8,128)(2,1)}, u32[]{:S(2)}, u32[]{:S(2)}) async-start(bf16[8,2,80,3200]{3,2,1,0:T(8,128)(2,1)} %bitcast.253), calls=%async_computation | async-start | bytes 16384000 | tf_op jit(solution)/shard_map/all_to_all | solution.py:612
  198.0 98.8 %collective-permute-start.15 = (bf16[512,3200]{1,0:T(8,128)(2,1)}, bf16[512,3200]{1,0:T(8,128)(2,1)}, u32[]{:S(2)}, u32[]{:S(2)}) collective-permute-start(bf16[512,3200]{1,0:T(8,128)(2,1)} %copy-done.25), channel_id=1, source_target_pairs={{0,1},{1,0},{2,3},{3,2},{4,5},{5,4},{6,7},{7,6},{8,9},{9,8},{10,11... | collective-permute-start | bytes 9830408 | tf_op jit(solution)/shard_map/ppermute | solution.py:609
  201.5 82.3 %collective-permute-start.13 = (bf16[192,1536]{1,0:T(8,128)(2,1)}, bf16[192,1536]{1,0:T(8,128)(2,1)}, u32[]{:S(2)}, u32[]{:S(2)}) collective-permute-start(bf16[192,1536]{1,0:T(8,128)(2,1)} %get-tuple-element.162), channel_id=1, source_target_pairs={{0,2},{1,3},{2,0},{3,1},{4,6},{5,7},{6,4},{7,5},{8,10},{9,11},{10,... | collective-permute-start | bytes 1769480 | tf_op jit(solution)/shard_map/ppermute | solution.py:594
  203.9 91.9 %collective-permute-start.14 = (bf16[192,1536]{1,0:T(8,128)(2,1)}, bf16[192,1536]{1,0:T(8,128)(2,1)}, u32[]{:S(2)}, u32[]{:S(2)}) collective-permute-start(bf16[192,1536]{1,0:T(8,128)(2,1)} %get-tuple-element.163), channel_id=1, source_target_pairs={{0,2},{1,3},{2,0},{3,1},{4,6},{5,7},{6,4},{7,5},{8,10},{9,11},{10,... | collective-permute-start | bytes 1769480 | tf_op jit(solution)/shard_map/ppermute | solution.py:594
  305.7 113.4 %all-to-all-start.1 = ((bf16[8,2,80,3200]{3,2,1,0:T(8,128)(2,1)}), bf16[8,2,80,3200]{3,2,1,0:T(8,128)(2,1)}, u32[]{:S(2)}, u32[]{:S(2)}) async-start(bf16[8,2,80,3200]{3,2,1,0:T(8,128)(2,1)} %bitcast.254), calls=%async_computation.1 | async-start | bytes 16384000 | tf_op jit(solution)/shard_map/all_to_all | solution.py:612
  310.6 232.0 %all-gather.13.cloned.1.call-start = ((), (), s32[]{:S(2)}) async-start(), calls=%async_computation.11 | async-start | bytes 14155776 | tf_op jit(solution)/shard_map/all_gather | solution.py:759
  311.1 105.9 %collective-permute-start.16 = (bf16[576,1536]{1,0:T(8,128)(2,1)S(1)}, bf16[576,1536]{1,0:T(8,128)(2,1)S(1)}, u32[]{:S(2)}, u32[]{:S(2)}) collective-permute-start(bf16[576,1536]{1,0:T(8,128)(2,1)S(1)} %pad_maximum_fusion.1), channel_id=1, source_target_pairs={{0,1},{1,2},{2,3},{3,0},{4,5},{5,6},{6,7},{7,4},{8,9},{9,10},{10,1... | collective-permute-start | bytes 5308424 | tf_op jit(solution)/shard_map/ppermute | solution.py:594
  313.5 105.6 %collective-permute-start.17 = (bf16[576,1536]{1,0:T(8,128)(2,1)S(1)}, bf16[576,1536]{1,0:T(8,128)(2,1)}, u32[]{:S(2)}, u32[]{:S(2)}) collective-permute-start(bf16[576,1536]{1,0:T(8,128)(2,1)S(1)} %pad_maximum_fusion.1), channel_id=1, source_target_pairs={{0,3},{1,0},{2,1},{3,2},{4,7},{5,4},{6,5},{7,6},{8,11},{9,8},{10,9... | collective-permute-start | bytes 5308424 | tf_op jit(solution)/shard_map/ppermute | solution.py:594
  314.9 102.0 %collective-permute-start.18 = (bf16[192,1536]{1,0:T(8,128)(2,1)}, bf16[192,1536]{1,0:T(8,128)(2,1)S(1)}, u32[]{:S(2)}, u32[]{:S(2)}) collective-permute-start(bf16[192,1536]{1,0:T(8,128)(2,1)} %get-tuple-element.172), channel_id=1, source_target_pairs={{0,2},{1,3},{2,0},{3,1},{4,6},{5,7},{6,4},{7,5},{8,10},{9,11},{10,... | collective-permute-start | bytes 1769480 | tf_op jit(solution)/shard_map/ppermute | solution.py:594
  419.7 55.6 %collective-permute-start.19 = (bf16[192,1536]{1,0:T(8,128)(2,1)}, bf16[192,1536]{1,0:T(8,128)(2,1)S(1)}, u32[]{:S(2)}, u32[]{:S(2)}) collective-permute-start(bf16[192,1536]{1,0:T(8,128)(2,1)} %get-tuple-element.175), channel_id=1, source_target_pairs={{0,2},{1,3},{2,0},{3,1},{4,6},{5,7},{6,4},{7,5},{8,10},{9,11},{10,... | collective-permute-start | bytes 1769480 | tf_op jit(solution)/shard_map/ppermute | solution.py:594
  419.8 55.6 %collective-permute-start.20 = (bf16[192,1536]{1,0:T(8,128)(2,1)}, bf16[192,1536]{1,0:T(8,128)(2,1)S(1)}, u32[]{:S(2)}, u32[]{:S(2)}) collective-permute-start(bf16[192,1536]{1,0:T(8,128)(2,1)} %get-tuple-element.176), channel_id=1, source_target_pairs={{0,2},{1,3},{2,0},{3,1},{4,6},{5,7},{6,4},{7,5},{8,10},{9,11},{10,... | collective-permute-start | bytes 1769480 | tf_op jit(solution)/shard_map/ppermute | solution.py:594
  476.4 66.2 %collective-permute-start.21 = (bf16[576,1536]{1,0:T(8,128)(2,1)}, bf16[576,1536]{1,0:T(8,128)(2,1)S(1)}, u32[]{:S(2)}, u32[]{:S(2)}) collective-permute-start(bf16[576,1536]{1,0:T(8,128)(2,1)} %get-tuple-element.188), channel_id=1, source_target_pairs={{0,1},{1,2},{2,3},{3,0},{4,5},{5,6},{6,7},{7,4},{8,9},{9,10},{10,1... | collective-permute-start | bytes 5308424 | tf_op jit(solution)/shard_map/ppermute | solution.py:594
  476.4 66.2 %collective-permute-start.22 = (bf16[192,1536]{1,0:T(8,128)(2,1)}, bf16[192,1536]{1,0:T(8,128)(2,1)}, u32[]{:S(2)}, u32[]{:S(2)}) collective-permute-start(bf16[192,1536]{1,0:T(8,128)(2,1)} %get-tuple-element.189), channel_id=1, source_target_pairs={{0,2},{1,3},{2,0},{3,1},{4,6},{5,7},{6,4},{7,5},{8,10},{9,11},{10,... | collective-permute-start | bytes 1769480 | tf_op jit(solution)/shard_map/ppermute | solution.py:594
  477.7 64.9 %all-to-all-start.2 = ((bf16[8,2,80,1536]{3,2,1,0:T(8,128)(2,1)}), bf16[8,2,80,1536]{3,2,1,0:T(8,128)(2,1)}, u32[]{:S(2)}, u32[]{:S(2)}) async-start(bf16[8,2,80,1536]{3,2,1,0:T(8,128)(2,1)} %get-tuple-element.197), calls=%async_computation.2 | async-start | bytes 7864320 | tf_op jit(solution)/shard_map/all_to_all | solution.py:612
  543.8 50.9 %all-to-all-start.3 = ((bf16[8,2,80,1536]{3,2,1,0:T(8,128)(2,1)}), bf16[8,2,80,1536]{3,2,1,0:T(8,128)(2,1)}, u32[]{:S(2)}, u32[]{:S(2)}) async-start(bf16[8,2,80,1536]{3,2,1,0:T(8,128)(2,1)} %get-tuple-element.203), calls=%async_computation.3 | async-start | bytes 7864320 | tf_op jit(solution)/shard_map/all_to_all | solution.py:612
  548.4 53.5 %collective-permute-start.23 = (bf16[576,1536]{1,0:T(8,128)(2,1)}, bf16[576,1536]{1,0:T(8,128)(2,1)S(1)}, u32[]{:S(2)}, u32[]{:S(2)}) collective-permute-start(bf16[576,1536]{1,0:T(8,128)(2,1)} %get-tuple-element.201), channel_id=1, source_target_pairs={{0,3},{1,0},{2,1},{3,2},{4,7},{5,4},{6,5},{7,6},{8,11},{9,8},{10,9... | collective-permute-start | bytes 5308424 | tf_op jit(solution)/shard_map/ppermute | solution.py:594
  601.9 46.2 %collective-permute-start.25 = (bf16[512,1536]{1,0:T(8,128)(2,1)}, bf16[512,1536]{1,0:T(8,128)(2,1)}, u32[]{:S(2)}, u32[]{:S(2)}) collective-permute-start(bf16[512,1536]{1,0:T(8,128)(2,1)} %fusion.11), channel_id=1, source_target_pairs={{0,1},{1,0},{2,3},{3,2},{4,5},{5,4},{6,7},{7,6},{8,9},{9,8},{10,11... | collective-permute-start | bytes 4718600 | tf_op jit(solution)/shard_map/ppermute | solution.py:609
  603.1 57.5 %all-to-all-start.4 = ((bf16[8,2,80,1664]{3,2,1,0:T(8,128)(2,1)}), bf16[8,2,80,1664]{3,2,1,0:T(8,128)(2,1)}, u32[]{:S(2)}, u32[]{:S(2)}) async-start(bf16[8,2,80,1664]{3,2,1,0:T(8,128)(2,1)} %get-tuple-element.209), calls=%async_computation.4 | async-start | bytes 8519680 | tf_op jit(solution)/shard_map/all_to_all | solution.py:612
  607.7 43.9 %collective-permute-start.24 = (bf16[192,1536]{1,0:T(8,128)(2,1)}, bf16[192,1536]{1,0:T(8,128)(2,1)}, u32[]{:S(2)}, u32[]{:S(2)}) collective-permute-start(bf16[192,1536]{1,0:T(8,128)(2,1)} %get-tuple-element.206), channel_id=1, source_target_pairs={{0,2},{1,3},{2,0},{3,1},{4,6},{5,7},{6,4},{7,5},{8,10},{9,11},{10,... | collective-permute-start | bytes 1769480 | tf_op jit(solution)/shard_map/ppermute | solution.py:594
  660.6 32.9 %collective-permute-start.26 = (bf16[192,1536]{1,0:T(8,128)(2,1)}, bf16[192,1536]{1,0:T(8,128)(2,1)}, u32[]{:S(2)}, u32[]{:S(2)}) collective-permute-start(bf16[192,1536]{1,0:T(8,128)(2,1)} %get-tuple-element.212), channel_id=1, source_target_pairs={{0,2},{1,3},{2,0},{3,1},{4,6},{5,7},{6,4},{7,5},{8,10},{9,11},{10,... | collective-permute-start | bytes 1769480 | tf_op jit(solution)/shard_map/ppermute | solution.py:594
  660.6 61.9 %all-to-all-start.5 = ((bf16[8,2,80,1664]{3,2,1,0:T(8,128)(2,1)}), bf16[8,2,80,1664]{3,2,1,0:T(8,128)(2,1)}, u32[]{:S(2)}, u32[]{:S(2)}) async-start(bf16[8,2,80,1664]{3,2,1,0:T(8,128)(2,1)} %get-tuple-element.226), calls=%async_computation.5 | async-start | bytes 8519680 | tf_op jit(solution)/shard_map/all_to_all | solution.py:612
  665.6 179.1 %reduce-scatter.2.cloned.1.call-start = ((), (), s32[]{:S(2)}) async-start(), calls=%async_computation.12 | async-start | bytes 12386304 | tf_op jit(solution)/shard_map/reduce_scatter | solution.py:818
  693.5 29.0 %collective-permute-start.27 = (bf16[192,1536]{1,0:T(8,128)(2,1)}, bf16[192,1536]{1,0:T(8,128)(2,1)}, u32[]{:S(2)}, u32[]{:S(2)}) collective-permute-start(bf16[192,1536]{1,0:T(8,128)(2,1)} %get-tuple-element.221), channel_id=1, source_target_pairs={{0,2},{1,3},{2,0},{3,1},{4,6},{5,7},{6,4},{7,5},{8,10},{9,11},{10,... | collective-permute-start | bytes 1769480 | tf_op jit(solution)/shard_map/ppermute | solution.py:594
  722.5 77.3 %all-to-all-start.6 = ((bf16[8,4,128,512]{3,2,1,0:T(8,128)(2,1)}), bf16[8,4,128,512]{3,2,1,0:T(8,128)(2,1)}, u32[]{:S(2)}, u32[]{:S(2)}) async-start(bf16[8,4,128,512]{3,2,1,0:T(8,128)(2,1)} %get-tuple-element.224), calls=%async_computation.6 | async-start | bytes 8388608 | tf_op jit(solution)/shard_map/all_to_all | solution.py:612
  727.1 182.3 %all-gather.15.cloned.1.call-start = ((), (), s32[]{:S(2)}) async-start(), calls=%async_computation.13 | async-start | bytes 3207168 | tf_op jit(solution)/shard_map/all_gather | solution.py:875
  737.1 65.0 %collective-permute-start.30 = (bf16[512,1664]{1,0:T(8,128)(2,1)}, bf16[512,1664]{1,0:T(8,128)(2,1)}, u32[]{:S(2)}, u32[]{:S(2)}) collective-permute-start(bf16[512,1664]{1,0:T(8,128)(2,1)} %fusion.3), channel_id=1, source_target_pairs={{0,1},{1,0},{2,3},{3,2},{4,5},{5,4},{6,7},{7,6},{8,9},{9,8},{10,11... | collective-permute-start | bytes 5111816 | tf_op jit(solution)/shard_map/ppermute | solution.py:609
  739.7 60.2 %collective-permute-start.28 = (bf16[192,1536]{1,0:T(8,128)(2,1)}, bf16[192,1536]{1,0:T(8,128)(2,1)}, u32[]{:S(2)}, u32[]{:S(2)}) collective-permute-start(bf16[192,1536]{1,0:T(8,128)(2,1)} %get-tuple-element.229), channel_id=1, source_target_pairs={{0,2},{1,3},{2,0},{3,1},{4,6},{5,7},{6,4},{7,5},{8,10},{9,11},{10,... | collective-permute-start | bytes 1769480 | tf_op jit(solution)/shard_map/ppermute | solution.py:594
  742.8 57.1 %collective-permute-start.29 = (bf16[192,1536]{1,0:T(8,128)(2,1)}, bf16[192,1536]{1,0:T(8,128)(2,1)}, u32[]{:S(2)}, u32[]{:S(2)}) collective-permute-start(bf16[192,1536]{1,0:T(8,128)(2,1)} %get-tuple-element.230), channel_id=1, source_target_pairs={{0,2},{1,3},{2,0},{3,1},{4,6},{5,7},{6,4},{7,5},{8,10},{9,11},{10,... | collective-permute-start | bytes 1769480 | tf_op jit(solution)/shard_map/ppermute | solution.py:594
  802.2 42.4 %collective-permute-start.31 = (bf16[576,1536]{1,0:T(8,128)(2,1)}, bf16[576,1536]{1,0:T(8,128)(2,1)}, u32[]{:S(2)}, u32[]{:S(2)}) collective-permute-start(bf16[576,1536]{1,0:T(8,128)(2,1)} %get-tuple-element.236), channel_id=1, source_target_pairs={{0,1},{1,2},{2,3},{3,0},{4,5},{5,6},{6,7},{7,4},{8,9},{9,10},{10,1... | collective-permute-start | bytes 5308424 | tf_op jit(solution)/shard_map/ppermute | solution.py:594
  846.1 13.2 %collective-permute-start.32 = (bf16[48,3712]{1,0:T(8,128)(2,1)S(1)}, bf16[48,3712]{1,0:T(8,128)(2,1)S(1)}, u32[]{:S(2)}, u32[]{:S(2)}) collective-permute-start(bf16[48,3712]{1,0:T(8,128)(2,1)S(1)} %get-tuple-element.286), channel_id=1, source_target_pairs={{0,1},{1,2},{2,3},{3,0},{4,5},{5,6},{6,7},{7,4},{8,9},{9,10},{10,1... | collective-permute-start | bytes 1069064 | tf_op jit(solution)/shard_map/ppermute | solution.py:594
  846.3 26.0 %collective-permute-start.33 = (bf16[48,3712]{1,0:T(8,128)(2,1)S(1)}, bf16[48,3712]{1,0:T(8,128)(2,1)S(1)}, u32[]{:S(2)}, u32[]{:S(2)}) collective-permute-start(bf16[48,3712]{1,0:T(8,128)(2,1)S(1)} %get-tuple-element.287), channel_id=1, source_target_pairs={{0,2},{1,3},{2,0},{3,1},{4,6},{5,7},{6,4},{7,5},{8,10},{9,11},{10,... | collective-permute-start | bytes 1069064 | tf_op jit(solution)/shard_map/ppermute | solution.py:594
  847.7 24.6 %collective-permute-start.34 = (bf16[48,3712]{1,0:T(8,128)(2,1)S(1)}, bf16[48,3712]{1,0:T(8,128)(2,1)S(1)}, u32[]{:S(2)}, u32[]{:S(2)}) collective-permute-start(bf16[48,3712]{1,0:T(8,128)(2,1)S(1)} %get-tuple-element.288), channel_id=1, source_target_pairs={{0,3},{1,0},{2,1},{3,2},{4,7},{5,4},{6,5},{7,6},{8,11},{9,8},{10,9... | collective-permute-start | bytes 1069064 | tf_op jit(solution)/shard_map/ppermute | solution.py:594
  883.9 45.8 %collective-permute-start.35 = (bf16[576,1536]{1,0:T(8,128)(2,1)}, bf16[576,1536]{1,0:T(8,128)(2,1)}, u32[]{:S(2)}, u32[]{:S(2)}) collective-permute-start(bf16[576,1536]{1,0:T(8,128)(2,1)} %get-tuple-element.248), channel_id=1, source_target_pairs={{0,3},{1,0},{2,1},{3,2},{4,7},{5,4},{6,5},{7,6},{8,11},{9,8},{10,9... | collective-permute-start | bytes 5308424 | tf_op jit(solution)/shard_map/ppermute | solution.py:594
  (48 other events, 996.5 us)
Sparse Core Ops, SparseCore 0:
  34.1 45.9 all-gather.6
  98.3 35.3 all-gather.8
  139.5 38.6 all-gather.10
  419.3 74.5 all-gather.12
  722.6 106.7 reduce-scatter.1
  873.4 36.0 all-gather.14

commit v4 on v3

--- a/solution.py
+++ b/solution.py
@@ -858,9 +858,10 @@
     )
     first_grads = first_grads[0]
     if merged:
-        first_grads, mixed_sums[0] = step(["q1"], (first_grads, mixed_sums[0]), [])
         fill(role * mine, pair_sum(operands["p0"], "p2a", "p2b", "p2c"))
         fill((1 - role) * mine, pair_sum(messages["p1"], "p3"))
+        fill(role * mine + 1, pair_sum(operands["q0"], "q2a", "q2b", "q2c"))
+        first_grads, mixed_sums[0], shards = step(["q1"], (first_grads, mixed_sums[0], shards), [])
     gain_columns = jnp.stack([first_grads, second_grads]).reshape(2, F, Dl).transpose(1, 0, 2)
     gain_columns = gain_columns.reshape(F, cut, -1)
     gain_count = gain_columns.shape[2]
@@ -871,7 +872,6 @@
     if merged:
         wide, far = step([], (wide, far), ["q3"])
         mixed_rows = mixed_sums[0] + far.astype(F32)
-        fill(role * mine + 1, pair_sum(operands["q0"], "q2a", "q2b", "q2c"))
     wide = lax.all_gather(wide, "ctx", axis=0, tiled=False)
     whole = wide[:, :, : D + width + 2 * KV * HD].reshape(Dl, -1).astype(F32)
     grad_projection, grad_query = whole[:, :D], whole[:, D : D + width]

time: 953 us -> 950 us (level)
  waiting for transfers between devices: 474 us -> 463 us
    ppermute x32, waiting for transfers between devices: 322 us -> 306 us  [shift(): return lax.ppermute(block, 'fsdp', [(i, (i + k) % F) for i in range(F)])]
    all_gather x1, waiting for transfers between devices: 9.95 us -> 19.7 us  [local(): wide = lax.all_gather(wide, 'ctx', axis=0, tiled=False)]
  transfers between devices with their start and end apart: 49 -> 49, of which waited for: 23 -> 22; matrix products, arithmetic and copies ran while one was open for 13% -> 13% of each run, Pallas kernels for 20% -> 20%
where the time goes in v4:
time: 950 us; the launch traced here: 942 us
  waiting for transfers between devices  463 us (49%)
  Pallas kernels  198 us (21%)
  starting transfers between devices  93.3 us (10%)
  local copies, waits for them, and re-layouts  61.8 us (7%)
  matrix products  60.3 us (6%)
  other arithmetic  50.3 us (5%)
  between operations  15.6 us (2%)
    ppermute x32, waiting for transfers between devices, shift(): return lax.ppermute(block, 'fsdp', [(i, (i + k) % F) for i in range(F)])  306 us
    pallas_call x2, Pallas kernels, run_expert(): pl.pallas_call(lambda *refs: expert_kernel(sides, w_mode, g_mode, *refs),...  104 us
    all_to_all x7, waiting for transfers between devices, exchange(): return lax.all_to_all(blocks, 'ctx', 0, 0, tiled=True)  89.9 us
    ppermute x32, starting transfers between devices, shift(): return lax.ppermute(block, 'fsdp', [(i, (i + k) % F) for i in range(F)])  55.1 us
    ppermute x4, waiting for transfers between devices, swap(): return lax.ppermute(block, 'fsdp', [(i, i ^ 1) for i in range(F)])  40.4 us
    all_to_all x7, starting transfers between devices, exchange(): return lax.all_to_all(blocks, 'ctx', 0, 0, tiled=True)  33.1 us
    dot_general x10, matrix products, mm_tn(): lax.dot_general(a, b, (((0,), (0,)), ((), ())), preferred_element_type=F32)  31.3 us
    pallas_call x1, Pallas kernels, attention_back(): pl.pallas_call(lambda *refs: attend_back_kernel(groups, *refs), grid_spec...  27.6 us
  transfers between devices with their start and end apart: 49, of which 22 were waited for; matrix products, arithmetic and copies ran while one was open for 13% of the time, Pallas kernels for 20%

profile of v4, /device:TPU:0, one launch (start us, length us, event | category | flops | bytes accessed | tf_op | source)
XLA Modules:
  0.0 942.3 jit_solution(18020554274511335845)
XLA Ops:
  11.1 5.0 collective-permute-start.1
  17.2 4.3 collective-permute-done.1
  21.5 11.3 %collective-permute-done.2 = bf16[48,2048]{1,0:T(8,128)(2,1)S(1)} collective-permute-done((bf16[48,2048]{1,0:T(8,128)(2,1)S(1)}, bf16[48,2048]{1,0:T(8,128)(2,1)S(1)}, u32[]{:S(2)}, u32[]{:S(2)}) %collective-permute-start.2) | collective-permute-done | bytes 196640 | tf_op jit(solution)/shard_map/ppermute | solution.py:594
  49.2 3.8 collective-permute-start.4
  57.8 20.2 %collective-permute-done.8 = bf16[2,384]{1,0:T(2,128)(2,1)S(1)} collective-permute-done((bf16[2,384]{1,0:T(2,128)(2,1)S(1)}, bf16[2,384]{1,0:T(2,128)(2,1)S(1)}, u32[]{:S(2)}, u32[]{:S(2)}) %collective-permute-start.8) | collective-permute-done | bytes 1568 | tf_op jit(solution)/shard_map/ppermute | solution.py:594
  78.0 4.1 collective-permute-start.5
  87.0 5.4 collective-permute-done.5
  93.4 4.8 shard_map.212
  103.4 4.3 fusion.refs_1_
  107.7 31.7 %collective-permute-done.7.refs_9_ = bf16[576,1536]{1,0:T(8,128)(2,1)} collective-permute-done((bf16[576,1536]{1,0:T(8,128)(2,1)}, bf16[576,1536]{1,0:T(8,128)(2,1)}, u32[]{:S(2)}, u32[]{:S(2)}) %collective-permute-start.7) | collective-permute-done | bytes 1769504 | tf_op jit(solution)/shard_map/ppermute | solution.py:594
  146.5 21.3 %shard_map.213 = (bf16[4,128,1536]{2,1,0:T(8,128)(2,1)}, f32[4,2,128,128]{3,2,1,0:T(8,128)}, bf16[4,128,1536]{2,1,0:T(8,128)(2,1)}) custom-call(s32[5]{0:T(128)} %pad_add_fusion.refs_0_, f32[4,128,1536]{2,1,0:T(8,128)} %fusion.refs_1_, bf16[4,1024,512]{2,1,0:T(8,128)(2,1)} %all-gather.9.cloned.1.call-done.refs_2_, ...), custom_call_target="tpu_custom_call" | custom-call | flops 22548578304 | bytes 10485760 | tf_op jit(solution)/shard_map/pallas_call | solution.py:156
  170.9 7.3 all-gather.11.cloned.1.call-done
  178.2 5.2 multiply_reduce_fusion.2
  186.3 6.7 convolution_convert_fusion.1
  193.1 4.9 all-to-all-start
  205.0 78.8 %collective-permute-done.13.refs_7_ = bf16[192,1536]{1,0:T(8,128)(2,1)} collective-permute-done((bf16[192,1536]{1,0:T(8,128)(2,1)}, bf16[192,1536]{1,0:T(8,128)(2,1)}, u32[]{:S(2)}, u32[]{:S(2)}) %collective-permute-start.13) | collective-permute-done | bytes 589856 | tf_op jit(solution)/shard_map/ppermute | solution.py:594
  283.8 12.0 %collective-permute-done.14.refs_8_ = bf16[192,1536]{1,0:T(8,128)(2,1)} collective-permute-done((bf16[192,1536]{1,0:T(8,128)(2,1)}, bf16[192,1536]{1,0:T(8,128)(2,1)}, u32[]{:S(2)}, u32[]{:S(2)}) %collective-permute-start.14) | collective-permute-done | bytes 589856 | tf_op jit(solution)/shard_map/ppermute | solution.py:594
  296.9 8.7 convolution_convert_fusion
  305.6 4.9 all-to-all-start.1
  315.5 101.4 %collective-permute-done.18.refs_6_ = bf16[192,1536]{1,0:T(8,128)(2,1)S(1)} collective-permute-done((bf16[192,1536]{1,0:T(8,128)(2,1)}, bf16[192,1536]{1,0:T(8,128)(2,1)S(1)}, u32[]{:S(2)}, u32[]{:S(2)}) %collective-permute-start.18) | collective-permute-done | bytes 589856 | tf_op jit(solution)/shard_map/ppermute | solution.py:594
  422.7 52.7 %shard_map.215 = (bf16[8,2,80,1536]{3,2,1,0:T(8,128)(2,1)}, bf16[8,2,80,1664]{3,2,1,0:T(8,128)(2,1)}, bf16[576,1536]{1,0:T(8,128)(2,1)}, bf16[576,1536]{1,0:T(8,...) custom-call(s32[3]{0:T(128)} %get-tuple-element.308.refs_0_, ...), custom_call_target="tpu_custom_call" | custom-call | flops 57378078720 | bytes 44040192 | tf_op jit(solution)/shard_map/pallas_call | solution.py:511
  477.8 4.5 all-to-all-start.2
  482.3 51.1 %shard_map.216 = (bf16[8,2,80,1536]{3,2,1,0:T(8,128)(2,1)}, bf16[8,2,80,1664]{3,2,1,0:T(8,128)(2,1)}, bf16[576,1536]{1,0:T(8,128)(2,1)}, bf16[576,1536]{1,0:T(8,...) custom-call(s32[3]{0:T(128)} %get-tuple-element.309.refs_0_, ...), custom_call_target="tpu_custom_call" | custom-call | flops 57378078720 | bytes 44040192 | tf_op jit(solution)/shard_map/pallas_call | solution.py:511
  533.5 9.2 collective-permute-done.22
  543.9 4.5 all-to-all-start.3
  548.7 46.1 %all-to-all-done.3 = bf16[8,2,80,1536]{3,2,1,0:T(8,128)(2,1)} async-done(((bf16[8,2,80,1536]{3,2,1,0:T(8,128)(2,1)}), bf16[8,2,80,1536]{3,2,1,0:T(8,128)(2,1)}, u32[]{:S(2)}, u32[]{:S(2)}) %all-to-all-start.3) | async-done | bytes 3932192 | tf_op jit(solution)/shard_map/all_to_all | solution.py:612
  597.7 4.2 fusion.11
  603.2 4.6 all-to-all-start.4
  611.0 37.2 %collective-permute-done.25 = bf16[512,1536]{1,0:T(8,128)(2,1)} collective-permute-done((bf16[512,1536]{1,0:T(8,128)(2,1)}, bf16[512,1536]{1,0:T(8,128)(2,1)}, u32[]{:S(2)}, u32[]{:S(2)}) %collective-permute-start.25) | collective-permute-done | bytes 1572896 | tf_op jit(solution)/shard_map/ppermute | solution.py:609
  648.2 3.5 convert_add_fusion.6
  657.0 3.7 convolution_convert_fusion.2
  660.7 5.0 all-to-all-start.5
  665.7 27.6 %shard_map.217 = (bf16[4,128,1536]{2,1,0:T(8,128)(2,1)}, bf16[8,4,128,512]{3,2,1,0:T(8,128)(2,1)}) custom-call(s32[5]{0:T(128)} %pad_add_fusion.refs_0_, bf16[4,128,1536]{2,1,0:T(8,128)(2,1)} %get-tuple-element.215.refs_1_, bf16[4,1024,512]{2,1,0:T(8,128)(2,1)} %all-gather.9.cloned.1.call-done.refs_2_, bf16[4,128,1536]{2,1,0:T(8,128)(2,1)} %bitcast.291, ...), custom_call_target="tpu_custom_call" | custom-call | flops 28991029248 | bytes 17825792 | tf_op jit(solution)/shard_map/pallas_call | solution.py:191
  696.4 24.9 %shard_map.218 = bf16[1536,3584]{1,0:T(8,128)(2,1)} custom-call(bf16[512,1536]{1,0:T(8,128)(2,1)} %bitcast.288, bf16[512,1536]{1,0:T(8,128)(2,1)} %copy-done.21, bf16[512,1536]{1,0:T(8,128)(2,1)} %fusion.7.x_ref.refs_2_, bf16[512,1536]{1,0:T(8,128)(2,1)} %bitcast.289, bf16[4096,1536]{1,0:T(8,128)(2,1)} %all-gather.13.cloned.1.call-done.refs_4_, ...), custom_call_target="tpu_custom_call" | custom-call | flops 22548578304 | bytes 12582912 | tf_op jit(solution)/shard_map/pallas_call | solution.py:402
  722.3 4.6 all-to-all-start.6
  728.1 3.7 fusion.22
  731.8 5.3 fusion.3
  739.6 4.6 convert_add_fusion.4
  750.8 5.1 bitcast_add_fusion
  755.9 43.8 %all-to-all-done.6.terms_ref = bf16[8,4,128,512]{3,2,1,0:T(8,128)(2,1)} async-done(((bf16[8,4,128,512]{3,2,1,0:T(8,128)(2,1)}), bf16[8,4,128,512]{3,2,1,0:T(8,128)(2,1)}, u32[]{:S(2)}, u32[]{:S(2)}) %all-to-all-start.6) | async-done | bytes 4194336 | tf_op jit(solution)/shard_map/all_to_all | solution.py:612
  809.7 4.2 convert_add_fusion.2
  813.9 15.5 %shard_map.219 = (f32[512,1536]{1,0:T(8,128)}, f32[1,1536]{1,0:T(1,128)}) custom-call(bf16[512,1536]{1,0:T(8,128)(2,1)} %bitcast.290, bf16[8,4,128,512]{3,2,1,0:T(8,128)(2,1)} %all-to-all-done.6.terms_ref, bf16[1536,2048]{1,0:T(8,128)(2,1)} %bitcast.258, bf16[512,1536]{1,0:T(8,128)(2,1)} %bitcast.251, f32[512,1]{1,0:T(8,128)} %copy.67.inverse_ref, ...), custom_call_target="tpu_custom_call" | custom-call | flops 12884901888 | bytes 12582912 | tf_op jit(solution)/shard_map/pallas_call | solution.py:450
  839.7 4.4 collective-permute-done.31
  850.3 9.6 %collective-permute-done.32 = bf16[48,3712]{1,0:T(8,128)(2,1)} collective-permute-done((bf16[48,3712]{1,0:T(8,128)(2,1)}, bf16[48,3712]{1,0:T(8,128)(2,1)}, u32[]{:S(2)}, u32[]{:S(2)}) %collective-permute-start.32) | collective-permute-done | bytes 356384 | tf_op jit(solution)/shard_map/ppermute | solution.py:594
  859.9 12.8 %collective-permute-done.33 = bf16[48,3712]{1,0:T(8,128)(2,1)} collective-permute-done((bf16[48,3712]{1,0:T(8,128)(2,1)}, bf16[48,3712]{1,0:T(8,128)(2,1)}, u32[]{:S(2)}, u32[]{:S(2)}) %collective-permute-start.33) | collective-permute-done | bytes 356384 | tf_op jit(solution)/shard_map/ppermute | solution.py:594
  875.0 8.2 collective-permute-start.35
  892.0 19.7 %all-gather.15.cloned.1.call-done = bf16[384,3712]{1,0:T(8,128)(2,1)} async-done(((bf16[48,3712]{1,0:T(8,128)(2,1)}), bf16[384,3712]{1,0:T(8,128)(2,1)}) %all-gather.15.cloned.1.call-update) | async-done | bytes 2850832 | tf_op jit(solution)/shard_map/all_gather | solution.py:875
  921.0 4.9 fusion.100
  (300 shorter events, 155.2 us)
Async XLA Ops:
  7.2 86.2 %all-gather.7.cloned.1.call-start = ((), (), s32[]{:S(2)}) async-start(), calls=%async_computation.8 | async-start | bytes 7077888 | tf_op jit(solution)/shard_map/all_gather | solution.py:615
  11.1 10.4 %collective-permute-start.1 = (bf16[48,2048]{1,0:T(8,128)(2,1)S(1)}, bf16[48,2048]{1,0:T(8,128)(2,1)S(1)}, u32[]{:S(2)}, u32[]{:S(2)}) collective-permute-start(bf16[48,2048]{1,0:T(8,128)(2,1)S(1)} %constant_dynamic-update-slice_fusion), channel_id=1, source_target_pairs={{0,3},{1,0},{2,1},{3,2},{4,7},{5,4},{6,5},{7,6},{8,11},{9,8},{10,9... | collective-permute-start | bytes 589832 | tf_op jit(solution)/shard_map/ppermute | solution.py:594
  16.2 16.7 %collective-permute-start.2 = (bf16[48,2048]{1,0:T(8,128)(2,1)S(1)}, bf16[48,2048]{1,0:T(8,128)(2,1)S(1)}, u32[]{:S(2)}, u32[]{:S(2)}) collective-permute-start(bf16[48,2048]{1,0:T(8,128)(2,1)S(1)} %constant_dynamic-update-slice_fusion), channel_id=1, source_target_pairs={{0,2},{1,3},{2,0},{3,1},{4,6},{5,7},{6,4},{7,5},{8,10},{9,11},{10,... | collective-permute-start | bytes 589832 | tf_op jit(solution)/shard_map/ppermute | solution.py:594
  16.2 16.7 %collective-permute-start.3 = (bf16[48,2048]{1,0:T(8,128)(2,1)S(1)}, bf16[48,2048]{1,0:T(8,128)(2,1)S(1)}, u32[]{:S(2)}, u32[]{:S(2)}) collective-permute-start(bf16[48,2048]{1,0:T(8,128)(2,1)S(1)} %constant_dynamic-update-slice_fusion), channel_id=1, source_target_pairs={{0,1},{1,2},{2,3},{3,0},{4,5},{5,6},{6,7},{7,4},{8,9},{9,10},{10,1... | collective-permute-start | bytes 589832 | tf_op jit(solution)/shard_map/ppermute | solution.py:594
  34.0 105.4 %all-gather.9.cloned.1.call-start = ((), (), s32[]{:S(2)}) async-start(), calls=%async_computation.9 | async-start | bytes 4718592 | tf_op jit(solution)/shard_map/all_gather | solution.py:714
  37.9 55.5 %collective-permute-start = (bf16[576,1536]{1,0:T(8,128)(2,1)}, bf16[576,1536]{1,0:T(8,128)(2,1)}, u32[]{:S(2)}, u32[]{:S(2)}) collective-permute-start(bf16[576,1536]{1,0:T(8,128)(2,1)} %pad_maximum_fusion), channel_id=1, source_target_pairs={{0,1},{1,2},{2,3},{3,0},{4,5},{5,6},{6,7},{7,4},{8,9},{9,10},{10,1... | collective-permute-start | bytes 5308424 | tf_op jit(solution)/shard_map/ppermute | solution.py:594
  45.2 32.8 %collective-permute-start.8 = (bf16[2,384]{1,0:T(2,128)(2,1)S(1)}, bf16[2,384]{1,0:T(2,128)(2,1)S(1)}, u32[]{:S(2)}, u32[]{:S(2)}) collective-permute-start(bf16[2,384]{1,0:T(2,128)(2,1)S(1)} %pad_maximum_fusion.8), channel_id=1, source_target_pairs={{0,3},{1,0},{2,1},{3,2},{4,7},{5,4},{6,5},{7,6},{8,11},{9,8},{10,9... | collective-permute-start | bytes 4616 | tf_op jit(solution)/shard_map/ppermute | solution.py:594
  48.2 33.9 %collective-permute-start.9 = (bf16[2,384]{1,0:T(2,128)(2,1)S(1)}, bf16[2,384]{1,0:T(2,128)(2,1)S(1)}, u32[]{:S(2)}, u32[]{:S(2)}) collective-permute-start(bf16[2,384]{1,0:T(2,128)(2,1)S(1)} %pad_maximum_fusion.8), channel_id=1, source_target_pairs={{0,2},{1,3},{2,0},{3,1},{4,6},{5,7},{6,4},{7,5},{8,10},{9,11},{10,... | collective-permute-start | bytes 4616 | tf_op jit(solution)/shard_map/ppermute | solution.py:594
  49.2 35.6 %collective-permute-start.10 = (bf16[2,384]{1,0:T(2,128)(2,1)S(1)}, bf16[2,384]{1,0:T(2,128)(2,1)S(1)}, u32[]{:S(2)}, u32[]{:S(2)}) collective-permute-start(bf16[2,384]{1,0:T(2,128)(2,1)S(1)} %pad_maximum_fusion.8), channel_id=1, source_target_pairs={{0,1},{1,2},{2,3},{3,0},{4,5},{5,6},{6,7},{7,4},{8,9},{9,10},{10,1... | collective-permute-start | bytes 4616 | tf_op jit(solution)/shard_map/ppermute | solution.py:594
  49.2 37.8 %collective-permute-start.4 = (bf16[48,1536]{1,0:T(8,128)(2,1)S(1)}, bf16[48,1536]{1,0:T(8,128)(2,1)S(1)}, u32[]{:S(2)}, u32[]{:S(2)}) collective-permute-start(bf16[48,1536]{1,0:T(8,128)(2,1)S(1)} %constant_dynamic-slice_fusion.3), channel_id=1, source_target_pairs={{0,3},{1,0},{2,1},{3,2},{4,7},{5,4},{6,5},{7,6},{8,11},{9,8},{10,9... | collective-permute-start | bytes 442376 | tf_op jit(solution)/shard_map/ppermute | solution.py:594
  78.0 14.4 %collective-permute-start.5 = (bf16[48,1536]{1,0:T(8,128)(2,1)S(1)}, bf16[48,1536]{1,0:T(8,128)(2,1)S(1)}, u32[]{:S(2)}, u32[]{:S(2)}) collective-permute-start(bf16[48,1536]{1,0:T(8,128)(2,1)S(1)} %constant_dynamic-slice_fusion.3), channel_id=1, source_target_pairs={{0,2},{1,3},{2,0},{3,1},{4,6},{5,7},{6,4},{7,5},{8,10},{9,11},{10,... | collective-permute-start | bytes 442376 | tf_op jit(solution)/shard_map/ppermute | solution.py:594
  98.2 80.0 %all-gather.11.cloned.1.call-start = ((), (), s32[]{:S(2)}) async-start(), calls=%async_computation.10 | async-start | bytes 5308416 | tf_op jit(solution)/shard_map/all_gather | solution.py:615
  98.2 41.2 %collective-permute-start.7 = (bf16[576,1536]{1,0:T(8,128)(2,1)}, bf16[576,1536]{1,0:T(8,128)(2,1)}, u32[]{:S(2)}, u32[]{:S(2)}) collective-permute-start(bf16[576,1536]{1,0:T(8,128)(2,1)} %pad_maximum_fusion), channel_id=1, source_target_pairs={{0,3},{1,0},{2,1},{3,2},{4,7},{5,4},{6,5},{7,6},{8,11},{9,8},{10,9... | collective-permute-start | bytes 5308424 | tf_op jit(solution)/shard_map/ppermute | solution.py:594
  143.9 27.1 %collective-permute-start.11 = (bf16[192,1536]{1,0:T(8,128)(2,1)S(1)}, bf16[192,1536]{1,0:T(8,128)(2,1)}, u32[]{:S(2)}, u32[]{:S(2)}) collective-permute-start(bf16[192,1536]{1,0:T(8,128)(2,1)S(1)} %get-tuple-element.154), channel_id=1, source_target_pairs={{0,2},{1,3},{2,0},{3,1},{4,6},{5,7},{6,4},{7,5},{8,10},{9,11},{10,... | collective-permute-start | bytes 1769480 | tf_op jit(solution)/shard_map/ppermute | solution.py:594
  143.9 23.9 %collective-permute-start.12 = (bf16[512,128]{1,0:T(8,128)(2,1)S(1)}, bf16[512,128]{1,0:T(8,128)(2,1)S(1)}, u32[]{:S(2)}, u32[]{:S(2)}) collective-permute-start(bf16[512,128]{1,0:T(8,128)(2,1)S(1)} %pad_maximum_fusion.5), channel_id=1, source_target_pairs={{0,1},{1,0},{2,3},{3,2},{4,5},{5,4},{6,7},{7,6},{8,9},{9,8},{10,11... | collective-permute-start | bytes 393224 | tf_op jit(solution)/shard_map/ppermute | solution.py:609
  193.1 103.7 %all-to-all-start = ((bf16[8,2,80,3200]{3,2,1,0:T(8,128)(2,1)}), bf16[8,2,80,3200]{3,2,1,0:T(8,128)(2,1)}, u32[]{:S(2)}, u32[]{:S(2)}) async-start(bf16[8,2,80,3200]{3,2,1,0:T(8,128)(2,1)} %bitcast.253), calls=%async_computation | async-start | bytes 16384000 | tf_op jit(solution)/shard_map/all_to_all | solution.py:612
  198.0 98.8 %collective-permute-start.15 = (bf16[512,3200]{1,0:T(8,128)(2,1)}, bf16[512,3200]{1,0:T(8,128)(2,1)}, u32[]{:S(2)}, u32[]{:S(2)}) collective-permute-start(bf16[512,3200]{1,0:T(8,128)(2,1)} %copy-done.23), channel_id=1, source_target_pairs={{0,1},{1,0},{2,3},{3,2},{4,5},{5,4},{6,7},{7,6},{8,9},{9,8},{10,11... | collective-permute-start | bytes 9830408 | tf_op jit(solution)/shard_map/ppermute | solution.py:609
  201.5 82.3 %collective-permute-start.13 = (bf16[192,1536]{1,0:T(8,128)(2,1)}, bf16[192,1536]{1,0:T(8,128)(2,1)}, u32[]{:S(2)}, u32[]{:S(2)}) collective-permute-start(bf16[192,1536]{1,0:T(8,128)(2,1)} %get-tuple-element.164), channel_id=1, source_target_pairs={{0,2},{1,3},{2,0},{3,1},{4,6},{5,7},{6,4},{7,5},{8,10},{9,11},{10,... | collective-permute-start | bytes 1769480 | tf_op jit(solution)/shard_map/ppermute | solution.py:594
  203.9 91.9 %collective-permute-start.14 = (bf16[192,1536]{1,0:T(8,128)(2,1)}, bf16[192,1536]{1,0:T(8,128)(2,1)}, u32[]{:S(2)}, u32[]{:S(2)}) collective-permute-start(bf16[192,1536]{1,0:T(8,128)(2,1)} %get-tuple-element.165), channel_id=1, source_target_pairs={{0,2},{1,3},{2,0},{3,1},{4,6},{5,7},{6,4},{7,5},{8,10},{9,11},{10,... | collective-permute-start | bytes 1769480 | tf_op jit(solution)/shard_map/ppermute | solution.py:594
  305.6 113.4 %all-to-all-start.1 = ((bf16[8,2,80,3200]{3,2,1,0:T(8,128)(2,1)}), bf16[8,2,80,3200]{3,2,1,0:T(8,128)(2,1)}, u32[]{:S(2)}, u32[]{:S(2)}) async-start(bf16[8,2,80,3200]{3,2,1,0:T(8,128)(2,1)} %bitcast.254), calls=%async_computation.1 | async-start | bytes 16384000 | tf_op jit(solution)/shard_map/all_to_all | solution.py:612
  310.6 232.1 %all-gather.13.cloned.1.call-start = ((), (), s32[]{:S(2)}) async-start(), calls=%async_computation.11 | async-start | bytes 14155776 | tf_op jit(solution)/shard_map/all_gather | solution.py:759
  311.0 105.9 %collective-permute-start.16 = (bf16[576,1536]{1,0:T(8,128)(2,1)S(1)}, bf16[576,1536]{1,0:T(8,128)(2,1)S(1)}, u32[]{:S(2)}, u32[]{:S(2)}) collective-permute-start(bf16[576,1536]{1,0:T(8,128)(2,1)S(1)} %pad_maximum_fusion.1), channel_id=1, source_target_pairs={{0,1},{1,2},{2,3},{3,0},{4,5},{5,6},{6,7},{7,4},{8,9},{9,10},{10,1... | collective-permute-start | bytes 5308424 | tf_op jit(solution)/shard_map/ppermute | solution.py:594
  313.5 105.6 %collective-permute-start.17 = (bf16[576,1536]{1,0:T(8,128)(2,1)S(1)}, bf16[576,1536]{1,0:T(8,128)(2,1)}, u32[]{:S(2)}, u32[]{:S(2)}) collective-permute-start(bf16[576,1536]{1,0:T(8,128)(2,1)S(1)} %pad_maximum_fusion.1), channel_id=1, source_target_pairs={{0,3},{1,0},{2,1},{3,2},{4,7},{5,4},{6,5},{7,6},{8,11},{9,8},{10,9... | collective-permute-start | bytes 5308424 | tf_op jit(solution)/shard_map/ppermute | solution.py:594
  314.9 102.0 %collective-permute-start.18 = (bf16[192,1536]{1,0:T(8,128)(2,1)}, bf16[192,1536]{1,0:T(8,128)(2,1)S(1)}, u32[]{:S(2)}, u32[]{:S(2)}) collective-permute-start(bf16[192,1536]{1,0:T(8,128)(2,1)} %get-tuple-element.174), channel_id=1, source_target_pairs={{0,2},{1,3},{2,0},{3,1},{4,6},{5,7},{6,4},{7,5},{8,10},{9,11},{10,... | collective-permute-start | bytes 1769480 | tf_op jit(solution)/shard_map/ppermute | solution.py:594
  419.8 55.6 %collective-permute-start.19 = (bf16[192,1536]{1,0:T(8,128)(2,1)}, bf16[192,1536]{1,0:T(8,128)(2,1)S(1)}, u32[]{:S(2)}, u32[]{:S(2)}) collective-permute-start(bf16[192,1536]{1,0:T(8,128)(2,1)} %get-tuple-element.177), channel_id=1, source_target_pairs={{0,2},{1,3},{2,0},{3,1},{4,6},{5,7},{6,4},{7,5},{8,10},{9,11},{10,... | collective-permute-start | bytes 1769480 | tf_op jit(solution)/shard_map/ppermute | solution.py:594
  419.8 55.6 %collective-permute-start.20 = (bf16[192,1536]{1,0:T(8,128)(2,1)}, bf16[192,1536]{1,0:T(8,128)(2,1)S(1)}, u32[]{:S(2)}, u32[]{:S(2)}) collective-permute-start(bf16[192,1536]{1,0:T(8,128)(2,1)} %get-tuple-element.178), channel_id=1, source_target_pairs={{0,2},{1,3},{2,0},{3,1},{4,6},{5,7},{6,4},{7,5},{8,10},{9,11},{10,... | collective-permute-start | bytes 1769480 | tf_op jit(solution)/shard_map/ppermute | solution.py:594
  476.4 66.2 %collective-permute-start.21 = (bf16[576,1536]{1,0:T(8,128)(2,1)}, bf16[576,1536]{1,0:T(8,128)(2,1)S(1)}, u32[]{:S(2)}, u32[]{:S(2)}) collective-permute-start(bf16[576,1536]{1,0:T(8,128)(2,1)} %get-tuple-element.190), channel_id=1, source_target_pairs={{0,1},{1,2},{2,3},{3,0},{4,5},{5,6},{6,7},{7,4},{8,9},{9,10},{10,1... | collective-permute-start | bytes 5308424 | tf_op jit(solution)/shard_map/ppermute | solution.py:594
  476.4 66.2 %collective-permute-start.22 = (bf16[192,1536]{1,0:T(8,128)(2,1)}, bf16[192,1536]{1,0:T(8,128)(2,1)}, u32[]{:S(2)}, u32[]{:S(2)}) collective-permute-start(bf16[192,1536]{1,0:T(8,128)(2,1)} %get-tuple-element.191), channel_id=1, source_target_pairs={{0,2},{1,3},{2,0},{3,1},{4,6},{5,7},{6,4},{7,5},{8,10},{9,11},{10,... | collective-permute-start | bytes 1769480 | tf_op jit(solution)/shard_map/ppermute | solution.py:594
  477.8 64.9 %all-to-all-start.2 = ((bf16[8,2,80,1536]{3,2,1,0:T(8,128)(2,1)}), bf16[8,2,80,1536]{3,2,1,0:T(8,128)(2,1)}, u32[]{:S(2)}, u32[]{:S(2)}) async-start(bf16[8,2,80,1536]{3,2,1,0:T(8,128)(2,1)} %get-tuple-element.199), calls=%async_computation.2 | async-start | bytes 7864320 | tf_op jit(solution)/shard_map/all_to_all | solution.py:612
  543.9 50.9 %all-to-all-start.3 = ((bf16[8,2,80,1536]{3,2,1,0:T(8,128)(2,1)}), bf16[8,2,80,1536]{3,2,1,0:T(8,128)(2,1)}, u32[]{:S(2)}, u32[]{:S(2)}) async-start(bf16[8,2,80,1536]{3,2,1,0:T(8,128)(2,1)} %get-tuple-element.205), calls=%async_computation.3 | async-start | bytes 7864320 | tf_op jit(solution)/shard_map/all_to_all | solution.py:612
  548.4 53.5 %collective-permute-start.23 = (bf16[576,1536]{1,0:T(8,128)(2,1)}, bf16[576,1536]{1,0:T(8,128)(2,1)S(1)}, u32[]{:S(2)}, u32[]{:S(2)}) collective-permute-start(bf16[576,1536]{1,0:T(8,128)(2,1)} %get-tuple-element.203), channel_id=1, source_target_pairs={{0,3},{1,0},{2,1},{3,2},{4,7},{5,4},{6,5},{7,6},{8,11},{9,8},{10,9... | collective-permute-start | bytes 5308424 | tf_op jit(solution)/shard_map/ppermute | solution.py:594
  602.0 46.2 %collective-permute-start.25 = (bf16[512,1536]{1,0:T(8,128)(2,1)}, bf16[512,1536]{1,0:T(8,128)(2,1)}, u32[]{:S(2)}, u32[]{:S(2)}) collective-permute-start(bf16[512,1536]{1,0:T(8,128)(2,1)} %fusion.11), channel_id=1, source_target_pairs={{0,1},{1,0},{2,3},{3,2},{4,5},{5,4},{6,7},{7,6},{8,9},{9,8},{10,11... | collective-permute-start | bytes 4718600 | tf_op jit(solution)/shard_map/ppermute | solution.py:609
  603.2 57.5 %all-to-all-start.4 = ((bf16[8,2,80,1664]{3,2,1,0:T(8,128)(2,1)}), bf16[8,2,80,1664]{3,2,1,0:T(8,128)(2,1)}, u32[]{:S(2)}, u32[]{:S(2)}) async-start(bf16[8,2,80,1664]{3,2,1,0:T(8,128)(2,1)} %get-tuple-element.211), calls=%async_computation.4 | async-start | bytes 8519680 | tf_op jit(solution)/shard_map/all_to_all | solution.py:612
  607.8 43.9 %collective-permute-start.24 = (bf16[192,1536]{1,0:T(8,128)(2,1)}, bf16[192,1536]{1,0:T(8,128)(2,1)}, u32[]{:S(2)}, u32[]{:S(2)}) collective-permute-start(bf16[192,1536]{1,0:T(8,128)(2,1)} %get-tuple-element.208), channel_id=1, source_target_pairs={{0,2},{1,3},{2,0},{3,1},{4,6},{5,7},{6,4},{7,5},{8,10},{9,11},{10,... | collective-permute-start | bytes 1769480 | tf_op jit(solution)/shard_map/ppermute | solution.py:594
  660.7 32.7 %collective-permute-start.26 = (bf16[192,1536]{1,0:T(8,128)(2,1)}, bf16[192,1536]{1,0:T(8,128)(2,1)}, u32[]{:S(2)}, u32[]{:S(2)}) collective-permute-start(bf16[192,1536]{1,0:T(8,128)(2,1)} %get-tuple-element.214), channel_id=1, source_target_pairs={{0,2},{1,3},{2,0},{3,1},{4,6},{5,7},{6,4},{7,5},{8,10},{9,11},{10,... | collective-permute-start | bytes 1769480 | tf_op jit(solution)/shard_map/ppermute | solution.py:594
  660.7 61.6 %all-to-all-start.5 = ((bf16[8,2,80,1664]{3,2,1,0:T(8,128)(2,1)}), bf16[8,2,80,1664]{3,2,1,0:T(8,128)(2,1)}, u32[]{:S(2)}, u32[]{:S(2)}) async-start(bf16[8,2,80,1664]{3,2,1,0:T(8,128)(2,1)} %get-tuple-element.228), calls=%async_computation.5 | async-start | bytes 8519680 | tf_op jit(solution)/shard_map/all_to_all | solution.py:612
  665.7 178.6 %reduce-scatter.2.cloned.1.call-start = ((), (), s32[]{:S(2)}) async-start(), calls=%async_computation.12 | async-start | bytes 12386304 | tf_op jit(solution)/shard_map/reduce_scatter | solution.py:818
  693.4 28.9 %collective-permute-start.27 = (bf16[192,1536]{1,0:T(8,128)(2,1)}, bf16[192,1536]{1,0:T(8,128)(2,1)}, u32[]{:S(2)}, u32[]{:S(2)}) collective-permute-start(bf16[192,1536]{1,0:T(8,128)(2,1)} %get-tuple-element.223), channel_id=1, source_target_pairs={{0,2},{1,3},{2,0},{3,1},{4,6},{5,7},{6,4},{7,5},{8,10},{9,11},{10,... | collective-permute-start | bytes 1769480 | tf_op jit(solution)/shard_map/ppermute | solution.py:594
  722.3 77.3 %all-to-all-start.6 = ((bf16[8,4,128,512]{3,2,1,0:T(8,128)(2,1)}), bf16[8,4,128,512]{3,2,1,0:T(8,128)(2,1)}, u32[]{:S(2)}, u32[]{:S(2)}) async-start(bf16[8,4,128,512]{3,2,1,0:T(8,128)(2,1)} %get-tuple-element.226), calls=%async_computation.6 | async-start | bytes 8388608 | tf_op jit(solution)/shard_map/all_to_all | solution.py:612
  726.9 184.8 %all-gather.15.cloned.1.call-start = ((), (), s32[]{:S(2)}) async-start(), calls=%async_computation.13 | async-start | bytes 3207168 | tf_op jit(solution)/shard_map/all_gather | solution.py:875
  737.1 65.0 %collective-permute-start.30 = (bf16[512,1664]{1,0:T(8,128)(2,1)}, bf16[512,1664]{1,0:T(8,128)(2,1)}, u32[]{:S(2)}, u32[]{:S(2)}) collective-permute-start(bf16[512,1664]{1,0:T(8,128)(2,1)} %fusion.3), channel_id=1, source_target_pairs={{0,1},{1,0},{2,3},{3,2},{4,5},{5,4},{6,7},{7,6},{8,9},{9,8},{10,11... | collective-permute-start | bytes 5111816 | tf_op jit(solution)/shard_map/ppermute | solution.py:609
  744.1 55.5 %collective-permute-start.28 = (bf16[192,1536]{1,0:T(8,128)(2,1)}, bf16[192,1536]{1,0:T(8,128)(2,1)}, u32[]{:S(2)}, u32[]{:S(2)}) collective-permute-start(bf16[192,1536]{1,0:T(8,128)(2,1)} %get-tuple-element.231), channel_id=1, source_target_pairs={{0,2},{1,3},{2,0},{3,1},{4,6},{5,7},{6,4},{7,5},{8,10},{9,11},{10,... | collective-permute-start | bytes 1769480 | tf_op jit(solution)/shard_map/ppermute | solution.py:594
  747.5 52.3 %collective-permute-start.29 = (bf16[192,1536]{1,0:T(8,128)(2,1)}, bf16[192,1536]{1,0:T(8,128)(2,1)}, u32[]{:S(2)}, u32[]{:S(2)}) collective-permute-start(bf16[192,1536]{1,0:T(8,128)(2,1)} %get-tuple-element.232), channel_id=1, source_target_pairs={{0,2},{1,3},{2,0},{3,1},{4,6},{5,7},{6,4},{7,5},{8,10},{9,11},{10,... | collective-permute-start | bytes 1769480 | tf_op jit(solution)/shard_map/ppermute | solution.py:594
  802.0 42.1 %collective-permute-start.31 = (bf16[576,1536]{1,0:T(8,128)(2,1)}, bf16[576,1536]{1,0:T(8,128)(2,1)}, u32[]{:S(2)}, u32[]{:S(2)}) collective-permute-start(bf16[576,1536]{1,0:T(8,128)(2,1)} %get-tuple-element.238), channel_id=1, source_target_pairs={{0,1},{1,2},{2,3},{3,0},{4,5},{5,6},{6,7},{7,4},{8,9},{9,10},{10,1... | collective-permute-start | bytes 5308424 | tf_op jit(solution)/shard_map/ppermute | solution.py:594
  846.5 13.5 %collective-permute-start.32 = (bf16[48,3712]{1,0:T(8,128)(2,1)}, bf16[48,3712]{1,0:T(8,128)(2,1)}, u32[]{:S(2)}, u32[]{:S(2)}) collective-permute-start(bf16[48,3712]{1,0:T(8,128)(2,1)} %get-tuple-element.290), channel_id=1, source_target_pairs={{0,1},{1,2},{2,3},{3,0},{4,5},{5,6},{6,7},{7,4},{8,9},{9,10},{10,1... | collective-permute-start | bytes 1069064 | tf_op jit(solution)/shard_map/ppermute | solution.py:594
  847.2 25.5 %collective-permute-start.33 = (bf16[48,3712]{1,0:T(8,128)(2,1)}, bf16[48,3712]{1,0:T(8,128)(2,1)}, u32[]{:S(2)}, u32[]{:S(2)}) collective-permute-start(bf16[48,3712]{1,0:T(8,128)(2,1)} %get-tuple-element.291), channel_id=1, source_target_pairs={{0,2},{1,3},{2,0},{3,1},{4,6},{5,7},{6,4},{7,5},{8,10},{9,11},{10,... | collective-permute-start | bytes 1069064 | tf_op jit(solution)/shard_map/ppermute | solution.py:594
  848.8 24.0 %collective-permute-start.34 = (bf16[48,3712]{1,0:T(8,128)(2,1)S(1)}, bf16[48,3712]{1,0:T(8,128)(2,1)}, u32[]{:S(2)}, u32[]{:S(2)}) collective-permute-start(bf16[48,3712]{1,0:T(8,128)(2,1)S(1)} %get-tuple-element.292), channel_id=1, source_target_pairs={{0,3},{1,0},{2,1},{3,2},{4,7},{5,4},{6,5},{7,6},{8,11},{9,8},{10,9... | collective-permute-start | bytes 1069064 | tf_op jit(solution)/shard_map/ppermute | solution.py:594
  875.0 50.8 %collective-permute-start.35 = (bf16[576,1536]{1,0:T(8,128)(2,1)}, bf16[576,1536]{1,0:T(8,128)(2,1)}, u32[]{:S(2)}, u32[]{:S(2)}) collective-permute-start(bf16[576,1536]{1,0:T(8,128)(2,1)} %get-tuple-element.262), channel_id=1, source_target_pairs={{0,3},{1,0},{2,1},{3,2},{4,7},{5,4},{6,5},{7,6},{8,11},{9,8},{10,9... | collective-permute-start | bytes 5308424 | tf_op jit(solution)/shard_map/ppermute | solution.py:594
  (46 other events, 972.1 us)
Sparse Core Ops, SparseCore 0:
  34.1 45.9 all-gather.6
  98.3 35.3 all-gather.8
  139.5 38.6 all-gather.10
  419.2 74.4 all-gather.12
  722.5 106.7 reduce-scatter.1
  875.1 36.5 all-gather.14

commit v5 on v4

--- a/solution.py
+++ b/solution.py
@@ -727,7 +727,7 @@
     second, inverse_two = norm_forward(hidden, second_scale)
     second_low = second.astype(BF16)
 
-    second_low, cot_wide = step([], (second_low, cot_wide), ["w2b", "w2c"])
+    second_low, cot_wide = step([], (second_low, cot_wide), ["w2b", "w2c", "v2a"])
     wide_rows = jnp.concatenate([second_low, cot_wide], axis=1)
     expert_rows = [exchange(to_slots(sels[0], wide_rows))]
     shards = None
@@ -736,7 +736,7 @@
         sels.append(route(far_table))
         shards = list(blank([(pieces, Dl, 2 * W), (pieces, W // F, D)]))
         far_rows, expert_rows[0], sels[1], shards = step(
-            ["w2b", "w2c"], (far_rows, expert_rows[0], sels[1], shards), ["v1", "v3", "v2a"]
+            ["w2b", "w2c", "v2a"], (far_rows, expert_rows[0], sels[1], shards), ["v1", "v3"]
         )
         expert_rows.append(exchange(to_slots(sels[1], far_rows)))
 
@@ -754,7 +754,7 @@
 
     if merged:
         expert_rows[1], normed_mine = step(
-            ["v1", "v3", "v2a"], (expert_rows[1], normed_low), ["v2b", "v2c"]
+            ["v1", "v3"], (expert_rows[1], normed_low), ["v2b", "v2c"]
         )
         every_normed = lax.all_gather(normed_mine, "ctx", axis=0, tiled=True)
         outs = [expert(0)]
@@ -880,9 +880,11 @@
     gain_sums = jnp.sum(wide[:, :, gain_at : gain_at + gain_count].astype(F32), axis=0)
     grad_first, grad_second = gain_sums.reshape(2, Dl)
 
-    grads = (grad_projection, grad_query, grad_pairs, grad_first, grad_second)
+    grad_key = grad_pairs[:, :, 0].reshape(Dl, KV * HD)
+    grad_value = grad_pairs[:, :, 1].reshape(Dl, KV * HD)
+    grads = (grad_projection, grad_query, grad_key, grad_value, grad_first, grad_second)
     grads = step(["q3"], grads, [])
-    grad_projection, grad_query, grad_pairs, grad_first, grad_second = grads
+    grad_projection, grad_query, grad_key, grad_value, grad_first, grad_second = grads
     block_rows = (hidden + mixed_rows[:, :D]).astype(BF16)
     router_by_expert = mixed_rows[:, D : D + EXPERTS]
     grad_router = jnp.sum(jnp.where(hit, router_by_expert[:, None, :], 0.0), axis=2)
@@ -906,8 +908,8 @@
         grad_first,
         grad_second,
         grad_query,
-        grad_pairs[:, :, 0].reshape(Dl, KV * HD),
-        grad_pairs[:, :, 1].reshape(Dl, KV * HD),
+        grad_key,
+        grad_value,
         grad_projection,
         grad_up,
         grad_down,

time: 950 us -> 944 us (level)
    ppermute x32, waiting for transfers between devices: 306 us -> 286 us  [shift(): return lax.ppermute(block, 'fsdp', [(i, (i + k) % F) for i in range(F)])]
    all_to_all x7, waiting for transfers between devices: 89.9 us -> 102 us  [exchange(): return lax.all_to_all(blocks, 'ctx', 0, 0, tiled=True)]
  transfers between devices with their start and end apart: 49 -> 49, of which waited for: 22 -> 24; matrix products, arithmetic and copies ran while one was open for 13% -> 13% of each run, Pallas kernels for 20% -> 21%
where the time goes in v5:
time: 944 us; the launch traced here: 937 us
  waiting for transfers between devices  454 us (48%)
  Pallas kernels  198 us (21%)
  starting transfers between devices  98.4 us (10%)
  local copies, waits for them, and re-layouts  61.1 us (6%)
  matrix products  60 us (6%)
  other arithmetic  50.3 us (5%)
  between operations  15.6 us (2%)
    ppermute x32, waiting for transfers between devices, shift(): return lax.ppermute(block, 'fsdp', [(i, (i + k) % F) for i in range(F)])  286 us
    pallas_call x2, Pallas kernels, run_expert(): pl.pallas_call(lambda *refs: expert_kernel(sides, w_mode, g_mode, *refs),...  104 us
    all_to_all x7, waiting for transfers between devices, exchange(): return lax.all_to_all(blocks, 'ctx', 0, 0, tiled=True)  102 us
    ppermute x32, starting transfers between devices, shift(): return lax.ppermute(block, 'fsdp', [(i, (i + k) % F) for i in range(F)])  59 us
    ppermute x4, waiting for transfers between devices, swap(): return lax.ppermute(block, 'fsdp', [(i, i ^ 1) for i in range(F)])  38.8 us
    all_to_all x7, starting transfers between devices, exchange(): return lax.all_to_all(blocks, 'ctx', 0, 0, tiled=True)  34.7 us
    dot_general x10, matrix products, mm_tn(): lax.dot_general(a, b, (((0,), (0,)), ((), ())), preferred_element_type=F32)  31 us
    pallas_call x1, Pallas kernels, attention_back(): pl.pallas_call(lambda *refs: attend_back_kernel(groups, *refs), grid_spec...  27.6 us
  transfers between devices with their start and end apart: 49, of which 24 were waited for; matrix products, arithmetic and copies ran while one was open for 13% of the time, Pallas kernels for 21%

profile of v5, /device:TPU:0, one launch (start us, length us, event | category | flops | bytes accessed | tf_op | source)
XLA Modules:
  0.0 937.0 jit_solution(13895256139034398827)
XLA Ops:
  11.1 5.0 collective-permute-start.1
  17.2 4.3 collective-permute-done.1
  21.5 11.3 %collective-permute-done.2 = bf16[48,2048]{1,0:T(8,128)(2,1)S(1)} collective-permute-done((bf16[48,2048]{1,0:T(8,128)(2,1)S(1)}, bf16[48,2048]{1,0:T(8,128)(2,1)S(1)}, u32[]{:S(2)}, u32[]{:S(2)}) %collective-permute-start.2) | collective-permute-done | bytes 196640 | tf_op jit(solution)/shard_map/ppermute | solution.py:594
  49.2 3.8 collective-permute-start.4
  57.8 20.1 %collective-permute-done.8 = bf16[2,384]{1,0:T(2,128)(2,1)S(1)} collective-permute-done((bf16[2,384]{1,0:T(2,128)(2,1)S(1)}, bf16[2,384]{1,0:T(2,128)(2,1)S(1)}, u32[]{:S(2)}, u32[]{:S(2)}) %collective-permute-start.8) | collective-permute-done | bytes 1568 | tf_op jit(solution)/shard_map/ppermute | solution.py:594
  78.0 4.1 collective-permute-start.5
  87.0 5.4 collective-permute-done.5
  93.4 4.8 shard_map.212
  103.4 4.3 fusion.refs_1_
  107.7 31.7 %collective-permute-done.7.refs_9_ = bf16[576,1536]{1,0:T(8,128)(2,1)} collective-permute-done((bf16[576,1536]{1,0:T(8,128)(2,1)}, bf16[576,1536]{1,0:T(8,128)(2,1)}, u32[]{:S(2)}, u32[]{:S(2)}) %collective-permute-start.7) | collective-permute-done | bytes 1769504 | tf_op jit(solution)/shard_map/ppermute | solution.py:594
  146.6 21.2 %shard_map.213 = (bf16[4,128,1536]{2,1,0:T(8,128)(2,1)}, f32[4,2,128,128]{3,2,1,0:T(8,128)}, bf16[4,128,1536]{2,1,0:T(8,128)(2,1)}) custom-call(s32[5]{0:T(128)} %pad_add_fusion.refs_0_, f32[4,128,1536]{2,1,0:T(8,128)} %fusion.refs_1_, bf16[4,1024,512]{2,1,0:T(8,128)(2,1)} %all-gather.9.cloned.1.call-done.refs_2_, ...), custom_call_target="tpu_custom_call" | custom-call | flops 22548578304 | bytes 10485760 | tf_op jit(solution)/shard_map/pallas_call | solution.py:156
  171.0 7.2 all-gather.11.cloned.1.call-done
  178.2 5.2 multiply_reduce_fusion.2
  186.3 6.8 convolution_convert_fusion.1
  193.1 4.9 all-to-all-start
  207.4 76.3 %collective-permute-done.13.refs_7_ = bf16[192,1536]{1,0:T(8,128)(2,1)} collective-permute-done((bf16[192,1536]{1,0:T(8,128)(2,1)}, bf16[192,1536]{1,0:T(8,128)(2,1)}, u32[]{:S(2)}, u32[]{:S(2)}) %collective-permute-start.13) | collective-permute-done | bytes 589856 | tf_op jit(solution)/shard_map/ppermute | solution.py:594
  283.8 12.6 %collective-permute-done.14.refs_8_ = bf16[192,1536]{1,0:T(8,128)(2,1)} collective-permute-done((bf16[192,1536]{1,0:T(8,128)(2,1)}, bf16[192,1536]{1,0:T(8,128)(2,1)}, u32[]{:S(2)}, u32[]{:S(2)}) %collective-permute-start.14) | collective-permute-done | bytes 589856 | tf_op jit(solution)/shard_map/ppermute | solution.py:594
  296.4 12.0 %collective-permute-done.15.refs_6_ = bf16[192,1536]{1,0:T(8,128)(2,1)} collective-permute-done((bf16[192,1536]{1,0:T(8,128)(2,1)}, bf16[192,1536]{1,0:T(8,128)(2,1)}, u32[]{:S(2)}, u32[]{:S(2)}) %collective-permute-start.15) | collective-permute-done | bytes 589856 | tf_op jit(solution)/shard_map/ppermute | solution.py:594
  309.6 8.7 convolution_convert_fusion
  318.3 5.4 all-to-all-start.1
  327.6 39.5 %collective-permute-done.17.refs_5_ = bf16[576,1536]{1,0:T(8,128)(2,1)S(1)} collective-permute-done((bf16[576,1536]{1,0:T(8,128)(2,1)S(1)}, bf16[576,1536]{1,0:T(8,128)(2,1)S(1)}, u32[]{:S(2)}, u32[]{:S(2)}) %collective-permute-start.17) | collective-permute-done | bytes 1769504 | tf_op jit(solution)/shard_map/ppermute | solution.py:594
  368.3 36.1 %collective-permute-done.18.refs_9_ = bf16[576,1536]{1,0:T(8,128)(2,1)} collective-permute-done((bf16[576,1536]{1,0:T(8,128)(2,1)S(1)}, bf16[576,1536]{1,0:T(8,128)(2,1)}, u32[]{:S(2)}, u32[]{:S(2)}) %collective-permute-start.18) | collective-permute-done | bytes 1769504 | tf_op jit(solution)/shard_map/ppermute | solution.py:594
  404.4 11.2 %all-to-all-done.1.refs_2_ = bf16[8,2,80,3200]{3,2,1,0:T(8,128)(2,1)} async-done(((bf16[8,2,80,3200]{3,2,1,0:T(8,128)(2,1)}), bf16[8,2,80,3200]{3,2,1,0:T(8,128)(2,1)}, u32[]{:S(2)}, u32[]{:S(2)}) %all-to-all-start.1) | async-done | bytes 8192032 | tf_op jit(solution)/shard_map/all_to_all | solution.py:612
  419.2 52.7 %shard_map.215 = (bf16[8,2,80,1536]{3,2,1,0:T(8,128)(2,1)}, bf16[8,2,80,1664]{3,2,1,0:T(8,128)(2,1)}, bf16[576,1536]{1,0:T(8,128)(2,1)}, bf16[576,1536]{1,0:T(8,...) custom-call(s32[3]{0:T(128)} %get-tuple-element.310.refs_0_, ...), custom_call_target="tpu_custom_call" | custom-call | flops 57378078720 | bytes 44040192 | tf_op jit(solution)/shard_map/pallas_call | solution.py:511
  476.8 4.5 all-to-all-start.2
  481.4 51.3 %shard_map.216 = (bf16[8,2,80,1536]{3,2,1,0:T(8,128)(2,1)}, bf16[8,2,80,1664]{3,2,1,0:T(8,128)(2,1)}, bf16[576,1536]{1,0:T(8,128)(2,1)}, bf16[576,1536]{1,0:T(8,...) custom-call(s32[3]{0:T(128)} %get-tuple-element.311.refs_0_, ...), custom_call_target="tpu_custom_call" | custom-call | flops 57378078720 | bytes 44040192 | tf_op jit(solution)/shard_map/pallas_call | solution.py:511
  537.1 5.8 all-to-all-start.3
  544.5 44.8 %all-to-all-done.3 = bf16[8,2,80,1536]{3,2,1,0:T(8,128)(2,1)} async-done(((bf16[8,2,80,1536]{3,2,1,0:T(8,128)(2,1)}), bf16[8,2,80,1536]{3,2,1,0:T(8,128)(2,1)}, u32[]{:S(2)}, u32[]{:S(2)}) %all-to-all-start.3) | async-done | bytes 3932192 | tf_op jit(solution)/shard_map/all_to_all | solution.py:612
  592.3 4.2 fusion.11
  597.7 4.6 all-to-all-start.4
  606.3 36.5 %collective-permute-done.25 = bf16[512,1536]{1,0:T(8,128)(2,1)} collective-permute-done((bf16[512,1536]{1,0:T(8,128)(2,1)}, bf16[512,1536]{1,0:T(8,128)(2,1)}, u32[]{:S(2)}, u32[]{:S(2)}) %collective-permute-start.25) | collective-permute-done | bytes 1572896 | tf_op jit(solution)/shard_map/ppermute | solution.py:609
  651.6 3.7 convolution_convert_fusion.2
  655.3 4.9 all-to-all-start.5
  660.3 27.6 %shard_map.217 = (bf16[4,128,1536]{2,1,0:T(8,128)(2,1)}, bf16[8,4,128,512]{3,2,1,0:T(8,128)(2,1)}) custom-call(s32[5]{0:T(128)} %pad_add_fusion.refs_0_, bf16[4,128,1536]{2,1,0:T(8,128)(2,1)} %get-tuple-element.216.refs_1_, bf16[4,1024,512]{2,1,0:T(8,128)(2,1)} %all-gather.9.cloned.1.call-done.refs_2_, bf16[4,128,1536]{2,1,0:T(8,128)(2,1)} %bitcast.291, ...), custom_call_target="tpu_custom_call" | custom-call | flops 28991029248 | bytes 17825792 | tf_op jit(solution)/shard_map/pallas_call | solution.py:191
  690.9 24.9 %shard_map.218 = bf16[1536,3584]{1,0:T(8,128)(2,1)} custom-call(bf16[512,1536]{1,0:T(8,128)(2,1)} %bitcast.288, bf16[512,1536]{1,0:T(8,128)(2,1)} %copy-done.21, bf16[512,1536]{1,0:T(8,128)(2,1)} %fusion.7.x_ref.refs_2_, bf16[512,1536]{1,0:T(8,128)(2,1)} %bitcast.289, bf16[4096,1536]{1,0:T(8,128)(2,1)} %all-gather.13.cloned.1.call-done.refs_4_, ...), custom_call_target="tpu_custom_call" | custom-call | flops 22548578304 | bytes 12582912 | tf_op jit(solution)/shard_map/pallas_call | solution.py:402
  717.8 4.6 all-to-all-start.6
  727.3 5.1 fusion.3
  734.7 4.6 convert_add_fusion.4
  745.4 5.1 bitcast_add_fusion
  750.5 45.6 %all-to-all-done.6.terms_ref = bf16[8,4,128,512]{3,2,1,0:T(8,128)(2,1)} async-done(((bf16[8,4,128,512]{3,2,1,0:T(8,128)(2,1)}), bf16[8,4,128,512]{3,2,1,0:T(8,128)(2,1)}, u32[]{:S(2)}, u32[]{:S(2)}) %all-to-all-start.6) | async-done | bytes 4194336 | tf_op jit(solution)/shard_map/all_to_all | solution.py:612
  804.3 4.2 convert_add_fusion.2
  808.5 15.5 %shard_map.219 = (f32[512,1536]{1,0:T(8,128)}, f32[1,1536]{1,0:T(1,128)}) custom-call(bf16[512,1536]{1,0:T(8,128)(2,1)} %bitcast.290, bf16[8,4,128,512]{3,2,1,0:T(8,128)(2,1)} %all-to-all-done.6.terms_ref, bf16[1536,2048]{1,0:T(8,128)(2,1)} %bitcast.258, bf16[512,1536]{1,0:T(8,128)(2,1)} %bitcast.251, f32[512,1]{1,0:T(8,128)} %copy.67.inverse_ref, ...), custom_call_target="tpu_custom_call" | custom-call | flops 12884901888 | bytes 12582912 | tf_op jit(solution)/shard_map/pallas_call | solution.py:450
  834.4 5.3 collective-permute-done.31
  845.8 9.7 %collective-permute-done.32 = bf16[48,3712]{1,0:T(8,128)(2,1)} collective-permute-done((bf16[48,3712]{1,0:T(8,128)(2,1)}, bf16[48,3712]{1,0:T(8,128)(2,1)}, u32[]{:S(2)}, u32[]{:S(2)}) %collective-permute-start.32) | collective-permute-done | bytes 356384 | tf_op jit(solution)/shard_map/ppermute | solution.py:594
  855.4 13.0 %collective-permute-done.33 = bf16[48,3712]{1,0:T(8,128)(2,1)} collective-permute-done((bf16[48,3712]{1,0:T(8,128)(2,1)}, bf16[48,3712]{1,0:T(8,128)(2,1)}, u32[]{:S(2)}, u32[]{:S(2)}) %collective-permute-start.33) | collective-permute-done | bytes 356384 | tf_op jit(solution)/shard_map/ppermute | solution.py:594
  870.7 6.8 collective-permute-start.35
  886.3 20.1 %all-gather.15.cloned.1.call-done = bf16[384,3712]{1,0:T(8,128)(2,1)} async-done(((bf16[48,3712]{1,0:T(8,128)(2,1)}), bf16[384,3712]{1,0:T(8,128)(2,1)}) %all-gather.15.cloned.1.call-update) | async-done | bytes 2850832 | tf_op jit(solution)/shard_map/all_gather | solution.py:875
  919.6 4.9 fusion.100
  (298 shorter events, 169.6 us)
Async XLA Ops:
  7.2 86.2 %all-gather.7.cloned.1.call-start = ((), (), s32[]{:S(2)}) async-start(), calls=%async_computation.8 | async-start | bytes 7077888 | tf_op jit(solution)/shard_map/all_gather | solution.py:615
  11.1 10.4 %collective-permute-start.1 = (bf16[48,2048]{1,0:T(8,128)(2,1)S(1)}, bf16[48,2048]{1,0:T(8,128)(2,1)S(1)}, u32[]{:S(2)}, u32[]{:S(2)}) collective-permute-start(bf16[48,2048]{1,0:T(8,128)(2,1)S(1)} %constant_dynamic-update-slice_fusion), channel_id=1, source_target_pairs={{0,3},{1,0},{2,1},{3,2},{4,7},{5,4},{6,5},{7,6},{8,11},{9,8},{10,9... | collective-permute-start | bytes 589832 | tf_op jit(solution)/shard_map/ppermute | solution.py:594
  16.2 16.7 %collective-permute-start.2 = (bf16[48,2048]{1,0:T(8,128)(2,1)S(1)}, bf16[48,2048]{1,0:T(8,128)(2,1)S(1)}, u32[]{:S(2)}, u32[]{:S(2)}) collective-permute-start(bf16[48,2048]{1,0:T(8,128)(2,1)S(1)} %constant_dynamic-update-slice_fusion), channel_id=1, source_target_pairs={{0,2},{1,3},{2,0},{3,1},{4,6},{5,7},{6,4},{7,5},{8,10},{9,11},{10,... | collective-permute-start | bytes 589832 | tf_op jit(solution)/shard_map/ppermute | solution.py:594
  16.2 16.7 %collective-permute-start.3 = (bf16[48,2048]{1,0:T(8,128)(2,1)S(1)}, bf16[48,2048]{1,0:T(8,128)(2,1)S(1)}, u32[]{:S(2)}, u32[]{:S(2)}) collective-permute-start(bf16[48,2048]{1,0:T(8,128)(2,1)S(1)} %constant_dynamic-update-slice_fusion), channel_id=1, source_target_pairs={{0,1},{1,2},{2,3},{3,0},{4,5},{5,6},{6,7},{7,4},{8,9},{9,10},{10,1... | collective-permute-start | bytes 589832 | tf_op jit(solution)/shard_map/ppermute | solution.py:594
  34.0 105.4 %all-gather.9.cloned.1.call-start = ((), (), s32[]{:S(2)}) async-start(), calls=%async_computation.9 | async-start | bytes 4718592 | tf_op jit(solution)/shard_map/all_gather | solution.py:714
  37.9 55.5 %collective-permute-start = (bf16[576,1536]{1,0:T(8,128)(2,1)}, bf16[576,1536]{1,0:T(8,128)(2,1)}, u32[]{:S(2)}, u32[]{:S(2)}) collective-permute-start(bf16[576,1536]{1,0:T(8,128)(2,1)} %pad_maximum_fusion), channel_id=1, source_target_pairs={{0,1},{1,2},{2,3},{3,0},{4,5},{5,6},{6,7},{7,4},{8,9},{9,10},{10,1... | collective-permute-start | bytes 5308424 | tf_op jit(solution)/shard_map/ppermute | solution.py:594
  45.2 32.8 %collective-permute-start.8 = (bf16[2,384]{1,0:T(2,128)(2,1)S(1)}, bf16[2,384]{1,0:T(2,128)(2,1)S(1)}, u32[]{:S(2)}, u32[]{:S(2)}) collective-permute-start(bf16[2,384]{1,0:T(2,128)(2,1)S(1)} %pad_maximum_fusion.8), channel_id=1, source_target_pairs={{0,3},{1,0},{2,1},{3,2},{4,7},{5,4},{6,5},{7,6},{8,11},{9,8},{10,9... | collective-permute-start | bytes 4616 | tf_op jit(solution)/shard_map/ppermute | solution.py:594
  48.2 33.9 %collective-permute-start.9 = (bf16[2,384]{1,0:T(2,128)(2,1)S(1)}, bf16[2,384]{1,0:T(2,128)(2,1)S(1)}, u32[]{:S(2)}, u32[]{:S(2)}) collective-permute-start(bf16[2,384]{1,0:T(2,128)(2,1)S(1)} %pad_maximum_fusion.8), channel_id=1, source_target_pairs={{0,2},{1,3},{2,0},{3,1},{4,6},{5,7},{6,4},{7,5},{8,10},{9,11},{10,... | collective-permute-start | bytes 4616 | tf_op jit(solution)/shard_map/ppermute | solution.py:594
  49.2 35.6 %collective-permute-start.10 = (bf16[2,384]{1,0:T(2,128)(2,1)S(1)}, bf16[2,384]{1,0:T(2,128)(2,1)S(1)}, u32[]{:S(2)}, u32[]{:S(2)}) collective-permute-start(bf16[2,384]{1,0:T(2,128)(2,1)S(1)} %pad_maximum_fusion.8), channel_id=1, source_target_pairs={{0,1},{1,2},{2,3},{3,0},{4,5},{5,6},{6,7},{7,4},{8,9},{9,10},{10,1... | collective-permute-start | bytes 4616 | tf_op jit(solution)/shard_map/ppermute | solution.py:594
  49.2 37.8 %collective-permute-start.4 = (bf16[48,1536]{1,0:T(8,128)(2,1)S(1)}, bf16[48,1536]{1,0:T(8,128)(2,1)S(1)}, u32[]{:S(2)}, u32[]{:S(2)}) collective-permute-start(bf16[48,1536]{1,0:T(8,128)(2,1)S(1)} %constant_dynamic-slice_fusion.3), channel_id=1, source_target_pairs={{0,3},{1,0},{2,1},{3,2},{4,7},{5,4},{6,5},{7,6},{8,11},{9,8},{10,9... | collective-permute-start | bytes 442376 | tf_op jit(solution)/shard_map/ppermute | solution.py:594
  78.0 14.4 %collective-permute-start.5 = (bf16[48,1536]{1,0:T(8,128)(2,1)S(1)}, bf16[48,1536]{1,0:T(8,128)(2,1)S(1)}, u32[]{:S(2)}, u32[]{:S(2)}) collective-permute-start(bf16[48,1536]{1,0:T(8,128)(2,1)S(1)} %constant_dynamic-slice_fusion.3), channel_id=1, source_target_pairs={{0,2},{1,3},{2,0},{3,1},{4,6},{5,7},{6,4},{7,5},{8,10},{9,11},{10,... | collective-permute-start | bytes 442376 | tf_op jit(solution)/shard_map/ppermute | solution.py:594
  98.2 80.0 %all-gather.11.cloned.1.call-start = ((), (), s32[]{:S(2)}) async-start(), calls=%async_computation.10 | async-start | bytes 5308416 | tf_op jit(solution)/shard_map/all_gather | solution.py:615
  98.2 41.2 %collective-permute-start.7 = (bf16[576,1536]{1,0:T(8,128)(2,1)}, bf16[576,1536]{1,0:T(8,128)(2,1)}, u32[]{:S(2)}, u32[]{:S(2)}) collective-permute-start(bf16[576,1536]{1,0:T(8,128)(2,1)} %pad_maximum_fusion), channel_id=1, source_target_pairs={{0,3},{1,0},{2,1},{3,2},{4,7},{5,4},{6,5},{7,6},{8,11},{9,8},{10,9... | collective-permute-start | bytes 5308424 | tf_op jit(solution)/shard_map/ppermute | solution.py:594
  144.0 27.1 %collective-permute-start.11 = (bf16[192,1536]{1,0:T(8,128)(2,1)S(1)}, bf16[192,1536]{1,0:T(8,128)(2,1)}, u32[]{:S(2)}, u32[]{:S(2)}) collective-permute-start(bf16[192,1536]{1,0:T(8,128)(2,1)S(1)} %get-tuple-element.155), channel_id=1, source_target_pairs={{0,2},{1,3},{2,0},{3,1},{4,6},{5,7},{6,4},{7,5},{8,10},{9,11},{10,... | collective-permute-start | bytes 1769480 | tf_op jit(solution)/shard_map/ppermute | solution.py:594
  144.0 23.9 %collective-permute-start.12 = (bf16[512,128]{1,0:T(8,128)(2,1)S(1)}, bf16[512,128]{1,0:T(8,128)(2,1)S(1)}, u32[]{:S(2)}, u32[]{:S(2)}) collective-permute-start(bf16[512,128]{1,0:T(8,128)(2,1)S(1)} %pad_maximum_fusion.5), channel_id=1, source_target_pairs={{0,1},{1,0},{2,3},{3,2},{4,5},{5,4},{6,7},{7,6},{8,9},{9,8},{10,11... | collective-permute-start | bytes 393224 | tf_op jit(solution)/shard_map/ppermute | solution.py:609
  193.1 116.4 %all-to-all-start = ((bf16[8,2,80,3200]{3,2,1,0:T(8,128)(2,1)}), bf16[8,2,80,3200]{3,2,1,0:T(8,128)(2,1)}, u32[]{:S(2)}, u32[]{:S(2)}) async-start(bf16[8,2,80,3200]{3,2,1,0:T(8,128)(2,1)} %bitcast.253), calls=%async_computation | async-start | bytes 16384000 | tf_op jit(solution)/shard_map/all_to_all | solution.py:612
  198.0 111.4 %collective-permute-start.16 = (bf16[512,3200]{1,0:T(8,128)(2,1)}, bf16[512,3200]{1,0:T(8,128)(2,1)}, u32[]{:S(2)}, u32[]{:S(2)}) collective-permute-start(bf16[512,3200]{1,0:T(8,128)(2,1)} %copy-done.23), channel_id=1, source_target_pairs={{0,1},{1,0},{2,3},{3,2},{4,5},{5,4},{6,7},{7,6},{8,9},{9,8},{10,11... | collective-permute-start | bytes 9830408 | tf_op jit(solution)/shard_map/ppermute | solution.py:609
  201.5 82.3 %collective-permute-start.13 = (bf16[192,1536]{1,0:T(8,128)(2,1)}, bf16[192,1536]{1,0:T(8,128)(2,1)}, u32[]{:S(2)}, u32[]{:S(2)}) collective-permute-start(bf16[192,1536]{1,0:T(8,128)(2,1)} %get-tuple-element.165), channel_id=1, source_target_pairs={{0,2},{1,3},{2,0},{3,1},{4,6},{5,7},{6,4},{7,5},{8,10},{9,11},{10,... | collective-permute-start | bytes 1769480 | tf_op jit(solution)/shard_map/ppermute | solution.py:594
  203.9 92.5 %collective-permute-start.14 = (bf16[192,1536]{1,0:T(8,128)(2,1)}, bf16[192,1536]{1,0:T(8,128)(2,1)}, u32[]{:S(2)}, u32[]{:S(2)}) collective-permute-start(bf16[192,1536]{1,0:T(8,128)(2,1)} %get-tuple-element.166), channel_id=1, source_target_pairs={{0,2},{1,3},{2,0},{3,1},{4,6},{5,7},{6,4},{7,5},{8,10},{9,11},{10,... | collective-permute-start | bytes 1769480 | tf_op jit(solution)/shard_map/ppermute | solution.py:594
  204.5 104.0 %collective-permute-start.15 = (bf16[192,1536]{1,0:T(8,128)(2,1)}, bf16[192,1536]{1,0:T(8,128)(2,1)}, u32[]{:S(2)}, u32[]{:S(2)}) collective-permute-start(bf16[192,1536]{1,0:T(8,128)(2,1)} %get-tuple-element.167), channel_id=1, source_target_pairs={{0,2},{1,3},{2,0},{3,1},{4,6},{5,7},{6,4},{7,5},{8,10},{9,11},{10,... | collective-permute-start | bytes 1769480 | tf_op jit(solution)/shard_map/ppermute | solution.py:594
  318.3 97.3 %all-to-all-start.1 = ((bf16[8,2,80,3200]{3,2,1,0:T(8,128)(2,1)}), bf16[8,2,80,3200]{3,2,1,0:T(8,128)(2,1)}, u32[]{:S(2)}, u32[]{:S(2)}) async-start(bf16[8,2,80,3200]{3,2,1,0:T(8,128)(2,1)} %bitcast.254), calls=%async_computation.1 | async-start | bytes 16384000 | tf_op jit(solution)/shard_map/all_to_all | solution.py:612
  323.6 212.3 %all-gather.13.cloned.1.call-start = ((), (), s32[]{:S(2)}) async-start(), calls=%async_computation.11 | async-start | bytes 14155776 | tf_op jit(solution)/shard_map/all_gather | solution.py:759
  323.7 43.3 %collective-permute-start.17 = (bf16[576,1536]{1,0:T(8,128)(2,1)S(1)}, bf16[576,1536]{1,0:T(8,128)(2,1)S(1)}, u32[]{:S(2)}, u32[]{:S(2)}) collective-permute-start(bf16[576,1536]{1,0:T(8,128)(2,1)S(1)} %pad_maximum_fusion.1), channel_id=1, source_target_pairs={{0,1},{1,2},{2,3},{3,0},{4,5},{5,6},{6,7},{7,4},{8,9},{9,10},{10,1... | collective-permute-start | bytes 5308424 | tf_op jit(solution)/shard_map/ppermute | solution.py:594
  326.2 78.2 %collective-permute-start.18 = (bf16[576,1536]{1,0:T(8,128)(2,1)S(1)}, bf16[576,1536]{1,0:T(8,128)(2,1)}, u32[]{:S(2)}, u32[]{:S(2)}) collective-permute-start(bf16[576,1536]{1,0:T(8,128)(2,1)S(1)} %pad_maximum_fusion.1), channel_id=1, source_target_pairs={{0,3},{1,0},{2,1},{3,2},{4,7},{5,4},{6,5},{7,6},{8,11},{9,8},{10,9... | collective-permute-start | bytes 5308424 | tf_op jit(solution)/shard_map/ppermute | solution.py:594
  416.3 55.6 %collective-permute-start.19 = (bf16[192,1536]{1,0:T(8,128)(2,1)}, bf16[192,1536]{1,0:T(8,128)(2,1)S(1)}, u32[]{:S(2)}, u32[]{:S(2)}) collective-permute-start(bf16[192,1536]{1,0:T(8,128)(2,1)} %get-tuple-element.178), channel_id=1, source_target_pairs={{0,2},{1,3},{2,0},{3,1},{4,6},{5,7},{6,4},{7,5},{8,10},{9,11},{10,... | collective-permute-start | bytes 1769480 | tf_op jit(solution)/shard_map/ppermute | solution.py:594
  418.6 53.3 %collective-permute-start.20 = (bf16[192,1536]{1,0:T(8,128)(2,1)}, bf16[192,1536]{1,0:T(8,128)(2,1)S(1)}, u32[]{:S(2)}, u32[]{:S(2)}) collective-permute-start(bf16[192,1536]{1,0:T(8,128)(2,1)} %get-tuple-element.179), channel_id=1, source_target_pairs={{0,2},{1,3},{2,0},{3,1},{4,6},{5,7},{6,4},{7,5},{8,10},{9,11},{10,... | collective-permute-start | bytes 1769480 | tf_op jit(solution)/shard_map/ppermute | solution.py:594
  472.9 63.0 %collective-permute-start.21 = (bf16[576,1536]{1,0:T(8,128)(2,1)}, bf16[576,1536]{1,0:T(8,128)(2,1)S(1)}, u32[]{:S(2)}, u32[]{:S(2)}) collective-permute-start(bf16[576,1536]{1,0:T(8,128)(2,1)} %get-tuple-element.191), channel_id=1, source_target_pairs={{0,1},{1,2},{2,3},{3,0},{4,5},{5,6},{6,7},{7,4},{8,9},{9,10},{10,1... | collective-permute-start | bytes 5308424 | tf_op jit(solution)/shard_map/ppermute | solution.py:594
  475.3 60.6 %collective-permute-start.22 = (bf16[192,1536]{1,0:T(8,128)(2,1)}, bf16[192,1536]{1,0:T(8,128)(2,1)}, u32[]{:S(2)}, u32[]{:S(2)}) collective-permute-start(bf16[192,1536]{1,0:T(8,128)(2,1)} %get-tuple-element.192), channel_id=1, source_target_pairs={{0,2},{1,3},{2,0},{3,1},{4,6},{5,7},{6,4},{7,5},{8,10},{9,11},{10,... | collective-permute-start | bytes 1769480 | tf_op jit(solution)/shard_map/ppermute | solution.py:594
  476.8 59.0 %all-to-all-start.2 = ((bf16[8,2,80,1536]{3,2,1,0:T(8,128)(2,1)}), bf16[8,2,80,1536]{3,2,1,0:T(8,128)(2,1)}, u32[]{:S(2)}, u32[]{:S(2)}) async-start(bf16[8,2,80,1536]{3,2,1,0:T(8,128)(2,1)} %get-tuple-element.200), calls=%async_computation.2 | async-start | bytes 7864320 | tf_op jit(solution)/shard_map/all_to_all | solution.py:612
  537.1 52.2 %all-to-all-start.3 = ((bf16[8,2,80,1536]{3,2,1,0:T(8,128)(2,1)}), bf16[8,2,80,1536]{3,2,1,0:T(8,128)(2,1)}, u32[]{:S(2)}, u32[]{:S(2)}) async-start(bf16[8,2,80,1536]{3,2,1,0:T(8,128)(2,1)} %get-tuple-element.206), calls=%async_computation.3 | async-start | bytes 7864320 | tf_op jit(solution)/shard_map/all_to_all | solution.py:612
  542.9 53.6 %collective-permute-start.23 = (bf16[576,1536]{1,0:T(8,128)(2,1)}, bf16[576,1536]{1,0:T(8,128)(2,1)S(1)}, u32[]{:S(2)}, u32[]{:S(2)}) collective-permute-start(bf16[576,1536]{1,0:T(8,128)(2,1)} %get-tuple-element.204), channel_id=1, source_target_pairs={{0,3},{1,0},{2,1},{3,2},{4,7},{5,4},{6,5},{7,6},{8,11},{9,8},{10,9... | collective-permute-start | bytes 5308424 | tf_op jit(solution)/shard_map/ppermute | solution.py:594
  596.5 46.3 %collective-permute-start.25 = (bf16[512,1536]{1,0:T(8,128)(2,1)}, bf16[512,1536]{1,0:T(8,128)(2,1)}, u32[]{:S(2)}, u32[]{:S(2)}) collective-permute-start(bf16[512,1536]{1,0:T(8,128)(2,1)} %fusion.11), channel_id=1, source_target_pairs={{0,1},{1,0},{2,3},{3,2},{4,5},{5,4},{6,7},{7,6},{8,9},{9,8},{10,11... | collective-permute-start | bytes 4718600 | tf_op jit(solution)/shard_map/ppermute | solution.py:609
  597.7 57.6 %all-to-all-start.4 = ((bf16[8,2,80,1664]{3,2,1,0:T(8,128)(2,1)}), bf16[8,2,80,1664]{3,2,1,0:T(8,128)(2,1)}, u32[]{:S(2)}, u32[]{:S(2)}) async-start(bf16[8,2,80,1664]{3,2,1,0:T(8,128)(2,1)} %get-tuple-element.212), calls=%async_computation.4 | async-start | bytes 8519680 | tf_op jit(solution)/shard_map/all_to_all | solution.py:612
  602.4 44.0 %collective-permute-start.24 = (bf16[192,1536]{1,0:T(8,128)(2,1)}, bf16[192,1536]{1,0:T(8,128)(2,1)}, u32[]{:S(2)}, u32[]{:S(2)}) collective-permute-start(bf16[192,1536]{1,0:T(8,128)(2,1)} %get-tuple-element.209), channel_id=1, source_target_pairs={{0,2},{1,3},{2,0},{3,1},{4,6},{5,7},{6,4},{7,5},{8,10},{9,11},{10,... | collective-permute-start | bytes 1769480 | tf_op jit(solution)/shard_map/ppermute | solution.py:594
  655.3 32.6 %collective-permute-start.26 = (bf16[192,1536]{1,0:T(8,128)(2,1)}, bf16[192,1536]{1,0:T(8,128)(2,1)}, u32[]{:S(2)}, u32[]{:S(2)}) collective-permute-start(bf16[192,1536]{1,0:T(8,128)(2,1)} %get-tuple-element.215), channel_id=1, source_target_pairs={{0,2},{1,3},{2,0},{3,1},{4,6},{5,7},{6,4},{7,5},{8,10},{9,11},{10,... | collective-permute-start | bytes 1769480 | tf_op jit(solution)/shard_map/ppermute | solution.py:594
  655.3 62.5 %all-to-all-start.5 = ((bf16[8,2,80,1664]{3,2,1,0:T(8,128)(2,1)}), bf16[8,2,80,1664]{3,2,1,0:T(8,128)(2,1)}, u32[]{:S(2)}, u32[]{:S(2)}) async-start(bf16[8,2,80,1664]{3,2,1,0:T(8,128)(2,1)} %get-tuple-element.229), calls=%async_computation.5 | async-start | bytes 8519680 | tf_op jit(solution)/shard_map/all_to_all | solution.py:612
  660.2 179.6 %reduce-scatter.2.cloned.1.call-start = ((), (), s32[]{:S(2)}) async-start(), calls=%async_computation.12 | async-start | bytes 12386304 | tf_op jit(solution)/shard_map/reduce_scatter | solution.py:818
  687.9 29.9 %collective-permute-start.27 = (bf16[192,1536]{1,0:T(8,128)(2,1)}, bf16[192,1536]{1,0:T(8,128)(2,1)}, u32[]{:S(2)}, u32[]{:S(2)}) collective-permute-start(bf16[192,1536]{1,0:T(8,128)(2,1)} %get-tuple-element.224), channel_id=1, source_target_pairs={{0,2},{1,3},{2,0},{3,1},{4,6},{5,7},{6,4},{7,5},{8,10},{9,11},{10,... | collective-permute-start | bytes 1769480 | tf_op jit(solution)/shard_map/ppermute | solution.py:594
  717.8 78.3 %all-to-all-start.6 = ((bf16[8,4,128,512]{3,2,1,0:T(8,128)(2,1)}), bf16[8,4,128,512]{3,2,1,0:T(8,128)(2,1)}, u32[]{:S(2)}, u32[]{:S(2)}) async-start(bf16[8,4,128,512]{3,2,1,0:T(8,128)(2,1)} %get-tuple-element.227), calls=%async_computation.6 | async-start | bytes 8388608 | tf_op jit(solution)/shard_map/all_to_all | solution.py:612
  722.4 183.9 %all-gather.15.cloned.1.call-start = ((), (), s32[]{:S(2)}) async-start(), calls=%async_computation.13 | async-start | bytes 3207168 | tf_op jit(solution)/shard_map/all_gather | solution.py:875
  732.3 65.1 %collective-permute-start.30 = (bf16[512,1664]{1,0:T(8,128)(2,1)}, bf16[512,1664]{1,0:T(8,128)(2,1)}, u32[]{:S(2)}, u32[]{:S(2)}) collective-permute-start(bf16[512,1664]{1,0:T(8,128)(2,1)} %fusion.3), channel_id=1, source_target_pairs={{0,1},{1,0},{2,3},{3,2},{4,5},{5,4},{6,7},{7,6},{8,9},{9,8},{10,11... | collective-permute-start | bytes 5111816 | tf_op jit(solution)/shard_map/ppermute | solution.py:609
  739.2 56.9 %collective-permute-start.28 = (bf16[192,1536]{1,0:T(8,128)(2,1)}, bf16[192,1536]{1,0:T(8,128)(2,1)}, u32[]{:S(2)}, u32[]{:S(2)}) collective-permute-start(bf16[192,1536]{1,0:T(8,128)(2,1)} %get-tuple-element.232), channel_id=1, source_target_pairs={{0,2},{1,3},{2,0},{3,1},{4,6},{5,7},{6,4},{7,5},{8,10},{9,11},{10,... | collective-permute-start | bytes 1769480 | tf_op jit(solution)/shard_map/ppermute | solution.py:594
  742.1 54.0 %collective-permute-start.29 = (bf16[192,1536]{1,0:T(8,128)(2,1)}, bf16[192,1536]{1,0:T(8,128)(2,1)}, u32[]{:S(2)}, u32[]{:S(2)}) collective-permute-start(bf16[192,1536]{1,0:T(8,128)(2,1)} %get-tuple-element.233), channel_id=1, source_target_pairs={{0,2},{1,3},{2,0},{3,1},{4,6},{5,7},{6,4},{7,5},{8,10},{9,11},{10,... | collective-permute-start | bytes 1769480 | tf_op jit(solution)/shard_map/ppermute | solution.py:594
  797.4 42.2 %collective-permute-start.31 = (bf16[576,1536]{1,0:T(8,128)(2,1)}, bf16[576,1536]{1,0:T(8,128)(2,1)}, u32[]{:S(2)}, u32[]{:S(2)}) collective-permute-start(bf16[576,1536]{1,0:T(8,128)(2,1)} %get-tuple-element.239), channel_id=1, source_target_pairs={{0,1},{1,2},{2,3},{3,0},{4,5},{5,6},{6,7},{7,4},{8,9},{9,10},{10,1... | collective-permute-start | bytes 5308424 | tf_op jit(solution)/shard_map/ppermute | solution.py:594
  841.9 13.5 %collective-permute-start.32 = (bf16[48,3712]{1,0:T(8,128)(2,1)}, bf16[48,3712]{1,0:T(8,128)(2,1)}, u32[]{:S(2)}, u32[]{:S(2)}) collective-permute-start(bf16[48,3712]{1,0:T(8,128)(2,1)} %get-tuple-element.292), channel_id=1, source_target_pairs={{0,1},{1,2},{2,3},{3,0},{4,5},{5,6},{6,7},{7,4},{8,9},{9,10},{10,1... | collective-permute-start | bytes 1069064 | tf_op jit(solution)/shard_map/ppermute | solution.py:594
  841.9 26.5 %collective-permute-start.33 = (bf16[48,3712]{1,0:T(8,128)(2,1)}, bf16[48,3712]{1,0:T(8,128)(2,1)}, u32[]{:S(2)}, u32[]{:S(2)}) collective-permute-start(bf16[48,3712]{1,0:T(8,128)(2,1)} %get-tuple-element.293), channel_id=1, source_target_pairs={{0,2},{1,3},{2,0},{3,1},{4,6},{5,7},{6,4},{7,5},{8,10},{9,11},{10,... | collective-permute-start | bytes 1069064 | tf_op jit(solution)/shard_map/ppermute | solution.py:594
  843.3 25.1 %collective-permute-start.34 = (bf16[48,3712]{1,0:T(8,128)(2,1)S(1)}, bf16[48,3712]{1,0:T(8,128)(2,1)}, u32[]{:S(2)}, u32[]{:S(2)}) collective-permute-start(bf16[48,3712]{1,0:T(8,128)(2,1)S(1)} %get-tuple-element.294), channel_id=1, source_target_pairs={{0,3},{1,0},{2,1},{3,2},{4,7},{5,4},{6,5},{7,6},{8,11},{9,8},{10,9... | collective-permute-start | bytes 1069064 | tf_op jit(solution)/shard_map/ppermute | solution.py:594
  870.7 53.8 %collective-permute-start.35 = (bf16[576,1536]{1,0:T(8,128)(2,1)}, bf16[576,1536]{1,0:T(8,128)(2,1)}, u32[]{:S(2)}, u32[]{:S(2)}) collective-permute-start(bf16[576,1536]{1,0:T(8,128)(2,1)} %get-tuple-element.263), channel_id=1, source_target_pairs={{0,3},{1,0},{2,1},{3,2},{4,7},{5,4},{6,5},{7,6},{8,11},{9,8},{10,9... | collective-permute-start | bytes 5308424 | tf_op jit(solution)/shard_map/ppermute | solution.py:594
  (45 other events, 957.5 us)
Sparse Core Ops, SparseCore 0:
  34.1 45.9 all-gather.6
  98.3 35.3 all-gather.8
  139.5 38.6 all-gather.10
  415.7 71.4 all-gather.12
  718.0 105.7 reduce-scatter.1
  870.8 35.5 all-gather.14

commit v6 on v5

--- a/solution.py
+++ b/solution.py
@@ -870,8 +870,11 @@
     wide = jnp.concatenate([weight_rows, gain_columns.astype(BF16)], axis=2)
     wide = fsdp_scatter_sum(wide).astype(BF16)
     if merged:
-        wide, far = step([], (wide, far), ["q3"])
         mixed_rows = mixed_sums[0] + far.astype(F32)
+    block_rows = (hidden + mixed_rows[:, :D]).astype(BF16)
+    router_by_expert = mixed_rows[:, D : D + EXPERTS]
+    grad_router = jnp.sum(jnp.where(hit, router_by_expert[:, None, :], 0.0), axis=2)
+    wide, block_rows, grad_router = step([], (wide, block_rows, grad_router), ["q3"])
     wide = lax.all_gather(wide, "ctx", axis=0, tiled=False)
     whole = wide[:, :, : D + width + 2 * KV * HD].reshape(Dl, -1).astype(F32)
     grad_projection, grad_query = whole[:, :D], whole[:, D : D + width]
@@ -885,10 +888,6 @@
     grads = (grad_projection, grad_query, grad_key, grad_value, grad_first, grad_second)
     grads = step(["q3"], grads, [])
     grad_projection, grad_query, grad_key, grad_value, grad_first, grad_second = grads
-    block_rows = (hidden + mixed_rows[:, :D]).astype(BF16)
-    router_by_expert = mixed_rows[:, D : D + EXPERTS]
-    grad_router = jnp.sum(jnp.where(hit, router_by_expert[:, None, :], 0.0), axis=2)
-
     if merged:
         fill((1 - role) * mine + 1, pair_sum(messages["q1"], "q3"))
         grad_up, grad_down = shards

time: 944 us -> 948 us (level)
  no operation moved by 1% of the time
where the time goes in v6:
time: 948 us; the launch traced here: 941 us
  waiting for transfers between devices  458 us (48%)
  Pallas kernels  198 us (21%)
  starting transfers between devices  98.3 us (10%)
  matrix products  60 us (6%)
  local copies, waits for them, and re-layouts  59.3 us (6%)
  other arithmetic  51.5 us (5%)
  between operations  15.6 us (2%)
    ppermute x32, waiting for transfers between devices, shift(): return lax.ppermute(block, 'fsdp', [(i, (i + k) % F) for i in range(F)])  281 us
    pallas_call x2, Pallas kernels, run_expert(): pl.pallas_call(lambda *refs: expert_kernel(sides, w_mode, g_mode, *refs),...  104 us
    all_to_all x7, waiting for transfers between devices, exchange(): return lax.all_to_all(blocks, 'ctx', 0, 0, tiled=True)  102 us
    ppermute x32, starting transfers between devices, shift(): return lax.ppermute(block, 'fsdp', [(i, (i + k) % F) for i in range(F)])  59 us
    ppermute x4, waiting for transfers between devices, swap(): return lax.ppermute(block, 'fsdp', [(i, i ^ 1) for i in range(F)])  38.8 us
    all_to_all x7, starting transfers between devices, exchange(): return lax.all_to_all(blocks, 'ctx', 0, 0, tiled=True)  34.6 us
    dot_general x10, matrix products, mm_tn(): lax.dot_general(a, b, (((0,), (0,)), ((), ())), preferred_element_type=F32)  31 us
    all_gather x1, waiting for transfers between devices, local(): wide = lax.all_gather(wide, 'ctx', axis=0, tiled=False)  29.1 us
  transfers between devices with their start and end apart: 49, of which 24 were waited for; matrix products, arithmetic and copies ran while one was open for 13% of the time, Pallas kernels for 21%

profile of v6, /device:TPU:0, one launch (start us, length us, event | category | flops | bytes accessed | tf_op | source)
XLA Modules:
  0.0 941.0 jit_solution(11757551195681340256)
XLA Ops:
  11.1 5.0 collective-permute-start
  17.2 4.3 collective-permute-done
  21.5 11.3 %collective-permute-done.1 = bf16[48,2048]{1,0:T(8,128)(2,1)S(1)} collective-permute-done((bf16[48,2048]{1,0:T(8,128)(2,1)S(1)}, bf16[48,2048]{1,0:T(8,128)(2,1)S(1)}, u32[]{:S(2)}, u32[]{:S(2)}) %collective-permute-start.1) | collective-permute-done | bytes 196640 | tf_op jit(solution)/shard_map/ppermute | solution.py:594
  49.2 3.8 collective-permute-start.4
  57.8 20.2 %collective-permute-done.8 = bf16[2,384]{1,0:T(2,128)(2,1)S(1)} collective-permute-done((bf16[2,384]{1,0:T(2,128)(2,1)S(1)}, bf16[2,384]{1,0:T(2,128)(2,1)S(1)}, u32[]{:S(2)}, u32[]{:S(2)}) %collective-permute-start.8) | collective-permute-done | bytes 1568 | tf_op jit(solution)/shard_map/ppermute | solution.py:594
  78.0 4.1 collective-permute-start.5
  87.0 5.4 collective-permute-done.5
  93.4 4.8 shard_map.212
  103.4 4.3 fusion.refs_1_
  107.7 31.7 %collective-permute-done.7.refs_9_ = bf16[576,1536]{1,0:T(8,128)(2,1)} collective-permute-done((bf16[576,1536]{1,0:T(8,128)(2,1)}, bf16[576,1536]{1,0:T(8,128)(2,1)}, u32[]{:S(2)}, u32[]{:S(2)}) %collective-permute-start.7) | collective-permute-done | bytes 1769504 | tf_op jit(solution)/shard_map/ppermute | solution.py:594
  146.6 21.3 %shard_map.213 = (bf16[4,128,1536]{2,1,0:T(8,128)(2,1)}, f32[4,2,128,128]{3,2,1,0:T(8,128)}, bf16[4,128,1536]{2,1,0:T(8,128)(2,1)}) custom-call(s32[5]{0:T(128)} %pad_add_fusion.refs_0_, f32[4,128,1536]{2,1,0:T(8,128)} %fusion.refs_1_, bf16[4,1024,512]{2,1,0:T(8,128)(2,1)} %all-gather.9.cloned.1.call-done.refs_2_, ...), custom_call_target="tpu_custom_call" | custom-call | flops 22548578304 | bytes 10485760 | tf_op jit(solution)/shard_map/pallas_call | solution.py:156
  171.0 7.2 all-gather.11.cloned.1.call-done
  178.2 5.2 multiply_reduce_fusion.2
  186.3 6.7 convolution_convert_fusion.1
  193.1 4.9 all-to-all-start
  207.4 76.3 %collective-permute-done.13.refs_7_ = bf16[192,1536]{1,0:T(8,128)(2,1)} collective-permute-done((bf16[192,1536]{1,0:T(8,128)(2,1)}, bf16[192,1536]{1,0:T(8,128)(2,1)}, u32[]{:S(2)}, u32[]{:S(2)}) %collective-permute-start.13) | collective-permute-done | bytes 589856 | tf_op jit(solution)/shard_map/ppermute | solution.py:594
  283.8 12.6 %collective-permute-done.14.refs_8_ = bf16[192,1536]{1,0:T(8,128)(2,1)} collective-permute-done((bf16[192,1536]{1,0:T(8,128)(2,1)}, bf16[192,1536]{1,0:T(8,128)(2,1)}, u32[]{:S(2)}, u32[]{:S(2)}) %collective-permute-start.14) | collective-permute-done | bytes 589856 | tf_op jit(solution)/shard_map/ppermute | solution.py:594
  296.4 12.0 %collective-permute-done.15.refs_6_ = bf16[192,1536]{1,0:T(8,128)(2,1)} collective-permute-done((bf16[192,1536]{1,0:T(8,128)(2,1)}, bf16[192,1536]{1,0:T(8,128)(2,1)}, u32[]{:S(2)}, u32[]{:S(2)}) %collective-permute-start.15) | collective-permute-done | bytes 589856 | tf_op jit(solution)/shard_map/ppermute | solution.py:594
  309.6 8.7 convolution_convert_fusion
  318.3 5.3 all-to-all-start.1
  327.5 39.5 %collective-permute-done.17.refs_5_ = bf16[576,1536]{1,0:T(8,128)(2,1)S(1)} collective-permute-done((bf16[576,1536]{1,0:T(8,128)(2,1)S(1)}, bf16[576,1536]{1,0:T(8,128)(2,1)S(1)}, u32[]{:S(2)}, u32[]{:S(2)}) %collective-permute-start.17) | collective-permute-done | bytes 1769504 | tf_op jit(solution)/shard_map/ppermute | solution.py:594
  368.2 36.1 %collective-permute-done.18.refs_9_ = bf16[576,1536]{1,0:T(8,128)(2,1)} collective-permute-done((bf16[576,1536]{1,0:T(8,128)(2,1)S(1)}, bf16[576,1536]{1,0:T(8,128)(2,1)}, u32[]{:S(2)}, u32[]{:S(2)}) %collective-permute-start.18) | collective-permute-done | bytes 1769504 | tf_op jit(solution)/shard_map/ppermute | solution.py:594
  404.3 11.2 %all-to-all-done.1.refs_2_ = bf16[8,2,80,3200]{3,2,1,0:T(8,128)(2,1)} async-done(((bf16[8,2,80,3200]{3,2,1,0:T(8,128)(2,1)}), bf16[8,2,80,3200]{3,2,1,0:T(8,128)(2,1)}, u32[]{:S(2)}, u32[]{:S(2)}) %all-to-all-start.1) | async-done | bytes 8192032 | tf_op jit(solution)/shard_map/all_to_all | solution.py:612
  419.2 52.7 %shard_map.215 = (bf16[8,2,80,1536]{3,2,1,0:T(8,128)(2,1)}, bf16[8,2,80,1664]{3,2,1,0:T(8,128)(2,1)}, bf16[576,1536]{1,0:T(8,128)(2,1)}, bf16[576,1536]{1,0:T(8,...) custom-call(s32[3]{0:T(128)} %get-tuple-element.312.refs_0_, ...), custom_call_target="tpu_custom_call" | custom-call | flops 57378078720 | bytes 44040192 | tf_op jit(solution)/shard_map/pallas_call | solution.py:511
  476.8 4.5 all-to-all-start.2
  481.4 51.3 %shard_map.216 = (bf16[8,2,80,1536]{3,2,1,0:T(8,128)(2,1)}, bf16[8,2,80,1664]{3,2,1,0:T(8,128)(2,1)}, bf16[576,1536]{1,0:T(8,128)(2,1)}, bf16[576,1536]{1,0:T(8,...) custom-call(s32[3]{0:T(128)} %get-tuple-element.313.refs_0_, ...), custom_call_target="tpu_custom_call" | custom-call | flops 57378078720 | bytes 44040192 | tf_op jit(solution)/shard_map/pallas_call | solution.py:511
  537.1 5.8 all-to-all-start.3
  544.5 44.8 %all-to-all-done.3 = bf16[8,2,80,1536]{3,2,1,0:T(8,128)(2,1)} async-done(((bf16[8,2,80,1536]{3,2,1,0:T(8,128)(2,1)}), bf16[8,2,80,1536]{3,2,1,0:T(8,128)(2,1)}, u32[]{:S(2)}, u32[]{:S(2)}) %all-to-all-start.3) | async-done | bytes 3932192 | tf_op jit(solution)/shard_map/all_to_all | solution.py:612
  592.3 4.2 fusion.11
  597.7 4.6 all-to-all-start.4
  606.3 36.5 %collective-permute-done.25 = bf16[512,1536]{1,0:T(8,128)(2,1)} collective-permute-done((bf16[512,1536]{1,0:T(8,128)(2,1)}, bf16[512,1536]{1,0:T(8,128)(2,1)}, u32[]{:S(2)}, u32[]{:S(2)}) %collective-permute-start.25) | collective-permute-done | bytes 1572896 | tf_op jit(solution)/shard_map/ppermute | solution.py:609
  655.3 4.9 all-to-all-start.5
  660.3 27.6 %shard_map.217 = (bf16[4,128,1536]{2,1,0:T(8,128)(2,1)}, bf16[8,4,128,512]{3,2,1,0:T(8,128)(2,1)}) custom-call(s32[5]{0:T(128)} %pad_add_fusion.refs_0_, bf16[4,128,1536]{2,1,0:T(8,128)(2,1)} %get-tuple-element.217.refs_1_, bf16[4,1024,512]{2,1,0:T(8,128)(2,1)} %all-gather.9.cloned.1.call-done.refs_2_, bf16[4,128,1536]{2,1,0:T(8,128)(2,1)} %bitcast.291, ...), custom_call_target="tpu_custom_call" | custom-call | flops 28991029248 | bytes 17825792 | tf_op jit(solution)/shard_map/pallas_call | solution.py:191
  690.9 24.9 %shard_map.218 = bf16[1536,3584]{1,0:T(8,128)(2,1)} custom-call(bf16[512,1536]{1,0:T(8,128)(2,1)} %bitcast.288, bf16[512,1536]{1,0:T(8,128)(2,1)} %copy-done.20, bf16[512,1536]{1,0:T(8,128)(2,1)} %fusion.7.x_ref.refs_2_, bf16[512,1536]{1,0:T(8,128)(2,1)} %bitcast.289, bf16[4096,1536]{1,0:T(8,128)(2,1)} %all-gather.13.cloned.1.call-done.refs_4_, ...), custom_call_target="tpu_custom_call" | custom-call | flops 22548578304 | bytes 12582912 | tf_op jit(solution)/shard_map/pallas_call | solution.py:402
  717.9 4.6 all-to-all-start.6
  727.2 5.1 fusion.3
  734.7 4.6 convert_add_fusion.4
  745.4 5.1 bitcast_add_fusion
  750.5 45.6 %all-to-all-done.6.terms_ref = bf16[8,4,128,512]{3,2,1,0:T(8,128)(2,1)} async-done(((bf16[8,4,128,512]{3,2,1,0:T(8,128)(2,1)}), bf16[8,4,128,512]{3,2,1,0:T(8,128)(2,1)}, u32[]{:S(2)}, u32[]{:S(2)}) %all-to-all-start.6) | async-done | bytes 4194336 | tf_op jit(solution)/shard_map/all_to_all | solution.py:612
  804.3 4.2 convert_add_fusion.2
  808.5 15.5 %shard_map.219 = (f32[512,1536]{1,0:T(8,128)}, f32[1,1536]{1,0:T(1,128)}) custom-call(bf16[512,1536]{1,0:T(8,128)(2,1)} %bitcast.290, bf16[8,4,128,512]{3,2,1,0:T(8,128)(2,1)} %all-to-all-done.6.terms_ref, bf16[1536,2048]{1,0:T(8,128)(2,1)} %bitcast.258, bf16[512,1536]{1,0:T(8,128)(2,1)} %bitcast.251, f32[512,1]{1,0:T(8,128)} %copy.67.inverse_ref, ...), custom_call_target="tpu_custom_call" | custom-call | flops 12884901888 | bytes 12582912 | tf_op jit(solution)/shard_map/pallas_call | solution.py:450
  834.4 5.2 collective-permute-done.31
  839.8 4.6 convert_add_fusion.5
  854.8 5.2 collective-permute-done.32
  860.0 13.0 %collective-permute-done.33 = bf16[48,3712]{1,0:T(8,128)(2,1)} collective-permute-done((bf16[48,3712]{1,0:T(8,128)(2,1)}, bf16[48,3712]{1,0:T(8,128)(2,1)}, u32[]{:S(2)}, u32[]{:S(2)}) %collective-permute-start.33) | collective-permute-done | bytes 356384 | tf_op jit(solution)/shard_map/ppermute | solution.py:594
  875.2 6.5 collective-permute-start.35
  881.8 29.1 %all-gather.15.cloned.1.call-done = bf16[384,3712]{1,0:T(8,128)(2,1)} async-done(((bf16[48,3712]{1,0:T(8,128)(2,1)}), bf16[384,3712]{1,0:T(8,128)(2,1)}) %all-gather.15.cloned.1.call-update) | async-done | bytes 2850832 | tf_op jit(solution)/shard_map/all_gather | solution.py:878
  924.1 4.9 fusion.100
  (297 shorter events, 168.4 us)
Async XLA Ops:
  7.2 86.2 %all-gather.7.cloned.1.call-start = ((), (), s32[]{:S(2)}) async-start(), calls=%async_computation.8 | async-start | bytes 7077888 | tf_op jit(solution)/shard_map/all_gather | solution.py:615
  11.1 10.4 %collective-permute-start = (bf16[48,2048]{1,0:T(8,128)(2,1)S(1)}, bf16[48,2048]{1,0:T(8,128)(2,1)S(1)}, u32[]{:S(2)}, u32[]{:S(2)}) collective-permute-start(bf16[48,2048]{1,0:T(8,128)(2,1)S(1)} %constant_dynamic-update-slice_fusion), channel_id=1, source_target_pairs={{0,3},{1,0},{2,1},{3,2},{4,7},{5,4},{6,5},{7,6},{8,11},{9,8},{10,9... | collective-permute-start | bytes 589832 | tf_op jit(solution)/shard_map/ppermute | solution.py:594
  16.2 16.7 %collective-permute-start.1 = (bf16[48,2048]{1,0:T(8,128)(2,1)S(1)}, bf16[48,2048]{1,0:T(8,128)(2,1)S(1)}, u32[]{:S(2)}, u32[]{:S(2)}) collective-permute-start(bf16[48,2048]{1,0:T(8,128)(2,1)S(1)} %constant_dynamic-update-slice_fusion), channel_id=1, source_target_pairs={{0,2},{1,3},{2,0},{3,1},{4,6},{5,7},{6,4},{7,5},{8,10},{9,11},{10,... | collective-permute-start | bytes 589832 | tf_op jit(solution)/shard_map/ppermute | solution.py:594
  16.2 16.7 %collective-permute-start.2 = (bf16[48,2048]{1,0:T(8,128)(2,1)S(1)}, bf16[48,2048]{1,0:T(8,128)(2,1)S(1)}, u32[]{:S(2)}, u32[]{:S(2)}) collective-permute-start(bf16[48,2048]{1,0:T(8,128)(2,1)S(1)} %constant_dynamic-update-slice_fusion), channel_id=1, source_target_pairs={{0,1},{1,2},{2,3},{3,0},{4,5},{5,6},{6,7},{7,4},{8,9},{9,10},{10,1... | collective-permute-start | bytes 589832 | tf_op jit(solution)/shard_map/ppermute | solution.py:594
  34.0 105.4 %all-gather.9.cloned.1.call-start = ((), (), s32[]{:S(2)}) async-start(), calls=%async_computation.9 | async-start | bytes 4718592 | tf_op jit(solution)/shard_map/all_gather | solution.py:714
  37.9 55.5 %collective-permute-start.3 = (bf16[576,1536]{1,0:T(8,128)(2,1)}, bf16[576,1536]{1,0:T(8,128)(2,1)}, u32[]{:S(2)}, u32[]{:S(2)}) collective-permute-start(bf16[576,1536]{1,0:T(8,128)(2,1)} %pad_maximum_fusion), channel_id=1, source_target_pairs={{0,1},{1,2},{2,3},{3,0},{4,5},{5,6},{6,7},{7,4},{8,9},{9,10},{10,1... | collective-permute-start | bytes 5308424 | tf_op jit(solution)/shard_map/ppermute | solution.py:594
  45.2 32.8 %collective-permute-start.8 = (bf16[2,384]{1,0:T(2,128)(2,1)S(1)}, bf16[2,384]{1,0:T(2,128)(2,1)S(1)}, u32[]{:S(2)}, u32[]{:S(2)}) collective-permute-start(bf16[2,384]{1,0:T(2,128)(2,1)S(1)} %pad_maximum_fusion.8), channel_id=1, source_target_pairs={{0,3},{1,0},{2,1},{3,2},{4,7},{5,4},{6,5},{7,6},{8,11},{9,8},{10,9... | collective-permute-start | bytes 4616 | tf_op jit(solution)/shard_map/ppermute | solution.py:594
  48.2 33.9 %collective-permute-start.9 = (bf16[2,384]{1,0:T(2,128)(2,1)S(1)}, bf16[2,384]{1,0:T(2,128)(2,1)S(1)}, u32[]{:S(2)}, u32[]{:S(2)}) collective-permute-start(bf16[2,384]{1,0:T(2,128)(2,1)S(1)} %pad_maximum_fusion.8), channel_id=1, source_target_pairs={{0,2},{1,3},{2,0},{3,1},{4,6},{5,7},{6,4},{7,5},{8,10},{9,11},{10,... | collective-permute-start | bytes 4616 | tf_op jit(solution)/shard_map/ppermute | solution.py:594
  49.2 35.6 %collective-permute-start.10 = (bf16[2,384]{1,0:T(2,128)(2,1)S(1)}, bf16[2,384]{1,0:T(2,128)(2,1)S(1)}, u32[]{:S(2)}, u32[]{:S(2)}) collective-permute-start(bf16[2,384]{1,0:T(2,128)(2,1)S(1)} %pad_maximum_fusion.8), channel_id=1, source_target_pairs={{0,1},{1,2},{2,3},{3,0},{4,5},{5,6},{6,7},{7,4},{8,9},{9,10},{10,1... | collective-permute-start | bytes 4616 | tf_op jit(solution)/shard_map/ppermute | solution.py:594
  49.2 37.8 %collective-permute-start.4 = (bf16[48,1536]{1,0:T(8,128)(2,1)S(1)}, bf16[48,1536]{1,0:T(8,128)(2,1)S(1)}, u32[]{:S(2)}, u32[]{:S(2)}) collective-permute-start(bf16[48,1536]{1,0:T(8,128)(2,1)S(1)} %constant_dynamic-slice_fusion.3), channel_id=1, source_target_pairs={{0,3},{1,0},{2,1},{3,2},{4,7},{5,4},{6,5},{7,6},{8,11},{9,8},{10,9... | collective-permute-start | bytes 442376 | tf_op jit(solution)/shard_map/ppermute | solution.py:594
  78.0 14.4 %collective-permute-start.5 = (bf16[48,1536]{1,0:T(8,128)(2,1)S(1)}, bf16[48,1536]{1,0:T(8,128)(2,1)S(1)}, u32[]{:S(2)}, u32[]{:S(2)}) collective-permute-start(bf16[48,1536]{1,0:T(8,128)(2,1)S(1)} %constant_dynamic-slice_fusion.3), channel_id=1, source_target_pairs={{0,2},{1,3},{2,0},{3,1},{4,6},{5,7},{6,4},{7,5},{8,10},{9,11},{10,... | collective-permute-start | bytes 442376 | tf_op jit(solution)/shard_map/ppermute | solution.py:594
  98.2 80.0 %all-gather.11.cloned.1.call-start = ((), (), s32[]{:S(2)}) async-start(), calls=%async_computation.10 | async-start | bytes 5308416 | tf_op jit(solution)/shard_map/all_gather | solution.py:615
  98.2 41.2 %collective-permute-start.7 = (bf16[576,1536]{1,0:T(8,128)(2,1)}, bf16[576,1536]{1,0:T(8,128)(2,1)}, u32[]{:S(2)}, u32[]{:S(2)}) collective-permute-start(bf16[576,1536]{1,0:T(8,128)(2,1)} %pad_maximum_fusion), channel_id=1, source_target_pairs={{0,3},{1,0},{2,1},{3,2},{4,7},{5,4},{6,5},{7,6},{8,11},{9,8},{10,9... | collective-permute-start | bytes 5308424 | tf_op jit(solution)/shard_map/ppermute | solution.py:594
  143.9 27.1 %collective-permute-start.11 = (bf16[192,1536]{1,0:T(8,128)(2,1)S(1)}, bf16[192,1536]{1,0:T(8,128)(2,1)}, u32[]{:S(2)}, u32[]{:S(2)}) collective-permute-start(bf16[192,1536]{1,0:T(8,128)(2,1)S(1)} %get-tuple-element.156), channel_id=1, source_target_pairs={{0,2},{1,3},{2,0},{3,1},{4,6},{5,7},{6,4},{7,5},{8,10},{9,11},{10,... | collective-permute-start | bytes 1769480 | tf_op jit(solution)/shard_map/ppermute | solution.py:594
  143.9 23.9 %collective-permute-start.12 = (bf16[512,128]{1,0:T(8,128)(2,1)S(1)}, bf16[512,128]{1,0:T(8,128)(2,1)S(1)}, u32[]{:S(2)}, u32[]{:S(2)}) collective-permute-start(bf16[512,128]{1,0:T(8,128)(2,1)S(1)} %pad_maximum_fusion.5), channel_id=1, source_target_pairs={{0,1},{1,0},{2,3},{3,2},{4,5},{5,4},{6,7},{7,6},{8,9},{9,8},{10,11... | collective-permute-start | bytes 393224 | tf_op jit(solution)/shard_map/ppermute | solution.py:609
  193.1 116.4 %all-to-all-start = ((bf16[8,2,80,3200]{3,2,1,0:T(8,128)(2,1)}), bf16[8,2,80,3200]{3,2,1,0:T(8,128)(2,1)}, u32[]{:S(2)}, u32[]{:S(2)}) async-start(bf16[8,2,80,3200]{3,2,1,0:T(8,128)(2,1)} %bitcast.253), calls=%async_computation | async-start | bytes 16384000 | tf_op jit(solution)/shard_map/all_to_all | solution.py:612
  198.0 111.4 %collective-permute-start.16 = (bf16[512,3200]{1,0:T(8,128)(2,1)}, bf16[512,3200]{1,0:T(8,128)(2,1)}, u32[]{:S(2)}, u32[]{:S(2)}) collective-permute-start(bf16[512,3200]{1,0:T(8,128)(2,1)} %copy-done.22), channel_id=1, source_target_pairs={{0,1},{1,0},{2,3},{3,2},{4,5},{5,4},{6,7},{7,6},{8,9},{9,8},{10,11... | collective-permute-start | bytes 9830408 | tf_op jit(solution)/shard_map/ppermute | solution.py:609
  201.5 82.3 %collective-permute-start.13 = (bf16[192,1536]{1,0:T(8,128)(2,1)}, bf16[192,1536]{1,0:T(8,128)(2,1)}, u32[]{:S(2)}, u32[]{:S(2)}) collective-permute-start(bf16[192,1536]{1,0:T(8,128)(2,1)} %get-tuple-element.166), channel_id=1, source_target_pairs={{0,2},{1,3},{2,0},{3,1},{4,6},{5,7},{6,4},{7,5},{8,10},{9,11},{10,... | collective-permute-start | bytes 1769480 | tf_op jit(solution)/shard_map/ppermute | solution.py:594
  203.9 92.5 %collective-permute-start.14 = (bf16[192,1536]{1,0:T(8,128)(2,1)}, bf16[192,1536]{1,0:T(8,128)(2,1)}, u32[]{:S(2)}, u32[]{:S(2)}) collective-permute-start(bf16[192,1536]{1,0:T(8,128)(2,1)} %get-tuple-element.167), channel_id=1, source_target_pairs={{0,2},{1,3},{2,0},{3,1},{4,6},{5,7},{6,4},{7,5},{8,10},{9,11},{10,... | collective-permute-start | bytes 1769480 | tf_op jit(solution)/shard_map/ppermute | solution.py:594
  204.4 104.0 %collective-permute-start.15 = (bf16[192,1536]{1,0:T(8,128)(2,1)}, bf16[192,1536]{1,0:T(8,128)(2,1)}, u32[]{:S(2)}, u32[]{:S(2)}) collective-permute-start(bf16[192,1536]{1,0:T(8,128)(2,1)} %get-tuple-element.168), channel_id=1, source_target_pairs={{0,2},{1,3},{2,0},{3,1},{4,6},{5,7},{6,4},{7,5},{8,10},{9,11},{10,... | collective-permute-start | bytes 1769480 | tf_op jit(solution)/shard_map/ppermute | solution.py:594
  318.3 97.3 %all-to-all-start.1 = ((bf16[8,2,80,3200]{3,2,1,0:T(8,128)(2,1)}), bf16[8,2,80,3200]{3,2,1,0:T(8,128)(2,1)}, u32[]{:S(2)}, u32[]{:S(2)}) async-start(bf16[8,2,80,3200]{3,2,1,0:T(8,128)(2,1)} %bitcast.254), calls=%async_computation.1 | async-start | bytes 16384000 | tf_op jit(solution)/shard_map/all_to_all | solution.py:612
  323.6 212.3 %all-gather.13.cloned.1.call-start = ((), (), s32[]{:S(2)}) async-start(), calls=%async_computation.11 | async-start | bytes 14155776 | tf_op jit(solution)/shard_map/all_gather | solution.py:759
  323.7 43.3 %collective-permute-start.17 = (bf16[576,1536]{1,0:T(8,128)(2,1)S(1)}, bf16[576,1536]{1,0:T(8,128)(2,1)S(1)}, u32[]{:S(2)}, u32[]{:S(2)}) collective-permute-start(bf16[576,1536]{1,0:T(8,128)(2,1)S(1)} %pad_maximum_fusion.1), channel_id=1, source_target_pairs={{0,1},{1,2},{2,3},{3,0},{4,5},{5,6},{6,7},{7,4},{8,9},{9,10},{10,1... | collective-permute-start | bytes 5308424 | tf_op jit(solution)/shard_map/ppermute | solution.py:594
  326.1 78.2 %collective-permute-start.18 = (bf16[576,1536]{1,0:T(8,128)(2,1)S(1)}, bf16[576,1536]{1,0:T(8,128)(2,1)}, u32[]{:S(2)}, u32[]{:S(2)}) collective-permute-start(bf16[576,1536]{1,0:T(8,128)(2,1)S(1)} %pad_maximum_fusion.1), channel_id=1, source_target_pairs={{0,3},{1,0},{2,1},{3,2},{4,7},{5,4},{6,5},{7,6},{8,11},{9,8},{10,9... | collective-permute-start | bytes 5308424 | tf_op jit(solution)/shard_map/ppermute | solution.py:594
  416.3 55.6 %collective-permute-start.19 = (bf16[192,1536]{1,0:T(8,128)(2,1)}, bf16[192,1536]{1,0:T(8,128)(2,1)S(1)}, u32[]{:S(2)}, u32[]{:S(2)}) collective-permute-start(bf16[192,1536]{1,0:T(8,128)(2,1)} %get-tuple-element.179), channel_id=1, source_target_pairs={{0,2},{1,3},{2,0},{3,1},{4,6},{5,7},{6,4},{7,5},{8,10},{9,11},{10,... | collective-permute-start | bytes 1769480 | tf_op jit(solution)/shard_map/ppermute | solution.py:594
  418.7 53.2 %collective-permute-start.20 = (bf16[192,1536]{1,0:T(8,128)(2,1)}, bf16[192,1536]{1,0:T(8,128)(2,1)S(1)}, u32[]{:S(2)}, u32[]{:S(2)}) collective-permute-start(bf16[192,1536]{1,0:T(8,128)(2,1)} %get-tuple-element.180), channel_id=1, source_target_pairs={{0,2},{1,3},{2,0},{3,1},{4,6},{5,7},{6,4},{7,5},{8,10},{9,11},{10,... | collective-permute-start | bytes 1769480 | tf_op jit(solution)/shard_map/ppermute | solution.py:594
  472.9 63.0 %collective-permute-start.21 = (bf16[576,1536]{1,0:T(8,128)(2,1)}, bf16[576,1536]{1,0:T(8,128)(2,1)S(1)}, u32[]{:S(2)}, u32[]{:S(2)}) collective-permute-start(bf16[576,1536]{1,0:T(8,128)(2,1)} %get-tuple-element.192), channel_id=1, source_target_pairs={{0,1},{1,2},{2,3},{3,0},{4,5},{5,6},{6,7},{7,4},{8,9},{9,10},{10,1... | collective-permute-start | bytes 5308424 | tf_op jit(solution)/shard_map/ppermute | solution.py:594
  475.3 60.6 %collective-permute-start.22 = (bf16[192,1536]{1,0:T(8,128)(2,1)}, bf16[192,1536]{1,0:T(8,128)(2,1)}, u32[]{:S(2)}, u32[]{:S(2)}) collective-permute-start(bf16[192,1536]{1,0:T(8,128)(2,1)} %get-tuple-element.193), channel_id=1, source_target_pairs={{0,2},{1,3},{2,0},{3,1},{4,6},{5,7},{6,4},{7,5},{8,10},{9,11},{10,... | collective-permute-start | bytes 1769480 | tf_op jit(solution)/shard_map/ppermute | solution.py:594
  476.8 59.1 %all-to-all-start.2 = ((bf16[8,2,80,1536]{3,2,1,0:T(8,128)(2,1)}), bf16[8,2,80,1536]{3,2,1,0:T(8,128)(2,1)}, u32[]{:S(2)}, u32[]{:S(2)}) async-start(bf16[8,2,80,1536]{3,2,1,0:T(8,128)(2,1)} %get-tuple-element.201), calls=%async_computation.2 | async-start | bytes 7864320 | tf_op jit(solution)/shard_map/all_to_all | solution.py:612
  537.1 52.2 %all-to-all-start.3 = ((bf16[8,2,80,1536]{3,2,1,0:T(8,128)(2,1)}), bf16[8,2,80,1536]{3,2,1,0:T(8,128)(2,1)}, u32[]{:S(2)}, u32[]{:S(2)}) async-start(bf16[8,2,80,1536]{3,2,1,0:T(8,128)(2,1)} %get-tuple-element.207), calls=%async_computation.3 | async-start | bytes 7864320 | tf_op jit(solution)/shard_map/all_to_all | solution.py:612
  542.9 53.6 %collective-permute-start.23 = (bf16[576,1536]{1,0:T(8,128)(2,1)}, bf16[576,1536]{1,0:T(8,128)(2,1)S(1)}, u32[]{:S(2)}, u32[]{:S(2)}) collective-permute-start(bf16[576,1536]{1,0:T(8,128)(2,1)} %get-tuple-element.205), channel_id=1, source_target_pairs={{0,3},{1,0},{2,1},{3,2},{4,7},{5,4},{6,5},{7,6},{8,11},{9,8},{10,9... | collective-permute-start | bytes 5308424 | tf_op jit(solution)/shard_map/ppermute | solution.py:594
  596.5 46.3 %collective-permute-start.25 = (bf16[512,1536]{1,0:T(8,128)(2,1)}, bf16[512,1536]{1,0:T(8,128)(2,1)}, u32[]{:S(2)}, u32[]{:S(2)}) collective-permute-start(bf16[512,1536]{1,0:T(8,128)(2,1)} %fusion.11), channel_id=1, source_target_pairs={{0,1},{1,0},{2,3},{3,2},{4,5},{5,4},{6,7},{7,6},{8,9},{9,8},{10,11... | collective-permute-start | bytes 4718600 | tf_op jit(solution)/shard_map/ppermute | solution.py:609
  597.7 57.6 %all-to-all-start.4 = ((bf16[8,2,80,1664]{3,2,1,0:T(8,128)(2,1)}), bf16[8,2,80,1664]{3,2,1,0:T(8,128)(2,1)}, u32[]{:S(2)}, u32[]{:S(2)}) async-start(bf16[8,2,80,1664]{3,2,1,0:T(8,128)(2,1)} %get-tuple-element.213), calls=%async_computation.4 | async-start | bytes 8519680 | tf_op jit(solution)/shard_map/all_to_all | solution.py:612
  602.3 44.0 %collective-permute-start.24 = (bf16[192,1536]{1,0:T(8,128)(2,1)}, bf16[192,1536]{1,0:T(8,128)(2,1)}, u32[]{:S(2)}, u32[]{:S(2)}) collective-permute-start(bf16[192,1536]{1,0:T(8,128)(2,1)} %get-tuple-element.210), channel_id=1, source_target_pairs={{0,2},{1,3},{2,0},{3,1},{4,6},{5,7},{6,4},{7,5},{8,10},{9,11},{10,... | collective-permute-start | bytes 1769480 | tf_op jit(solution)/shard_map/ppermute | solution.py:594
  655.3 32.6 %collective-permute-start.26 = (bf16[192,1536]{1,0:T(8,128)(2,1)}, bf16[192,1536]{1,0:T(8,128)(2,1)}, u32[]{:S(2)}, u32[]{:S(2)}) collective-permute-start(bf16[192,1536]{1,0:T(8,128)(2,1)} %get-tuple-element.216), channel_id=1, source_target_pairs={{0,2},{1,3},{2,0},{3,1},{4,6},{5,7},{6,4},{7,5},{8,10},{9,11},{10,... | collective-permute-start | bytes 1769480 | tf_op jit(solution)/shard_map/ppermute | solution.py:594
  655.3 62.5 %all-to-all-start.5 = ((bf16[8,2,80,1664]{3,2,1,0:T(8,128)(2,1)}), bf16[8,2,80,1664]{3,2,1,0:T(8,128)(2,1)}, u32[]{:S(2)}, u32[]{:S(2)}) async-start(bf16[8,2,80,1664]{3,2,1,0:T(8,128)(2,1)} %get-tuple-element.230), calls=%async_computation.5 | async-start | bytes 8519680 | tf_op jit(solution)/shard_map/all_to_all | solution.py:612
  660.2 184.1 %reduce-scatter.2.cloned.1.call-start = ((), (), s32[]{:S(2)}) async-start(), calls=%async_computation.12 | async-start | bytes 12386304 | tf_op jit(solution)/shard_map/reduce_scatter | solution.py:818
  687.9 29.9 %collective-permute-start.27 = (bf16[192,1536]{1,0:T(8,128)(2,1)}, bf16[192,1536]{1,0:T(8,128)(2,1)}, u32[]{:S(2)}, u32[]{:S(2)}) collective-permute-start(bf16[192,1536]{1,0:T(8,128)(2,1)} %get-tuple-element.225), channel_id=1, source_target_pairs={{0,2},{1,3},{2,0},{3,1},{4,6},{5,7},{6,4},{7,5},{8,10},{9,11},{10,... | collective-permute-start | bytes 1769480 | tf_op jit(solution)/shard_map/ppermute | solution.py:594
  717.9 78.2 %all-to-all-start.6 = ((bf16[8,4,128,512]{3,2,1,0:T(8,128)(2,1)}), bf16[8,4,128,512]{3,2,1,0:T(8,128)(2,1)}, u32[]{:S(2)}, u32[]{:S(2)}) async-start(bf16[8,4,128,512]{3,2,1,0:T(8,128)(2,1)} %get-tuple-element.228), calls=%async_computation.7 | async-start | bytes 8388608 | tf_op jit(solution)/shard_map/all_to_all | solution.py:612
  722.4 188.4 %all-gather.15.cloned.1.call-start = ((), (), s32[]{:S(2)}) async-start(), calls=%async_computation.13 | async-start | bytes 3207168 | tf_op jit(solution)/shard_map/all_gather | solution.py:878
  732.4 65.1 %collective-permute-start.30 = (bf16[512,1664]{1,0:T(8,128)(2,1)}, bf16[512,1664]{1,0:T(8,128)(2,1)}, u32[]{:S(2)}, u32[]{:S(2)}) collective-permute-start(bf16[512,1664]{1,0:T(8,128)(2,1)} %fusion.3), channel_id=1, source_target_pairs={{0,1},{1,0},{2,3},{3,2},{4,5},{5,4},{6,7},{7,6},{8,9},{9,8},{10,11... | collective-permute-start | bytes 5111816 | tf_op jit(solution)/shard_map/ppermute | solution.py:609
  739.3 56.8 %collective-permute-start.28 = (bf16[192,1536]{1,0:T(8,128)(2,1)}, bf16[192,1536]{1,0:T(8,128)(2,1)}, u32[]{:S(2)}, u32[]{:S(2)}) collective-permute-start(bf16[192,1536]{1,0:T(8,128)(2,1)} %get-tuple-element.234), channel_id=1, source_target_pairs={{0,2},{1,3},{2,0},{3,1},{4,6},{5,7},{6,4},{7,5},{8,10},{9,11},{10,... | collective-permute-start | bytes 1769480 | tf_op jit(solution)/shard_map/ppermute | solution.py:594
  742.1 54.0 %collective-permute-start.29 = (bf16[192,1536]{1,0:T(8,128)(2,1)}, bf16[192,1536]{1,0:T(8,128)(2,1)}, u32[]{:S(2)}, u32[]{:S(2)}) collective-permute-start(bf16[192,1536]{1,0:T(8,128)(2,1)} %get-tuple-element.235), channel_id=1, source_target_pairs={{0,2},{1,3},{2,0},{3,1},{4,6},{5,7},{6,4},{7,5},{8,10},{9,11},{10,... | collective-permute-start | bytes 1769480 | tf_op jit(solution)/shard_map/ppermute | solution.py:594
  797.4 42.2 %collective-permute-start.31 = (bf16[576,1536]{1,0:T(8,128)(2,1)}, bf16[576,1536]{1,0:T(8,128)(2,1)}, u32[]{:S(2)}, u32[]{:S(2)}) collective-permute-start(bf16[576,1536]{1,0:T(8,128)(2,1)} %get-tuple-element.241), channel_id=1, source_target_pairs={{0,1},{1,2},{2,3},{3,0},{4,5},{5,6},{6,7},{7,4},{8,9},{9,10},{10,1... | collective-permute-start | bytes 5308424 | tf_op jit(solution)/shard_map/ppermute | solution.py:594
  846.5 13.5 %collective-permute-start.32 = (bf16[48,3712]{1,0:T(8,128)(2,1)}, bf16[48,3712]{1,0:T(8,128)(2,1)}, u32[]{:S(2)}, u32[]{:S(2)}) collective-permute-start(bf16[48,3712]{1,0:T(8,128)(2,1)} %get-tuple-element.294), channel_id=1, source_target_pairs={{0,1},{1,2},{2,3},{3,0},{4,5},{5,6},{6,7},{7,4},{8,9},{9,10},{10,1... | collective-permute-start | bytes 1069064 | tf_op jit(solution)/shard_map/ppermute | solution.py:594
  846.5 26.5 %collective-permute-start.33 = (bf16[48,3712]{1,0:T(8,128)(2,1)}, bf16[48,3712]{1,0:T(8,128)(2,1)}, u32[]{:S(2)}, u32[]{:S(2)}) collective-permute-start(bf16[48,3712]{1,0:T(8,128)(2,1)} %get-tuple-element.295), channel_id=1, source_target_pairs={{0,2},{1,3},{2,0},{3,1},{4,6},{5,7},{6,4},{7,5},{8,10},{9,11},{10,... | collective-permute-start | bytes 1069064 | tf_op jit(solution)/shard_map/ppermute | solution.py:594
  847.9 25.1 %collective-permute-start.34 = (bf16[48,3712]{1,0:T(8,128)(2,1)}, bf16[48,3712]{1,0:T(8,128)(2,1)}, u32[]{:S(2)}, u32[]{:S(2)}) collective-permute-start(bf16[48,3712]{1,0:T(8,128)(2,1)} %get-tuple-element.296), channel_id=1, source_target_pairs={{0,3},{1,0},{2,1},{3,2},{4,7},{5,4},{6,5},{7,6},{8,11},{9,8},{10,9... | collective-permute-start | bytes 1069064 | tf_op jit(solution)/shard_map/ppermute | solution.py:594
  875.2 53.7 %collective-permute-start.35 = (bf16[576,1536]{1,0:T(8,128)(2,1)}, bf16[576,1536]{1,0:T(8,128)(2,1)S(1)}, u32[]{:S(2)}, u32[]{:S(2)}) collective-permute-start(bf16[576,1536]{1,0:T(8,128)(2,1)} %get-tuple-element.265), channel_id=1, source_target_pairs={{0,3},{1,0},{2,1},{3,2},{4,7},{5,4},{6,5},{7,6},{8,11},{9,8},{10,9... | collective-permute-start | bytes 5308424 | tf_op jit(solution)/shard_map/ppermute | solution.py:594
  (45 other events, 956.5 us)
Sparse Core Ops, SparseCore 0:
  34.1 45.9 all-gather.6
  98.3 35.3 all-gather.8
  139.5 38.6 all-gather.10
  415.7 71.4 all-gather.12
  718.0 105.7 reduce-scatter.1
  875.3 35.4 all-gather.14
